TPU v7x, 32 devices: a whole 2x2x4 slice. The times are simulated.
32 devices in a mesh: groups: 2 (over y), aperture: 4 (over z), beam: 2 (over x), range: 2 (over core).
Axes of the slice: x: 2, y: 2, z: 4, core: 2. Of those that a mesh axis runs over, the one named last changes fastest.
Arguments:
- echoes: bfloat16 [2, 2048, 1024], P(None, ('groups', 'aperture', 'beam'), 'range'), parts along dimension 1, may hold values from -6 to 6
- chirp_taps: bfloat16 [2, 64], replicated, may hold values from -0.75 to 0.75
- steer_phase: float32 [256, 512], P(None, 'beam'), may hold values from -3.140625 to 3.140625
- ang_table: int32 [2, 2, 2, 512], P(None, None, None, 'beam'), may hold values from 0 to 255
- range_table: int32 [2, 2, 2, 512], P(None, None, None, 'beam'), may hold values from -13 to 12
- interp_taps: float32 [2, 2, 2, 2, 8, 512], P(None, None, None, None, None, 'beam'), may hold values from -1 to 1
- phase_twist: float32 [2, 2, 2, 512], P(None, None, None, 'beam'), may hold values from -12 to 12
Outputs:
- scene_image: float32 [8, 2, 512, 1024], P(('groups', 'aperture'), None, 'beam', 'range'), parts along dimension 0
There are 2 independent parts, one for each index of `groups`. A program takes and returns all parts, laid end to end along the dimension named above; an argument that names none is the same for every part. Nothing has to cross between parts.
Inputs may be any that keep to these rules, and one draw needn't show every extreme that they name: `ang_table`: entry (l, h, c, j) counts from the first beam of the block of 256 beams that holds beam j.
All inputs are finite; a program needn't handle non-finite values.
Results may differ from a plain program's by a relative error of at most 0.0037.
Values may be sent and summed in bfloat16 or wider, within the bound.
No kernel may reach another device: no remote copies, remote signals or barrier semaphores. Data moves between devices by JAX's collectives and lax.ppermute only.
A program may use at most 128 MiB of HBM per device.

v0:
```python
import jax
import jax.numpy as jnp
from jax import lax
from jax.sharding import PartitionSpec as P

INTERP_LEN = 8
RIM_CELLS = 16


def from_behind(value, axis, steps):
    count = lax.axis_size(axis)
    leading, last = (max(0, -steps), min(count, count - steps))
    return lax.ppermute(value, axis, [(source, source + steps) for source in range(leading, last)])


def with_halo(x, sides, width):
    for axis, dim in sides:
        peers, length = (lax.axis_size(axis), x.shape[dim])
        up = [(i, (i + 1) % peers) for i in range(peers - 1)]
        down = [(j, i) for i, j in up]
        last = lax.slice_in_dim(x, length - width, length, axis=dim)
        leading = lax.slice_in_dim(x, 0, width, axis=dim)
        before = lax.ppermute(last, axis, up)
        after = lax.ppermute(leading, axis, down)
        x = jnp.concatenate([before, x, after], axis=dim)
    return x


def swapped(value, axis, stride):
    mask = 2**stride
    pairs = [(source, source ^ mask) for source in range(lax.axis_size(axis))]
    return lax.ppermute(value, axis, pairs)


def transposed_dot(left_side, right_side):
    return lax.dot_general(
        left_side, right_side, (((0,), (0,)), ((), ())), preferred_element_type=jnp.float32
    )


def toeplitz_matrix(chirp_taps):
    tap_count = chirp_taps.shape[1]
    row_index = lax.broadcasted_iota(jnp.int32, (128 + tap_count, 128), 0)
    col_index = lax.broadcasted_iota(jnp.int32, (128 + tap_count, 128), 1)
    lag_index = row_index - col_index
    tap_index = lax.iota(jnp.int32, tap_count)
    tap_hits = (lag_index[:, :, None] == tap_index[None, None, :]).astype(jnp.float32)
    real_part = jnp.sum(tap_hits * chirp_taps[0].astype(jnp.float32), axis=2)
    imag_part = jnp.sum(tap_hits * chirp_taps[1].astype(jnp.float32), axis=2)
    upper_half = jnp.concatenate([real_part, -imag_part], axis=1)
    lower_half = jnp.concatenate([imag_part, real_part], axis=1)
    return jnp.concatenate([upper_half, lower_half], axis=0).astype(jnp.bfloat16)


def compress(main_cols, upper_rim, kernel):
    piece_rows = main_cols.shape[1]
    range_width = main_cols.shape[2]
    tap_count = upper_rim.shape[2]
    blocks = range_width // 128
    filler = jnp.zeros((2, piece_rows, 128 - tap_count), main_cols.dtype)
    padded = jnp.concatenate([main_cols, upper_rim, filler], axis=2)
    head_cols = padded[:, :, :range_width].reshape(2, piece_rows, blocks, 128)
    tail_cols = padded[:, :, 128 : range_width + 128].reshape(2, piece_rows, blocks, 128)[
        :, :, :, :tap_count
    ]
    windows = jnp.concatenate([head_cols, tail_cols], axis=3)
    row_blocks = jnp.transpose(windows, (1, 2, 0, 3)).reshape(
        piece_rows * blocks, 2 * (128 + tap_count)
    )
    result = jnp.dot(row_blocks, kernel, preferred_element_type=jnp.float32)
    result = result.reshape(piece_rows, blocks, 2, 128)
    return (
        jnp.transpose(result, (2, 0, 1, 3)).reshape(2, piece_rows, range_width).astype(jnp.bfloat16)
    )


def contribute(extended, angles, offsets, weights, rates, fraction):
    range_width = fraction.shape[0]
    span = 2 * RIM_CELLS + 1
    picked = jnp.take(extended, angles, axis=1)
    shift_list = lax.iota(jnp.int32, span) - RIM_CELLS
    tap_list = lax.iota(jnp.int32, INTERP_LEN)
    lag_table = offsets[None, :] + tap_list[:, None] - (INTERP_LEN // 2 - 1)
    hits = (lag_table[None, :, :] == shift_list[:, None, None]).astype(jnp.float32)
    spread_real = jnp.sum(hits * weights[0][None, :, :], axis=1)
    spread_imag = jnp.sum(hits * weights[1][None, :, :], axis=1)
    real_part = jnp.zeros((angles.shape[0], range_width), jnp.float32)
    imag_part = jnp.zeros((angles.shape[0], range_width), jnp.float32)
    for shift_index in range(span):
        tap_real = spread_real[shift_index][:, None]
        tap_imag = spread_imag[shift_index][:, None]
        part_real = picked[0, :, shift_index : shift_index + range_width]
        part_imag = picked[1, :, shift_index : shift_index + range_width]
        real_part = real_part + tap_real * part_real - tap_imag * part_imag
        imag_part = imag_part + tap_real * part_imag + tap_imag * part_real
    rot_angle = rates[:, None] * fraction[None, :]
    cosine = jnp.cos(rot_angle)
    sine_value = jnp.sin(rot_angle)
    return jnp.stack(
        [real_part * cosine - imag_part * sine_value, real_part * sine_value + imag_part * cosine]
    )


def shards(echoes, chirp_taps, steer_phase, ang_table, range_table, interp_taps, phase_twist):
    tap_count = chirp_taps.shape[1]
    kernel = toeplitz_matrix(chirp_taps)
    upper_rim = from_behind(echoes[:, :, :tap_count], "range", -1)
    sub_rows = steer_phase.shape[0]
    range_width = echoes.shape[2]
    steer_scale = sub_rows ** (-0.5)
    cos_table = (jnp.cos(steer_phase) * steer_scale).astype(jnp.bfloat16)
    sin_table = (-jnp.sin(steer_phase) * steer_scale).astype(jnp.bfloat16)
    compressed = compress(echoes, upper_rim, kernel)
    shard_rows = lax.all_gather(compressed, "beam", axis=1, tiled=True)
    real_part = transposed_dot(cos_table, shard_rows[0]) - transposed_dot(sin_table, shard_rows[1])
    imag_part = transposed_dot(cos_table, shard_rows[1]) + transposed_dot(sin_table, shard_rows[0])
    images = jnp.stack([real_part, imag_part])
    slot_index = lax.axis_index("aperture")
    level_count = lax.axis_size("aperture").bit_length() - 1
    range_total = range_width * lax.axis_size("range")
    fraction = (lax.axis_index("range") * range_width + lax.iota(jnp.int32, range_width)).astype(
        jnp.float32
    ) / range_total
    for level_index in range(level_count):
        own_half = slot_index >> level_index & 1
        far_half = 1 - own_half
        extended = with_halo(images, (("range", 2),), RIM_CELLS)
        own_share = contribute(
            extended,
            ang_table[level_index, own_half, own_half],
            range_table[level_index, own_half, own_half],
            interp_taps[level_index, own_half, own_half],
            phase_twist[level_index, own_half, own_half],
            fraction,
        )
        partner_image = swapped(extended, "aperture", level_index)
        images = own_share + contribute(
            partner_image,
            ang_table[level_index, own_half, far_half],
            range_table[level_index, own_half, far_half],
            interp_taps[level_index, own_half, far_half],
            phase_twist[level_index, own_half, far_half],
            fraction,
        )
    return images[None]


def solution(mesh):
    return jax.shard_map(
        shards,
        mesh=mesh,
        in_specs=(
            P(None, ("groups", "aperture", "beam"), "range"),
            P(),
            P(None, "beam"),
            P(None, None, None, "beam"),
            P(None, None, None, "beam"),
            P(None, None, None, None, None, "beam"),
            P(None, None, None, "beam"),
        ),
        out_specs=P(("groups", "aperture"), None, "beam", "range"),
        check_vma=False,
    )
```

profile of v0, /device:TPU:1, one launch (start us, length us, event | category | flops | bytes accessed | tf_op | source)
XLA Modules:
  0.0 177.4 jit_solution(5854377821586344285)
XLA Ops:
  1.2 2.0 %collective-permute-start = (bf16[2,128,64]{1,2,0:T(8,128)(2,1)S(1)}, bf16[2,128,64]{1,2,0:T(8,128)(2,1)S(1)}, u32[]{:S(2)}, u32[]{:S(2)}) collective-permute-start(bf16[2,128,64]{1,2,0:T(8,128)(2,1)S(1)} %slice.3000), channel_id=1, source_target_pairs={{1,0},{3,2},{5,4},{7,6},{9,8},{11,10},{13,12},{15,14},{17,16},{19,... | collective-permute-start | bytes 98312 | tf_op jit(solution)/shard_map/ppermute | solution.py:13
  15.4 3.2 %select_reduce_fusion = (f32[192,128]{1,0:T(8,128)S(1)}, bf16[192,128]{1,0:T(8,128)(2,1)S(1)}) fusion(f32[64]{0:T(128)S(1)} %get-tuple-element.329, s32[192,128]{1,0:T(8,128)S(1)} %iota_subtract_fusion, f32[64]{0:T(128)S(1)} %get-tuple-element.328), kind=kLoop, calls=%fused_computation.4 | loop fusion | flops 7815168 | bytes 246272 | tf_op jit(solution)/shard_map/reduce_sum | solution.py:49
  19.5 9.5 %all_gather.3 = bf16[2,256,512]{1,2,0:T(8,128)(2,1)S(1)} all-gather(bf16[2,128,512]{1,2,0:T(8,128)(2,1)S(1)} %bitcast.347), channel_id=1, replica_groups=mesh['groups'=2,'aperture'=4,'beam'=2,'range'=2] {'beam'}, dimensions={1}, use_global_device_ids=true | all-gather | bytes 786432 | tf_op jit(solution)/shard_map/all_gather | solution.py:114
  33.4 1.3 collective-permute-start.1
  34.7 3.2 %collective-permute-start.2 = (f32[2,256,16]{2,1,0:T(8,128)S(1)}, f32[2,256,16]{2,1,0:T(8,128)S(1)}, u32[]{:S(2)}, u32[]{:S(2)}) collective-permute-start(f32[2,256,16]{2,1,0:T(8,128)S(1)} %get-tuple-element.37), channel_id=1, source_target_pairs={{1,0},{3,2},{5,4},{7,6},{9,8},{11,10},{13,12},{15,14},{17,16},{19,... | collective-permute-start | bytes 98312 | tf_op jit(solution)/shard_map/ppermute | solution.py:24
  39.4 1.4 copy.58
  41.8 2.1 %collective-permute-start.3 = (f32[2,256,544]{1,2,0:T(8,128)}, f32[2,256,544]{1,2,0:T(8,128)}, u32[]{:S(2)}, u32[]{:S(2)}) collective-permute-start(f32[2,256,544]{1,2,0:T(8,128)} %copy.58), channel_id=1, source_target_pairs={{0,4},{4,0},{8,12},{12,8},{1,5},{5,1},{9,13},{13,9},{2,6},{6,2},{1... | collective-permute-start | bytes 3342344 | tf_op jit(solution)/shard_map/ppermute | solution.py:32
  43.9 2.2 %gather_fusion = f32[256,2,544]{2,1,0:T(2,128)S(1)} fusion(f32[2,256,544]{2,0,1:T(2,128)S(1)} %copy.56, s32[1024]{0:T(1024)S(1)} %pad_clamp_fusion.3), kind=kCustom, calls=%fused_computation.clone | custom fusion | bytes 2229248 | tf_op jit(solution)/shard_map/jit(_take)/gather | solution.py:80
  47.7 13.4 %fusion.33 = (f32[1,256,512]{2,1,0:T(8,128)S(1)}, f32[1,256,512]{2,1,0:T(8,128)}, f32[1,256,512]{2,1,0:T(8,128)}) fusion(f32[512]{0:T(512)S(1)} %convert_multiply_fusion, f32[256]{0:T(256)S(1)} %bitcast.356, f32[2,256,544]{2,1,0:T(8,128)S(1)} %fusion.3, f32[256]{0:T(256)S(1)} %bitcast.575, f32[256]{0:T(256)S(1)} %bitcast.608, f32[256]{0:T(256)S(1)} %bitcast.576, ...), kind=kLoop, calls=%fused_computation.59 | loop fusion | flops 34865152 | bytes 36246528 | tf_op jit(solution)/shard_map/sub | solution.py:100
  61.1 7.7 %collective-permute-done.3 = f32[2,256,544]{1,2,0:T(8,128)} collective-permute-done((f32[2,256,544]{1,2,0:T(8,128)}, f32[2,256,544]{1,2,0:T(8,128)}, u32[]{:S(2)}, u32[]{:S(2)}) %collective-permute-start.3) | collective-permute-done | bytes 1114144 | tf_op jit(solution)/shard_map/ppermute | solution.py:32
  68.8 2.6 %copy.59 = f32[2,256,544]{2,0,1:T(2,128)S(1)} copy(f32[2,256,544]{1,2,0:T(8,128)} %collective-permute-done.3) | data formatting | bytes 2228224 | tf_op jit(solution)/shard_map/ppermute | solution.py:32
  71.4 2.2 %gather_fusion.1 = f32[256,2,544]{2,1,0:T(2,128)S(1)} fusion(f32[2,256,544]{2,0,1:T(2,128)S(1)} %copy.59, s32[1024]{0:T(1024)S(1)} %pad_clamp_fusion.2), kind=kCustom, calls=%fused_computation.1.clone | custom fusion | bytes 2229248 | tf_op jit(solution)/shard_map/jit(_take)/gather | solution.py:80
  75.2 15.3 %fusion.31 = (f32[1,256,512]{2,1,0:T(8,128)S(1)}, f32[1,256,512]{2,1,0:T(8,128)S(1)}, f32[1,256,512]{2,1,0:T(8,128)S(1)}) fusion(f32[256]{0:T(256)S(1)} %bitcast.354, f32[512]{0:T(512)S(1)} %convert_multiply_fusion, f32[2,256,544]{2,1,0:T(8,128)S(1)} %fusion.2, f32[256]{0:T(256)S(1)} %bitcast.509, f32[256]{0:T(256)} %bitcast.542, f32[256]{0:T(256)S(1)} %bitcast.510, ...), kind=kLoop, calls=%fused_computation.57 | loop fusion | flops 34865152 | bytes 36246528 | tf_op jit(solution)/shard_map/sub | solution.py:100
  90.5 4.1 %fusion.32 = (f32[1,256,512]{2,1,0:T(8,128)S(1)}, f32[1,256,512]{2,1,0:T(8,128)S(1)}) fusion(f32[1,256,512]{2,1,0:T(8,128)S(1)} %get-tuple-element.30, f32[1,256,512]{2,1,0:T(8,128)S(1)} %get-tuple-element.29, f32[256]{0:T(256)S(1)} %bitcast.355, f32[512]{0:T(512)S(1)} %convert_multiply_fusion, f32[1,256,512]{2,1,0:T(8,128)S(1)} %copy-done.3, ...), kind=kLoop, calls=%fused_computation.58 | loop fusion | flops 1048576 | bytes 3149824 | tf_op jit(solution)/shard_map/add | solution.py:100
  96.3 3.3 %collective-permute-start.5 = (f32[2,256,16]{2,1,0:T(8,128)S(1)}, f32[2,256,16]{2,1,0:T(8,128)S(1)}, u32[]{:S(2)}, u32[]{:S(2)}) collective-permute-start(f32[2,256,16]{2,1,0:T(8,128)S(1)} %get-tuple-element.35), channel_id=1, source_target_pairs={{1,0},{3,2},{5,4},{7,6},{9,8},{11,10},{13,12},{15,14},{17,16},{19,... | collective-permute-start | bytes 98312 | tf_op jit(solution)/shard_map/ppermute | solution.py:24
  101.0 1.4 copy.63
  103.4 2.3 %collective-permute-start.6 = (f32[2,256,544]{1,2,0:T(8,128)}, f32[2,256,544]{1,2,0:T(8,128)}, u32[]{:S(2)}, u32[]{:S(2)}) collective-permute-start(f32[2,256,544]{1,2,0:T(8,128)} %copy.63), channel_id=1, source_target_pairs={{0,8},{4,12},{8,0},{12,4},{1,9},{5,13},{9,1},{13,5},{2,10},{6,14},... | collective-permute-start | bytes 3342344 | tf_op jit(solution)/shard_map/ppermute | solution.py:32
  105.6 2.2 %gather_fusion.2 = f32[256,2,544]{2,1,0:T(2,128)S(1)} fusion(f32[2,256,544]{2,0,1:T(2,128)S(1)} %copy.61, s32[1024]{0:T(1024)S(1)} %pad_clamp_fusion.1), kind=kCustom, calls=%fused_computation.2.clone | custom fusion | bytes 2229248 | tf_op jit(solution)/shard_map/jit(_take)/gather | solution.py:80
  108.8 12.6 %fusion.28 = (f32[1,1,256,512]{3,2,1,0:T(8,128)S(1)}, f32[1,256,512]{2,1,0:T(8,128)}, f32[1,256,512]{2,1,0:T(8,128)}) fusion(f32[256]{0:T(256)S(1)} %bitcast.352, f32[512]{0:T(512)S(1)} %convert_multiply_fusion, f32[2,256,544]{2,1,0:T(8,128)S(1)} %fusion.1, f32[256]{0:T(256)S(1)} %bitcast.443, f32[256]{0:T(256)S(1)} %bitcast.476, f32[256]{0:T(256)S(1)} %bitcast.444, ...), kind=kLoop, calls=%fused_computation.54 | loop fusion | flops 34865152 | bytes 36246528 | tf_op jit(solution)/shard_map/stack | solution.py:99
  121.5 32.8 %collective-permute-done.6 = f32[2,256,544]{1,2,0:T(8,128)} collective-permute-done((f32[2,256,544]{1,2,0:T(8,128)}, f32[2,256,544]{1,2,0:T(8,128)}, u32[]{:S(2)}, u32[]{:S(2)}) %collective-permute-start.6) | collective-permute-done | bytes 1114144 | tf_op jit(solution)/shard_map/ppermute | solution.py:32
  154.3 2.6 %copy.64 = f32[2,256,544]{2,0,1:T(2,128)S(1)} copy(f32[2,256,544]{1,2,0:T(8,128)} %collective-permute-done.6) | data formatting | bytes 2228224 | tf_op jit(solution)/shard_map/ppermute | solution.py:32
  156.9 2.2 %gather_fusion.3 = f32[256,2,544]{2,1,0:T(2,128)S(1)} fusion(f32[2,256,544]{2,0,1:T(2,128)S(1)} %copy.64, s32[1024]{0:T(1024)S(1)} %pad_clamp_fusion), kind=kCustom, calls=%fused_computation.3.clone | custom fusion | bytes 2229248 | tf_op jit(solution)/shard_map/jit(_take)/gather | solution.py:80
  159.3 12.8 %fusion.24 = (f32[1,1,256,512]{3,2,1,0:T(8,128)S(1)}, f32[1,256,512]{2,1,0:T(8,128)S(1)}, f32[1,256,512]{2,1,0:T(8,128)S(1)}) fusion(f32[256]{0:T(256)S(1)} %bitcast.350, f32[512]{0:T(512)S(1)} %convert_multiply_fusion, f32[2,256,544]{2,1,0:T(8,128)S(1)} %fusion, f32[256]{0:T(256)S(1)} %bitcast.410, f32[256]{0:T(256)S(1)} %bitcast.377, f32[256]{0:T(256)S(1)} %bitcast.411, ...), kind=kLoop, calls=%fused_computation.50 | loop fusion | flops 34865152 | bytes 36246528 | tf_op jit(solution)/shard_map/stack | solution.py:99
  172.1 4.1 %fusion.26 = (f32[1,1,256,512]{3,2,1,0:T(8,128)S(1)}, f32[1,1,256,512]{3,2,1,0:T(8,128)S(1)}) fusion(f32[1,256,512]{2,1,0:T(8,128)S(1)} %get-tuple-element.24, f32[1,256,512]{2,1,0:T(8,128)S(1)} %get-tuple-element.23, f32[256]{0:T(256)S(1)} %bitcast.351, f32[512]{0:T(512)S(1)} %convert_multiply_fusion, f32[1,256,512]{2,1,0:T(8,128)S(1)} %copy-done.1, ...), kind=kLoop, calls=%fused_computation.52 | loop fusion | flops 1048576 | bytes 3149824 | tf_op jit(solution)/shard_map/stack | solution.py:99
  (327 shorter events, 28.9 us)
Async XLA Ops:
  0.0 15.3 %copy-start.124 = (bf16[2,64]{1,0:T(2,128)(2,1)S(1)}, bf16[2,64]{1,0:T(2,128)(2,1)}, u32[]{:S(2)}) copy-start(bf16[2,64]{1,0:T(2,128)(2,1)} %param.10) | copy-start | bytes 772
  0.0 15.3 %copy-start.123 = (f32[2,2,2,256]{3,2,1,0:T(2,128)S(1)}, f32[2,2,2,256]{3,2,1,0:T(2,128)}, u32[]{:S(2)}) copy-start(f32[2,2,2,256]{3,2,1,0:T(2,128)} %param.15) | copy-start | bytes 24580
  1.2 17.7 %collective-permute-start = (bf16[2,128,64]{1,2,0:T(8,128)(2,1)S(1)}, bf16[2,128,64]{1,2,0:T(8,128)(2,1)S(1)}, u32[]{:S(2)}, u32[]{:S(2)}) collective-permute-start(bf16[2,128,64]{1,2,0:T(8,128)(2,1)S(1)} %slice.3000), channel_id=1, source_target_pairs={{1,0},{3,2},{5,4},{7,6},{9,8},{11,10},{13,12},{15,14},{17,16},{19,... | collective-permute-start | bytes 98312 | tf_op jit(solution)/shard_map/ppermute | solution.py:13
  19.1 9.9 %copy-start = (f32[256,256]{1,0:T(8,128)S(1)}, f32[256,256]{1,0:T(8,128)}, u32[]{:S(2)}) copy-start(f32[256,256]{1,0:T(8,128)} %param.11) | copy-start | bytes 786436
  33.4 4.6 %collective-permute-start.1 = (f32[2,256,16]{2,1,0:T(8,128)S(1)}, f32[2,256,16]{2,1,0:T(8,128)S(1)}, u32[]{:S(2)}, u32[]{:S(2)}) collective-permute-start(f32[2,256,16]{2,1,0:T(8,128)S(1)} %get-tuple-element.36), channel_id=1, source_target_pairs={{0,1},{2,3},{4,5},{6,7},{8,9},{10,11},{12,13},{14,15},{16,17},{18,... | collective-permute-start | bytes 98312 | tf_op jit(solution)/shard_map/ppermute | solution.py:23
  34.7 4.2 %collective-permute-start.2 = (f32[2,256,16]{2,1,0:T(8,128)S(1)}, f32[2,256,16]{2,1,0:T(8,128)S(1)}, u32[]{:S(2)}, u32[]{:S(2)}) collective-permute-start(f32[2,256,16]{2,1,0:T(8,128)S(1)} %get-tuple-element.37), channel_id=1, source_target_pairs={{1,0},{3,2},{5,4},{7,6},{9,8},{11,10},{13,12},{15,14},{17,16},{19,... | collective-permute-start | bytes 98312 | tf_op jit(solution)/shard_map/ppermute | solution.py:24
  41.8 27.0 %collective-permute-start.3 = (f32[2,256,544]{1,2,0:T(8,128)}, f32[2,256,544]{1,2,0:T(8,128)}, u32[]{:S(2)}, u32[]{:S(2)}) collective-permute-start(f32[2,256,544]{1,2,0:T(8,128)} %copy.58), channel_id=1, source_target_pairs={{0,4},{4,0},{8,12},{12,8},{1,5},{5,1},{9,13},{13,9},{2,6},{6,2},{1... | collective-permute-start | bytes 3342344 | tf_op jit(solution)/shard_map/ppermute | solution.py:32
  46.0 1.3 copy-start.82
  46.0 1.3 copy-start.83
  46.1 1.3 copy-start.84
  46.1 1.3 copy-start.85
  46.1 1.3 copy-start.86
  46.1 1.3 copy-start.87
  46.1 1.3 copy-start.88
  75.2 15.3 %copy-start.3 = (f32[1,256,512]{2,1,0:T(8,128)S(1)}, f32[1,256,512]{2,1,0:T(8,128)}, u32[]{:S(2)}) copy-start(f32[1,256,512]{2,1,0:T(8,128)} %get-tuple-element.32) | copy-start | bytes 1572868
  75.2 15.3 %copy-start.4 = (f32[1,256,512]{2,1,0:T(8,128)S(1)}, f32[1,256,512]{2,1,0:T(8,128)}, u32[]{:S(2)}) copy-start(f32[1,256,512]{2,1,0:T(8,128)} %get-tuple-element.33) | copy-start | bytes 1572868
  94.6 5.0 %copy-start.122 = (s32[256]{0:T(256)S(1)}, s32[256]{0:T(256)}, u32[]{:S(2)}) copy-start(s32[256]{0:T(256)} %compare_select_fusion.8) | copy-start | bytes 3076
  95.0 4.6 %collective-permute-start.4 = (f32[2,256,16]{2,1,0:T(8,128)S(1)}, f32[2,256,16]{2,1,0:T(8,128)S(1)}, u32[]{:S(2)}, u32[]{:S(2)}) collective-permute-start(f32[2,256,16]{2,1,0:T(8,128)S(1)} %get-tuple-element.34), channel_id=1, source_target_pairs={{0,1},{2,3},{4,5},{6,7},{8,9},{10,11},{12,13},{14,15},{16,17},{18,... | collective-permute-start | bytes 98312 | tf_op jit(solution)/shard_map/ppermute | solution.py:23
  96.3 4.2 %collective-permute-start.5 = (f32[2,256,16]{2,1,0:T(8,128)S(1)}, f32[2,256,16]{2,1,0:T(8,128)S(1)}, u32[]{:S(2)}, u32[]{:S(2)}) collective-permute-start(f32[2,256,16]{2,1,0:T(8,128)S(1)} %get-tuple-element.35), channel_id=1, source_target_pairs={{1,0},{3,2},{5,4},{7,6},{9,8},{11,10},{13,12},{15,14},{17,16},{19,... | collective-permute-start | bytes 98312 | tf_op jit(solution)/shard_map/ppermute | solution.py:24
  103.4 4.4 %copy-start.125 = (pred[256]{0:T(512)(128)(4,1)S(1)}, pred[256]{0:T(512)(128)(4,1)}, u32[]{:S(2)}) copy-start(pred[256]{0:T(512)(128)(4,1)} %get-tuple-element.330) | copy-start | bytes 772
  103.4 50.9 %collective-permute-start.6 = (f32[2,256,544]{1,2,0:T(8,128)}, f32[2,256,544]{1,2,0:T(8,128)}, u32[]{:S(2)}, u32[]{:S(2)}) collective-permute-start(f32[2,256,544]{1,2,0:T(8,128)} %copy.63), channel_id=1, source_target_pairs={{0,8},{4,12},{8,0},{12,4},{1,9},{5,13},{9,1},{13,5},{2,10},{6,14},... | collective-permute-start | bytes 3342344 | tf_op jit(solution)/shard_map/ppermute | solution.py:32
  156.9 2.2 %copy-start.126 = (pred[256]{0:T(512)(128)(4,1)S(1)}, pred[256]{0:T(512)(128)(4,1)}, u32[]{:S(2)}) copy-start(pred[256]{0:T(512)(128)(4,1)} %compare_and_fusion) | copy-start | bytes 772
  159.3 12.8 %copy-start.1 = (f32[1,256,512]{2,1,0:T(8,128)S(1)}, f32[1,256,512]{2,1,0:T(8,128)}, u32[]{:S(2)}) copy-start(f32[1,256,512]{2,1,0:T(8,128)} %get-tuple-element.26) | copy-start | bytes 1572868
  159.3 12.8 %copy-start.2 = (f32[1,256,512]{2,1,0:T(8,128)S(1)}, f32[1,256,512]{2,1,0:T(8,128)}, u32[]{:S(2)}) copy-start(f32[1,256,512]{2,1,0:T(8,128)} %get-tuple-element.27) | copy-start | bytes 1572868
  (110 other events, 112.5 us)
where the time goes:
time: 179 us; the launch traced here: 177 us
  other arithmetic  73.3 us (41%)
  waiting for transfers between devices  42.3 us (24%)
  local copies, waits for them, and re-layouts  30.1 us (17%)
  starting transfers between devices  15.4 us (9%)
  blocking collectives  9.49 us (5%)
  matrix products  4.57 us (3%)
  between operations  2.16 us (1%)
    ppermute x2, waiting for transfers between devices, swapped(): return lax.ppermute(value, axis, pairs)  40.5 us
    another operation x3, other arithmetic, contribute(): jnp.stack([real_part * cosine - imag_part * sine_value, real_part * sine_...  29.5 us
    sub x2, other arithmetic, contribute(): real_part * cosine - imag_part * sine_value  28.7 us
    all_gather x1, blocking collectives, shards(): shard_rows = lax.all_gather(compressed, 'beam', axis=1, tiled=True)  9.49 us
    gather x4, local copies, waits for them, and re-layouts, contribute(): picked = jnp.take(extended, angles, axis=1)  8.64 us
    ppermute x2, starting transfers between devices, with_halo(): after = lax.ppermute(leading, axis, down)  6.52 us
    ppermute x2, local copies, waits for them, and re-layouts, swapped(): return lax.ppermute(value, axis, pairs)  5.18 us
    concatenate x4, local copies, waits for them, and re-layouts, with_halo(): x = jnp.concatenate([before, x, after], axis=dim)  4.76 us
  transfers between devices with their start and end apart: 7, of which 4 were waited for; matrix products, arithmetic and copies ran while one was open for 26% of the time, Pallas kernels for 0%

commit v1 on v0

--- a/solution.py
+++ b/solution.py
@@ -1,6 +1,10 @@
+import functools
+
 import jax
 import jax.numpy as jnp
 from jax import lax
+from jax.experimental import pallas as pl
+from jax.experimental.pallas import tpu as pltpu
 from jax.sharding import PartitionSpec as P
 
 INTERP_LEN = 8
@@ -101,7 +105,7 @@
     )
 
 
-def shards(echoes, chirp_taps, steer_phase, ang_table, range_table, interp_taps, phase_twist):
+def level_by_level(echoes, chirp_taps, steer_phase, ang_table, range_table, interp_taps, phase_twist):
     tap_count = chirp_taps.shape[1]
     kernel = toeplitz_matrix(chirp_taps)
     upper_rim = from_behind(echoes[:, :, :tap_count], "range", -1)
@@ -145,9 +149,269 @@
     return images[None]
 
 
+LANES = 128
+SUBS = 8
+STEP = 16
+SPAN = 2 * RIM_CELLS
+
+
+def merge_tables(level, own_half, range_table, interp_taps, phase_twist, first_bin, half_bins, total):
+    steps = half_bins // STEP
+    sign = jnp.array([1.0, -1.0], jnp.float32).reshape(2, 1, 1, 1)
+
+    def rows(x):
+        lead = x.shape[:-1]
+        x = x.reshape(lead + (1, 1, 2, LANES))
+        return jnp.broadcast_to(x, lead + (2, 2, 2, LANES))
+
+    taps = rows(interp_taps[level, own_half])
+    phase = rows(phase_twist[level, own_half]) * sign
+    within = (lax.iota(jnp.int32, STEP).astype(jnp.float32) / total).reshape(STEP, 1, 1, 1, 1)
+    start = first_bin + lax.broadcasted_iota(jnp.int32, (steps, 1, 2, 1, 1), 0) * STEP
+    start = start + lax.broadcasted_iota(jnp.int32, (steps, 1, 2, 1, 1), 2) * half_bins
+    start = start.astype(jnp.float32) / total
+    near, far = phase[:, None] * within, phase[:, None] * start
+    table = jnp.concatenate(
+        [taps[:, 0], taps[:, 1] * sign, jnp.cos(near), jnp.sin(near), jnp.cos(far), jnp.sin(far)],
+        axis=1,
+    )
+    table = table.reshape(2, table.shape[1], SUBS, LANES)
+    shift = rows(range_table[level, own_half] + (RIM_CELLS - INTERP_LEN // 2 + 1))
+    return table, shift.reshape(2, SUBS, LANES)
+
+
+def squeeze(parts, sibling, core, near_mat, edge_mat, c_ref, index):
+    bins = parts[0].shape[-1]
+
+    def columns(low, high):
+        found = []
+        for own, other in zip(parts, sibling):
+            tiles = []
+            for tile in range(low, high):
+                if tile == 0:
+                    rim = other[:, bins - LANES :]
+                    tiles.append(jnp.where(core == 1, rim, jnp.zeros_like(rim)))
+                elif tile == bins // LANES + 1:
+                    rim = other[:, :LANES]
+                    tiles.append(jnp.where(core == 0, rim, jnp.zeros_like(rim)))
+                else:
+                    tiles.append(own[:, (tile - 1) * LANES : tile * LANES])
+            found += tiles
+        return jnp.concatenate(found, axis=1)
+
+    def times(matrix, cols):
+        return lax.dot_general(
+            matrix, cols, (((1,), (1,)), ((), ())), preferred_element_type=jnp.float32
+        )
+
+    for block in range(bins // LANES + 2):
+        if block == 0:
+            rows = jnp.concatenate([near_mat[LANES - SPAN : LANES], near_mat[2 * LANES - SPAN :]], 0)
+            result = times(rows, columns(0, 2))
+            result = jnp.where(core == 1, result, 0.0).astype(jnp.bfloat16)
+            place, count = 0, SPAN
+        elif block <= bins // LANES:
+            result = times(near_mat[...], columns(block, block + 2)).astype(jnp.bfloat16)
+            place, count = SPAN + (block - 1) * LANES, LANES
+        else:
+            result = times(edge_mat[...], columns(block, block + 1)).astype(jnp.bfloat16)
+            place, count = SPAN + bins, SPAN
+        c_ref[index, 0, place : place + count] = result[:count]
+        c_ref[index, 1, place : place + count] = result[count:]
+
+
+def form(c_ref, slot, steer_ref, x_ref):
+    pieces = [c_ref[slot * 2 + x, ri] for ri in (0, 1) for x in (0, 1)]
+    image = jnp.dot(
+        jnp.concatenate(pieces, axis=1), steer_ref[...], preferred_element_type=jnp.float32
+    ).astype(jnp.bfloat16)
+    beams = x_ref.shape[2]
+    x_ref[0] = image[:, :beams]
+    x_ref[1] = image[:, beams:]
+
+
+def merge_child(x_ref, ang, shift, table, child, s_ref, y_ref, o_ref, half_bins, fresh):
+    beams = x_ref.shape[2]
+    beam_index = lax.broadcasted_iota(jnp.int32, (beams, beams), 0)
+    hits = jnp.where(beam_index == ang[child], 1.0, 0.0).astype(jnp.bfloat16)
+    length = half_bins + SPAN
+    for ri in (0, 1):
+        picked = jnp.dot(x_ref[ri], hits, preferred_element_type=jnp.float32)
+        for half in (0, 1):
+            for part in (0, 1):
+                s_ref[pl.ds(ri * 4 + half * 2 + part, length, stride=SUBS), :] = picked[
+                    half * half_bins : half * half_bins + length, part * LANES : (part + 1) * LANES
+                ]
+    offset = shift[child]
+    bits = [(offset & (1 << b)) != 0 for b in range(5)]
+
+    def align(step, carry):
+        base = pl.multiple_of(step * (STEP * SUBS), STEP * SUBS)
+        row = [s_ref[pl.ds(base + k * SUBS, SUBS), :] for k in range(STEP + 31)]
+        for b in (4, 3, 2, 1, 0):
+            d = 1 << b
+            row = [jnp.where(bits[b], row[k + d], row[k]) for k in range(len(row) - d)]
+        for k in range(STEP):
+            y_ref[pl.ds(base + k * SUBS, SUBS), :] = row[k]
+        return carry
+
+    lax.fori_loop(0, half_bins // STEP + 1, align, 0)
+    taps = INTERP_LEN
+    near, far = 2 * taps, 2 * taps + 2 * STEP
+    steps = half_bins // STEP
+
+    def weigh(step, carry):
+        base = pl.multiple_of(step * (STEP * SUBS), STEP * SUBS)
+        far_r, far_i = table[child, far + step], table[child, far + steps + step]
+        w_r, w_i = [], []
+        for t in range(taps):
+            a, b = table[child, t], table[child, taps + t]
+            w_r.append(a * far_r - b * far_i)
+            w_i.append(a * far_i + b * far_r)
+        for low in range(0, STEP, SUBS):
+            row = [y_ref[pl.ds(base + (low + k) * SUBS, SUBS), :] for k in range(SUBS + taps - 1)]
+            for k in range(SUBS):
+                a, b = row[k] * w_r[0], row[k] * w_i[0]
+                for t in range(1, taps):
+                    a = a + row[k + t] * w_r[t]
+                    b = b + row[k + t] * w_i[t]
+                e_r, e_i = table[child, near + low + k], table[child, near + STEP + low + k]
+                value = (e_r * a - e_i * b) + pltpu.roll(e_i * a + e_r * b, SUBS // 2, 0)
+                place = pl.ds(base + (low + k) * SUBS, SUBS)
+                o_ref[place, :] = value if fresh else o_ref[place, :] + value
+        return carry
+
+    lax.fori_loop(0, steps, weigh, 0)
+
+
+def merged_image(o_ref, x_ref, half_bins, first_bin, total):
+    for half in (0, 1):
+        bin_index = lax.broadcasted_iota(jnp.int32, (half_bins, 2 * LANES), 0)
+        bin_index = bin_index + (first_bin + half * half_bins)
+        inside = (bin_index >= 0) & (bin_index < total)
+        for ri in (0, 1):
+            value = jnp.concatenate(
+                [
+                    o_ref[pl.ds(ri * 4 + half * 2 + part, half_bins, stride=SUBS), :]
+                    for part in (0, 1)
+                ],
+                axis=1,
+            )
+            x_ref[ri, half * half_bins : (half + 1) * half_bins] = jnp.where(
+                inside, value, 0.0
+            ).astype(jnp.bfloat16)
+
+
+def finished(o_ref, out_ref, half_bins):
+    for ri in (0, 1):
+        for half in (0, 1):
+            for part in (0, 1):
+                value = o_ref[pl.ds(ri * 4 + half * 2 + part, half_bins, stride=SUBS), :]
+                out_ref[
+                    0, ri, part * LANES : (part + 1) * LANES, half * half_bins : (half + 1) * half_bins
+                ] = value.T
+
+
+def all_kernel(*refs, total):
+    meta = refs[0]
+    pieces, siblings = refs[1:10], refs[10:19]
+    near_mat, edge_mat, steer, ang, shift, table0, table1 = refs[19:26]
+    out_ref = refs[26]
+    c_ref, x0_ref, x1_ref, s_ref, y_ref, o0_ref, o1_ref = refs[27:]
+    core = meta[0]
+    bins = out_ref.shape[3]
+    whole = lambda ref: [ref.at[0], ref.at[1]]
+    for i in range(8):
+        if i < 7:
+            own, other = whole(pieces[i]), whole(siblings[i])
+        else:
+            own, other = [pieces[7].at[0], pieces[8].at[0]], [siblings[7].at[0], siblings[8].at[0]]
+        squeeze(own, other, core, near_mat, edge_mat, c_ref, meta[3 + i])
+    half0, half1 = (bins + SPAN) // 2, bins // 2
+    for top in (0, 1):
+        for low in (0, 1):
+            form(c_ref, top * 2 + low, steer, x0_ref)
+            merge_child(x0_ref, ang.at[0], shift.at[0], table0, low, s_ref, y_ref, o0_ref, half0, low == 0)
+        merged_image(o0_ref, x1_ref, half0, core * bins - RIM_CELLS, total)
+        merge_child(x1_ref, ang.at[1], shift.at[1], table1, top, s_ref, y_ref, o1_ref, half1, top == 0)
+    finished(o1_ref, out_ref, half1)
+
+
+def ring_of_chips(echoes, chirp_taps, steer_phase, ang_table, range_table, interp_taps, phase_twist):
+    pulses, bins = echoes.shape[1:]
+    beams = steer_phase.shape[1]
+    total = bins * lax.axis_size("range")
+    slots = lax.axis_size("aperture")
+    slot, column, core = (lax.axis_index(a) for a in ("aperture", "beam", "range"))
+    axes = ("aperture", "beam")
+    order = [z * 2 for z in range(slots)] + [z * 2 + 1 for z in reversed(range(slots))]
+    ahead = [(order[i], order[(i + 1) % len(order)]) for i in range(len(order))]
+    behind = [(b, a) for a, b in ahead]
+    place = jnp.where(column == 0, slot, 2 * slots - 1 - slot)
+
+    up = down = echoes
+    pieces = [echoes]
+    sources = [place]
+    for step in range(1, slots):
+        up, down = lax.ppermute(up, axes, ahead), lax.ppermute(down, axes, behind)
+        pieces += [up, down]
+        sources += [place - step, place + step]
+    pieces += [lax.ppermute(up[:1], axes, ahead), lax.ppermute(down[1:], axes, behind)]
+    sources.append(place + slots)
+    siblings = [lax.ppermute(x, "range", [(0, 1), (1, 0)]) for x in pieces]
+    ring = jnp.stack(sources) % (2 * slots)
+    ring = jnp.where(ring < slots, 2 * ring, 2 * (2 * slots - 1 - ring) + 1)
+    meta = jnp.concatenate([jnp.stack([core, slot & 1, slot >> 1]), ring]).astype(jnp.int32)
+
+    lag = lax.broadcasted_iota(jnp.int32, (LANES, 2 * LANES), 1)
+    lag = lag - lax.broadcasted_iota(jnp.int32, (LANES, 2 * LANES), 0)
+    hits = (lag[:, :, None] == lax.iota(jnp.int32, chirp_taps.shape[1])).astype(jnp.float32)
+    t_r, t_i = (jnp.sum(hits * chirp_taps[i].astype(jnp.float32), axis=2) for i in (0, 1))
+    near_mat = jnp.block([[t_r, t_i], [-t_i, t_r]]).astype(jnp.bfloat16)
+    e_r, e_i = t_r[:SPAN, :LANES], t_i[:SPAN, :LANES]
+    edge_mat = jnp.block([[e_r, e_i], [-e_i, e_r]]).astype(jnp.bfloat16)
+    scale = steer_phase.shape[0] ** (-0.5)
+    cos_table = (jnp.cos(steer_phase) * scale).astype(jnp.bfloat16)
+    sin_table = (-jnp.sin(steer_phase) * scale).astype(jnp.bfloat16)
+    steer = jnp.block([[cos_table, sin_table], [-sin_table, cos_table]])
+    halves = (slot & 1, slot >> 1 & 1)
+    half0, half1 = (bins + SPAN) // 2, bins // 2
+    first = core * bins
+    table0, shift0 = merge_tables(
+        0, halves[0], range_table, interp_taps, phase_twist, first - RIM_CELLS, half0, total
+    )
+    table1, shift1 = merge_tables(
+        1, halves[1], range_table, interp_taps, phase_twist, first, half1, total
+    )
+    shift = jnp.stack([shift0, shift1])
+    ang = jnp.stack([ang_table[level, halves[level]] for level in (0, 1)])[:, :, None, :]
+
+    vmem = pl.BlockSpec(memory_space=pltpu.VMEM)
+    rows = half0 + SPAN + 32
+    window = bins + 2 * SPAN
+    return pl.pallas_call(
+        functools.partial(all_kernel, total=total),
+        out_shape=jax.ShapeDtypeStruct((1, 2, beams, bins), jnp.float32),
+        in_specs=[pl.BlockSpec(memory_space=pltpu.SMEM)] + [vmem] * 25,
+        out_specs=vmem,
+        scratch_shapes=[
+            pltpu.VMEM((2 * slots, 2, window, pulses), jnp.bfloat16),
+            pltpu.VMEM((2, window, beams), jnp.bfloat16),
+            pltpu.VMEM((2, window - SPAN, beams), jnp.bfloat16),
+            pltpu.VMEM((rows * SUBS, LANES), jnp.float32),
+            pltpu.VMEM((rows * SUBS, LANES), jnp.float32),
+            pltpu.VMEM((half0 * SUBS, LANES), jnp.float32),
+            pltpu.VMEM((half1 * SUBS, LANES), jnp.float32),
+        ],
+        compiler_params=pltpu.CompilerParams(vmem_limit_bytes=40 * 1024 * 1024),
+        name="backproject",
+    )(meta, *pieces, *siblings, near_mat, edge_mat, steer, ang, shift, table0, table1)
+
+
 def solution(mesh):
+    small = (mesh.shape["aperture"], mesh.shape["beam"], mesh.shape["range"]) == (4, 2, 2)
     return jax.shard_map(
-        shards,
+        ring_of_chips if small else level_by_level,
         mesh=mesh,
         in_specs=(
             P(None, ("groups", "aperture", "beam"), "range"),

time: 179 us -> 64.8 us (0.36)
  other arithmetic: 73.3 us -> 13.2 us
  waiting for transfers between devices: 42.3 us -> 9.75 us
  local copies, waits for them, and re-layouts: 30.1 us -> 2.85 us
  Pallas kernels: 0 us -> 20.1 us
  blocking collectives: 9.49 us -> 0 us
  matrix products: 4.57 us -> 0 us
  starting transfers between devices: 15.4 us -> 17.9 us
  between operations: 2.16 us -> 0.36 us
    ppermute x7 -> x17, waiting for transfers between devices: 42.3 us -> 9.75 us  [the longest x6 8.91 us: ring_of_chips(): up, down = (lax.ppermute(up, axes, ahead), lax.ppermute(down, axes, behind))]
    another operation x4, other arithmetic: 29.5 us -> 0.69 us  [the longest x3 29.5 us: contribute(): jnp.stack([real_part * cosine - imag_part * sine_value, real_part * sine_...]
    sub x6 -> x1, other arithmetic: 28.8 us -> 0.01 us  [ring_of_chips(): lag = lag - lax.broadcasted_iota(jnp.int32, (LANES, 2 * LANES), 0)]
    pallas_call x0 -> x1, Pallas kernels: none -> 20.1 us  [ring_of_chips(): pl.pallas_call(functools.partial(all_kernel, total=total), out_shape=jax....]
    all_gather x1 -> x0, blocking collectives: 9.49 us -> none  [shards(): shard_rows = lax.all_gather(compressed, 'beam', axis=1, tiled=True)]
    gather x4 -> x0, local copies, waits for them, and re-layouts: 8.64 us -> none  [contribute(): picked = jnp.take(extended, angles, axis=1)]
    slice x20 -> x7, local copies, waits for them, and re-layouts: 6.83 us -> 0.05 us  [the longest x3 0.03 us: merge_tables(): taps[:, 1] * sign]
    add x3, other arithmetic: 5.5 us -> 0.01 us  [the longest x2 0.01 us: merge_tables(): first_bin + lax.broadcasted_iota(jnp.int32, (steps, 1, 2, 1, 1), 0) * STEP]
  transfers between devices with their start and end apart: 7 -> 17, of which waited for: 4 -> 4; matrix products, arithmetic and copies ran while one was open for 26% -> 25% of each run, Pallas kernels for 0% -> 0%
where the time goes in v1:
time: 64.8 us; the launch traced here: 64.2 us
  Pallas kernels  20.1 us (31%)
  starting transfers between devices  17.9 us (28%)
  other arithmetic  13.2 us (20%)
  waiting for transfers between devices  9.75 us (15%)
  local copies, waits for them, and re-layouts  2.85 us (4%)
    pallas_call x1, Pallas kernels, ring_of_chips(): pl.pallas_call(functools.partial(all_kernel, total=total), out_shape=jax....  20.1 us
    ppermute x9, starting transfers between devices, ring_of_chips(): siblings = [lax.ppermute(x, 'range', [(0, 1), (1, 0)]) for x in pieces]  10.6 us
    ppermute x6, waiting for transfers between devices, ring_of_chips(): up, down = (lax.ppermute(up, axes, ahead), lax.ppermute(down, axes, behind))  8.91 us
    ppermute x6, starting transfers between devices, ring_of_chips(): up, down = (lax.ppermute(up, axes, ahead), lax.ppermute(down, axes, behind))  5.62 us
    reduce_sum x1, other arithmetic, ring_of_chips(): jnp.sum(hits * chirp_taps[i].astype(jnp.float32), axis=2)  4.18 us
    unnamed x5, other arithmetic  2.92 us
    neg x1, other arithmetic, ring_of_chips(): steer = jnp.block([[cos_table, sin_table], [-sin_table, cos_table]])  1.57 us
    convert_element_type x1, other arithmetic, ring_of_chips(): cos_table = (jnp.cos(steer_phase) * scale).astype(jnp.bfloat16)  1.51 us
  transfers between devices with their start and end apart: 17, of which 4 were waited for; matrix products, arithmetic and copies ran while one was open for 25% of the time, Pallas kernels for 0%

profile of v1, /device:TPU:1, one launch (start us, length us, event | category | flops | bytes accessed | tf_op | source)
XLA Modules:
  0.0 64.2 jit_solution(17233421702149161510)
XLA Ops:
  0.0 2.1 %collective-permute-start = (bf16[2,128,512]{2,1,0:T(8,128)(2,1)}, bf16[2,128,512]{2,1,0:T(8,128)(2,1)S(1)}, u32[]{:S(2)}, u32[]{:S(2)}) collective-permute-start(bf16[2,128,512]{2,1,0:T(8,128)(2,1)} %refs_1_.1), channel_id=1, source_target_pairs={{0,4},{4,8},{8,12},{12,14},{14,10},{10,6},{6,2},{2,0},{1,5},{5,9},... | collective-permute-start | bytes 786440 | tf_op jit(solution)/shard_map/ppermute | solution.py:356
  2.1 1.0 %collective-permute-start.8 = (bf16[2,128,512]{2,1,0:T(8,128)(2,1)}, bf16[2,128,512]{2,1,0:T(8,128)(2,1)S(1)}, u32[]{:S(2)}, u32[]{:S(2)}) collective-permute-start(bf16[2,128,512]{2,1,0:T(8,128)(2,1)} %refs_1_.1), channel_id=1, source_target_pairs={{0,1},{1,0},{2,3},{3,2},{4,5},{5,4},{6,7},{7,6},{8,9},{9,8},{10,11... | collective-permute-start | bytes 786440 | tf_op jit(solution)/shard_map/ppermute | solution.py:361
  3.1 0.8 %dynamic-slice_bitcast_fusion = (f32[2,2,8,2,128]{4,2,3,1,0:T(8,128)S(1)}, f32[2,2,8,2,128]{4,2,3,1,0:T(8,128)S(1)}) fusion(f32[2,2,2,2,8,256]{5,4,3,2,1,0:T(8,128)} %param.14, s32[]{:T(128)S(6)} %select_n.30, s32[]{:T(128)S(6)} %select_n.29), kind=kLoop, calls=%fused_computation.28 | loop fusion | bytes 131080 | tf_op jit(solution)/shard_map/broadcast_in_dim | solution.py:165
  4.1 0.7 %mul.183 = f32[2,2,2]{2,1,0:T(2,128)S(1)} broadcast(f32[2]{0:T(128)} %constant.75.clone), dimensions={0} | broadcast | bytes 40 | tf_op jit(solution)/shard_map/mul | solution.py:175
  4.9 0.7 %constant_dynamic-slice_fusion = (f32[1,1,2,256]{3,2,1,0:T(2,128)S(1)}, f32[1,1,2,256]{3,2,1,0:T(2,128)S(1)}) fusion(f32[2,2,2,256]{3,2,1,0:T(2,128)} %param.15, s32[]{:T(128)S(6)} %select_n.30, s32[]{:T(128)S(6)} %select_n.29), kind=kLoop, calls=%fused_computation.49 | loop fusion | bytes 8200 | tf_op jit(solution)/shard_map/dynamic_slice | solution.py:168
  6.2 0.9 %fusion.4 = (f32[2,80,8,128]{3,2,1,0:T(8,128)S(1)}, f32[2,82,8,128]{3,2,1,0:T(8,128)S(1)}) fusion(f32[2,80,8,128]{3,2,1,0:T(8,128)S(1)} %get-tuple-element.29, f32[2,8,128]{2,1,0:T(8,128)S(1)} %get-tuple-element.27, f32[16]{0:T(128)S(1)} %convert_multiply_fusion.2, f32[2,82,8,128]{3,2,1,0:T(8,128)S(1)} %get-tuple-element.30, ...), kind=kLoop, calls=%fused_computation.19 | loop fusion | flops 65536 | bytes 279040
  7.1 0.9 %fusion.5 = (f32[2,80,8,128]{3,2,1,0:T(8,128)S(1)}, f32[2,82,8,128]{3,2,1,0:T(8,128)S(1)}) fusion(f32[2,80,8,128]{3,2,1,0:T(8,128)S(1)} %get-tuple-element.25, f32[2,8,128]{2,1,0:T(8,128)S(1)} %get-tuple-element.27, f32[16]{0:T(128)S(1)} %convert_multiply_fusion.2, f32[2,82,8,128]{3,2,1,0:T(8,128)S(1)} %get-tuple-element.26, ...), kind=kLoop, calls=%fused_computation.20 | loop fusion | flops 65536 | bytes 279040
  9.1 4.2 %select_reduce_fusion = (f32[128,256]{1,0:T(8,128)S(1)}, bf16[128,256]{1,0:T(8,128)(2,1)S(1)}) fusion(f32[64]{0:T(128)S(1)} %get-tuple-element.32, s32[128,256]{1,0:T(8,128)S(1)} %iota_subtract_fusion, f32[64]{0:T(128)S(1)} %get-tuple-element.31), kind=kLoop, calls=%fused_computation | loop fusion | flops 10420224 | bytes 328192 | tf_op jit(solution)/shard_map/reduce_sum | solution.py:369
  15.0 1.5 %multiply_convert_fusion.1 = bf16[256,256]{1,0:T(8,128)(2,1)} fusion(f32[256,256]{1,0:T(8,128)S(1)} %copy-done.1), kind=kLoop, calls=%fused_computation.6 | loop fusion | flops 131072 | bytes 393216 | tf_op jit(solution)/shard_map/convert_element_type | solution.py:374
  16.5 1.7 %collective-permute-start.2 = (bf16[2,128,512]{2,1,0:T(8,128)(2,1)S(1)}, bf16[2,128,512]{2,1,0:T(8,128)(2,1)S(1)}, u32[]{:S(2)}, u32[]{:S(2)}) collective-permute-start(bf16[2,128,512]{2,1,0:T(8,128)(2,1)S(1)} %collective-permute-done.refs_2_), channel_id=1, source_target_pairs={{0,4},{4,8},{8,12},{12,14},{14,10},{10,6},{6,2},{2,0},{1,5},{5,9},... | collective-permute-start | bytes 786440 | tf_op jit(solution)/shard_map/ppermute | solution.py:356
  18.4 1.6 %fusion.9 = (bf16[256,256]{1,0:T(8,128)(2,1)}, bf16[256,256]{1,0:T(8,128)(2,1)}) fusion(f32[256,256]{1,0:T(8,128)S(1)} %copy-done.1), kind=kLoop, calls=%fused_computation.64 | loop fusion | flops 393216 | bytes 524288 | tf_op jit(solution)/shard_map/neg | solution.py:376
  19.9 4.8 %collective-permute-done.2.refs_4_ = bf16[2,128,512]{2,1,0:T(8,128)(2,1)S(1)} collective-permute-done((bf16[2,128,512]{2,1,0:T(8,128)(2,1)S(1)}, bf16[2,128,512]{2,1,0:T(8,128)(2,1)S(1)}, u32[]{:S(2)}, u32[]{:S(2)}) %collective-permute-start.2) | collective-permute-done | bytes 262176 | tf_op jit(solution)/shard_map/ppermute | solution.py:356
  24.8 1.4 %collective-permute-start.4 = (bf16[2,128,512]{2,1,0:T(8,128)(2,1)S(1)}, bf16[2,128,512]{2,1,0:T(8,128)(2,1)S(1)}, u32[]{:S(2)}, u32[]{:S(2)}) collective-permute-start(bf16[2,128,512]{2,1,0:T(8,128)(2,1)S(1)} %collective-permute-done.2.refs_4_), channel_id=1, source_target_pairs={{0,4},{4,8},{8,12},{12,14},{14,10},{10,6},{6,2},{2,0},{1,5},{5,9},... | collective-permute-start | bytes 786440 | tf_op jit(solution)/shard_map/ppermute | solution.py:356
  26.3 1.3 %collective-permute-done.3.refs_5_ = bf16[2,128,512]{2,1,0:T(8,128)(2,1)S(1)} collective-permute-done((bf16[2,128,512]{2,1,0:T(8,128)(2,1)S(1)}, bf16[2,128,512]{2,1,0:T(8,128)(2,1)S(1)}, u32[]{:S(2)}, u32[]{:S(2)}) %collective-permute-start.3) | collective-permute-done | bytes 262176 | tf_op jit(solution)/shard_map/ppermute | solution.py:356
  27.9 1.1 %collective-permute-start.10 = (bf16[2,128,512]{2,1,0:T(8,128)(2,1)S(1)}, bf16[2,128,512]{2,1,0:T(8,128)(2,1)S(1)}, u32[]{:S(2)}, u32[]{:S(2)}) collective-permute-start(bf16[2,128,512]{2,1,0:T(8,128)(2,1)S(1)} %collective-permute-done.1.refs_3_), channel_id=1, source_target_pairs={{0,1},{1,0},{2,3},{3,2},{4,5},{5,4},{6,7},{7,6},{8,9},{9,8},{10,11... | collective-permute-start | bytes 786440 | tf_op jit(solution)/shard_map/ppermute | solution.py:361
  29.1 2.8 %collective-permute-done.4.refs_6_ = bf16[2,128,512]{2,1,0:T(8,128)(2,1)S(1)} collective-permute-done((bf16[2,128,512]{2,1,0:T(8,128)(2,1)S(1)}, bf16[2,128,512]{2,1,0:T(8,128)(2,1)S(1)}, u32[]{:S(2)}, u32[]{:S(2)}) %collective-permute-start.4) | collective-permute-done | bytes 262176 | tf_op jit(solution)/shard_map/ppermute | solution.py:356
  31.9 1.6 %collective-permute-start.11 = (bf16[2,128,512]{2,1,0:T(8,128)(2,1)S(1)}, bf16[2,128,512]{2,1,0:T(8,128)(2,1)S(1)}, u32[]{:S(2)}, u32[]{:S(2)}) collective-permute-start(bf16[2,128,512]{2,1,0:T(8,128)(2,1)S(1)} %collective-permute-done.2.refs_4_), channel_id=1, source_target_pairs={{0,1},{1,0},{2,3},{3,2},{4,5},{5,4},{6,7},{7,6},{8,9},{9,8},{10,11... | collective-permute-start | bytes 786440 | tf_op jit(solution)/shard_map/ppermute | solution.py:361
  33.5 0.9 %maximum_maximum_fusion.1.refs_19_ = bf16[256,512]{1,0:T(8,128)(2,1)S(1)} fusion(bf16[128,256]{1,0:T(8,128)(2,1)S(1)} %get-tuple-element.6, bf16[128,256]{1,0:T(8,128)(2,1)} %get-tuple-element.12, bf16[128,256]{1,0:T(8,128)(2,1)} %get-tuple-element.11), kind=kLoop, calls=%fused_computation.4 | loop fusion | flops 1048576 | bytes 458752 | tf_op jit(solution)/shard_map/jit(block)/concatenate | solution.py:370
  34.4 1.5 %collective-permute-start.6 = (bf16[1,128,512]{2,1,0:T(8,128)(2,1)S(1)}, bf16[1,128,512]{2,1,0:T(8,128)(2,1)S(1)}, u32[]{:S(2)}, u32[]{:S(2)}) collective-permute-start(bf16[1,128,512]{2,1,0:T(8,128)(2,1)S(1)} %slice.50), channel_id=1, source_target_pairs={{0,4},{4,8},{8,12},{12,14},{14,10},{10,6},{6,2},{2,0},{1,5},{5,9},... | collective-permute-start | bytes 393224 | tf_op jit(solution)/shard_map/ppermute | solution.py:359
  36.2 2.4 %collective-permute-start.12 = (bf16[2,128,512]{2,1,0:T(8,128)(2,1)S(1)}, bf16[2,128,512]{2,1,0:T(8,128)(2,1)S(1)}, u32[]{:S(2)}, u32[]{:S(2)}) collective-permute-start(bf16[2,128,512]{2,1,0:T(8,128)(2,1)S(1)} %collective-permute-done.3.refs_5_), channel_id=1, source_target_pairs={{0,1},{1,0},{2,3},{3,2},{4,5},{5,4},{6,7},{7,6},{8,9},{9,8},{10,11... | collective-permute-start | bytes 786440 | tf_op jit(solution)/shard_map/ppermute | solution.py:361
  39.2 2.1 %collective-permute-start.15 = (bf16[1,128,512]{2,1,0:T(8,128)(2,1)S(1)}, bf16[1,128,512]{2,1,0:T(8,128)(2,1)S(1)}, u32[]{:S(2)}, u32[]{:S(2)}) collective-permute-start(bf16[1,128,512]{2,1,0:T(8,128)(2,1)S(1)} %collective-permute-done.6.refs_8_), channel_id=1, source_target_pairs={{0,1},{1,0},{2,3},{3,2},{4,5},{5,4},{6,7},{7,6},{8,9},{9,8},{10,11... | collective-permute-start | bytes 393224 | tf_op jit(solution)/shard_map/ppermute | solution.py:361
  41.2 1.8 %collective-permute-start.16 = (bf16[1,128,512]{2,1,0:T(8,128)(2,1)S(1)}, bf16[1,128,512]{2,1,0:T(8,128)(2,1)S(1)}, u32[]{:S(2)}, u32[]{:S(2)}) collective-permute-start(bf16[1,128,512]{2,1,0:T(8,128)(2,1)S(1)} %collective-permute-done.7.refs_9_), channel_id=1, source_target_pairs={{0,1},{1,0},{2,3},{3,2},{4,5},{5,4},{6,7},{7,6},{8,9},{9,8},{10,11... | collective-permute-start | bytes 393224 | tf_op jit(solution)/shard_map/ppermute | solution.py:361
  43.2 0.8 %collective-permute-done.16.refs_18_ = bf16[1,128,512]{2,1,0:T(8,128)(2,1)S(1)} collective-permute-done((bf16[1,128,512]{2,1,0:T(8,128)(2,1)S(1)}, bf16[1,128,512]{2,1,0:T(8,128)(2,1)S(1)}, u32[]{:S(2)}, u32[]{:S(2)}) %collective-permute-start.16) | collective-permute-done | bytes 131104 | tf_op jit(solution)/shard_map/ppermute | solution.py:361
  44.1 20.1 %backproject.1 = f32[1,2,256,512]{3,2,1,0:T(8,128)} custom-call(s32[11]{0:T(128)S(1)} %pad_add_fusion.2.refs_0_, bf16[2,128,512]{2,1,0:T(8,128)(2,1)S(1)} %copy-done, bf16[2,128,512]{2,1,0:T(8,128)(2,1)S(1)} %collective-permute-done.refs_2_, bf16[2,128,512]{2,1,0:T(8,128)(2,1)S(1)} %collective-permute-done.1.refs_3_, ...), custom_call_target="tpu_custom_call" | custom-call | tf_op jit(solution)/shard_map/backproject/pallas_call | solution.py:392
  (91 shorter events, 5.0 us)
Async XLA Ops:
  0.0 16.5 %collective-permute-start = (bf16[2,128,512]{2,1,0:T(8,128)(2,1)}, bf16[2,128,512]{2,1,0:T(8,128)(2,1)S(1)}, u32[]{:S(2)}, u32[]{:S(2)}) collective-permute-start(bf16[2,128,512]{2,1,0:T(8,128)(2,1)} %refs_1_.1), channel_id=1, source_target_pairs={{0,4},{4,8},{8,12},{12,14},{14,10},{10,6},{6,2},{2,0},{1,5},{5,9},... | collective-permute-start | bytes 786440 | tf_op jit(solution)/shard_map/ppermute | solution.py:356
  2.1 17.8 %collective-permute-start.1 = (bf16[2,128,512]{2,1,0:T(8,128)(2,1)}, bf16[2,128,512]{2,1,0:T(8,128)(2,1)S(1)}, u32[]{:S(2)}, u32[]{:S(2)}) collective-permute-start(bf16[2,128,512]{2,1,0:T(8,128)(2,1)} %refs_1_.1), channel_id=1, source_target_pairs={{4,0},{8,4},{12,8},{14,12},{10,14},{6,10},{2,6},{0,2},{5,1},{9,5},... | collective-permute-start | bytes 786440 | tf_op jit(solution)/shard_map/ppermute | solution.py:356
  2.1 33.8 %collective-permute-start.8 = (bf16[2,128,512]{2,1,0:T(8,128)(2,1)}, bf16[2,128,512]{2,1,0:T(8,128)(2,1)S(1)}, u32[]{:S(2)}, u32[]{:S(2)}) collective-permute-start(bf16[2,128,512]{2,1,0:T(8,128)(2,1)} %refs_1_.1), channel_id=1, source_target_pairs={{0,1},{1,0},{2,3},{3,2},{4,5},{5,4},{6,7},{7,6},{8,9},{9,8},{10,11... | collective-permute-start | bytes 786440 | tf_op jit(solution)/shard_map/ppermute | solution.py:361
  6.1 8.9 %copy-start.1 = (f32[256,256]{1,0:T(8,128)S(1)}, f32[256,256]{1,0:T(8,128)}, u32[]{:S(2)}) copy-start(f32[256,256]{1,0:T(8,128)} %param.11) | copy-start | bytes 786436
  8.6 19.3 %copy-start.5 = (s32[2,2,2,256]{3,2,1,0:T(2,128)S(1)}, s32[2,2,2,256]{3,2,1,0:T(2,128)}, u32[]{:S(2)}) copy-start(s32[2,2,2,256]{3,2,1,0:T(2,128)} %param.13) | copy-start | bytes 24580
  15.0 21.2 %copy-start.6 = (s32[2,2,2,256]{3,2,1,0:T(2,128)S(1)}, s32[2,2,2,256]{3,2,1,0:T(2,128)}, u32[]{:S(2)}) copy-start(s32[2,2,2,256]{3,2,1,0:T(2,128)} %param.12) | copy-start | bytes 24580
  16.5 8.2 %collective-permute-start.2 = (bf16[2,128,512]{2,1,0:T(8,128)(2,1)S(1)}, bf16[2,128,512]{2,1,0:T(8,128)(2,1)S(1)}, u32[]{:S(2)}, u32[]{:S(2)}) collective-permute-start(bf16[2,128,512]{2,1,0:T(8,128)(2,1)S(1)} %collective-permute-done.refs_2_), channel_id=1, source_target_pairs={{0,4},{4,8},{8,12},{12,14},{14,10},{10,6},{6,2},{2,0},{1,5},{5,9},... | collective-permute-start | bytes 786440 | tf_op jit(solution)/shard_map/ppermute | solution.py:356
  19.9 7.6 %collective-permute-start.3 = (bf16[2,128,512]{2,1,0:T(8,128)(2,1)S(1)}, bf16[2,128,512]{2,1,0:T(8,128)(2,1)S(1)}, u32[]{:S(2)}, u32[]{:S(2)}) collective-permute-start(bf16[2,128,512]{2,1,0:T(8,128)(2,1)S(1)} %collective-permute-done.1.refs_3_), channel_id=1, source_target_pairs={{4,0},{8,4},{12,8},{14,12},{10,14},{6,10},{2,6},{0,2},{5,1},{9,5},... | collective-permute-start | bytes 786440 | tf_op jit(solution)/shard_map/ppermute | solution.py:356
  24.8 7.2 %collective-permute-start.4 = (bf16[2,128,512]{2,1,0:T(8,128)(2,1)S(1)}, bf16[2,128,512]{2,1,0:T(8,128)(2,1)S(1)}, u32[]{:S(2)}, u32[]{:S(2)}) collective-permute-start(bf16[2,128,512]{2,1,0:T(8,128)(2,1)S(1)} %collective-permute-done.2.refs_4_), channel_id=1, source_target_pairs={{0,4},{4,8},{8,12},{12,14},{14,10},{10,6},{6,2},{2,0},{1,5},{5,9},... | collective-permute-start | bytes 786440 | tf_op jit(solution)/shard_map/ppermute | solution.py:356
  26.2 17.8 %copy-start = (bf16[2,128,512]{2,1,0:T(8,128)(2,1)S(1)}, bf16[2,128,512]{2,1,0:T(8,128)(2,1)}, u32[]{:S(2)}) copy-start(bf16[2,128,512]{2,1,0:T(8,128)(2,1)} %refs_1_.1) | copy-start | bytes 786436
  27.6 6.9 %collective-permute-start.5 = (bf16[2,128,512]{2,1,0:T(8,128)(2,1)S(1)}, bf16[2,128,512]{2,1,0:T(8,128)(2,1)S(1)}, u32[]{:S(2)}, u32[]{:S(2)}) collective-permute-start(bf16[2,128,512]{2,1,0:T(8,128)(2,1)S(1)} %collective-permute-done.3.refs_5_), channel_id=1, source_target_pairs={{4,0},{8,4},{12,8},{14,12},{10,14},{6,10},{2,6},{0,2},{5,1},{9,5},... | collective-permute-start | bytes 786440 | tf_op jit(solution)/shard_map/ppermute | solution.py:356
  27.9 15.3 %copy-start.2 = (bf16[256,256]{1,0:T(8,128)(2,1)S(1)}, bf16[256,256]{1,0:T(8,128)(2,1)}, u32[]{:S(2)}) copy-start(bf16[256,256]{1,0:T(8,128)(2,1)} %multiply_convert_fusion.1) | copy-start | bytes 393220
  27.9 15.3 %copy-start.3 = (bf16[256,256]{1,0:T(8,128)(2,1)S(1)}, bf16[256,256]{1,0:T(8,128)(2,1)}, u32[]{:S(2)}) copy-start(bf16[256,256]{1,0:T(8,128)(2,1)} %get-tuple-element.7) | copy-start | bytes 393220
  27.9 15.3 %copy-start.4 = (bf16[256,256]{1,0:T(8,128)(2,1)S(1)}, bf16[256,256]{1,0:T(8,128)(2,1)}, u32[]{:S(2)}) copy-start(bf16[256,256]{1,0:T(8,128)(2,1)} %get-tuple-element.8) | copy-start | bytes 393220
  27.9 8.3 %collective-permute-start.10 = (bf16[2,128,512]{2,1,0:T(8,128)(2,1)S(1)}, bf16[2,128,512]{2,1,0:T(8,128)(2,1)S(1)}, u32[]{:S(2)}, u32[]{:S(2)}) collective-permute-start(bf16[2,128,512]{2,1,0:T(8,128)(2,1)S(1)} %collective-permute-done.1.refs_3_), channel_id=1, source_target_pairs={{0,1},{1,0},{2,3},{3,2},{4,5},{5,4},{6,7},{7,6},{8,9},{9,8},{10,11... | collective-permute-start | bytes 786440 | tf_op jit(solution)/shard_map/ppermute | solution.py:361
  29.1 9.6 %collective-permute-start.9 = (bf16[2,128,512]{2,1,0:T(8,128)(2,1)S(1)}, bf16[2,128,512]{2,1,0:T(8,128)(2,1)S(1)}, u32[]{:S(2)}, u32[]{:S(2)}) collective-permute-start(bf16[2,128,512]{2,1,0:T(8,128)(2,1)S(1)} %collective-permute-done.refs_2_), channel_id=1, source_target_pairs={{0,1},{1,0},{2,3},{3,2},{4,5},{5,4},{6,7},{7,6},{8,9},{9,8},{10,11... | collective-permute-start | bytes 786440 | tf_op jit(solution)/shard_map/ppermute | solution.py:361
  31.9 6.8 %collective-permute-start.11 = (bf16[2,128,512]{2,1,0:T(8,128)(2,1)S(1)}, bf16[2,128,512]{2,1,0:T(8,128)(2,1)S(1)}, u32[]{:S(2)}, u32[]{:S(2)}) collective-permute-start(bf16[2,128,512]{2,1,0:T(8,128)(2,1)S(1)} %collective-permute-done.2.refs_4_), channel_id=1, source_target_pairs={{0,1},{1,0},{2,3},{3,2},{4,5},{5,4},{6,7},{7,6},{8,9},{9,8},{10,11... | collective-permute-start | bytes 786440 | tf_op jit(solution)/shard_map/ppermute | solution.py:361
  34.4 4.7 %collective-permute-start.6 = (bf16[1,128,512]{2,1,0:T(8,128)(2,1)S(1)}, bf16[1,128,512]{2,1,0:T(8,128)(2,1)S(1)}, u32[]{:S(2)}, u32[]{:S(2)}) collective-permute-start(bf16[1,128,512]{2,1,0:T(8,128)(2,1)S(1)} %slice.50), channel_id=1, source_target_pairs={{0,4},{4,8},{8,12},{12,14},{14,10},{10,6},{6,2},{2,0},{1,5},{5,9},... | collective-permute-start | bytes 393224 | tf_op jit(solution)/shard_map/ppermute | solution.py:359
  35.9 5.3 %collective-permute-start.7 = (bf16[1,128,512]{2,1,0:T(8,128)(2,1)S(1)}, bf16[1,128,512]{2,1,0:T(8,128)(2,1)S(1)}, u32[]{:S(2)}, u32[]{:S(2)}) collective-permute-start(bf16[1,128,512]{2,1,0:T(8,128)(2,1)S(1)} %slice.51), channel_id=1, source_target_pairs={{4,0},{8,4},{12,8},{14,12},{10,14},{6,10},{2,6},{0,2},{5,1},{9,5},... | collective-permute-start | bytes 393224 | tf_op jit(solution)/shard_map/ppermute | solution.py:359
  36.2 7.0 %collective-permute-start.12 = (bf16[2,128,512]{2,1,0:T(8,128)(2,1)S(1)}, bf16[2,128,512]{2,1,0:T(8,128)(2,1)S(1)}, u32[]{:S(2)}, u32[]{:S(2)}) collective-permute-start(bf16[2,128,512]{2,1,0:T(8,128)(2,1)S(1)} %collective-permute-done.3.refs_5_), channel_id=1, source_target_pairs={{0,1},{1,0},{2,3},{3,2},{4,5},{5,4},{6,7},{7,6},{8,9},{9,8},{10,11... | collective-permute-start | bytes 786440 | tf_op jit(solution)/shard_map/ppermute | solution.py:361
  38.6 5.4 %collective-permute-start.13 = (bf16[2,128,512]{2,1,0:T(8,128)(2,1)S(1)}, bf16[2,128,512]{2,1,0:T(8,128)(2,1)S(1)}, u32[]{:S(2)}, u32[]{:S(2)}) collective-permute-start(bf16[2,128,512]{2,1,0:T(8,128)(2,1)S(1)} %collective-permute-done.4.refs_6_), channel_id=1, source_target_pairs={{0,1},{1,0},{2,3},{3,2},{4,5},{5,4},{6,7},{7,6},{8,9},{9,8},{10,11... | collective-permute-start | bytes 786440 | tf_op jit(solution)/shard_map/ppermute | solution.py:361
  38.7 5.3 %collective-permute-start.14 = (bf16[2,128,512]{2,1,0:T(8,128)(2,1)S(1)}, bf16[2,128,512]{2,1,0:T(8,128)(2,1)S(1)}, u32[]{:S(2)}, u32[]{:S(2)}) collective-permute-start(bf16[2,128,512]{2,1,0:T(8,128)(2,1)S(1)} %collective-permute-done.5.refs_7_), channel_id=1, source_target_pairs={{0,1},{1,0},{2,3},{3,2},{4,5},{5,4},{6,7},{7,6},{8,9},{9,8},{10,11... | collective-permute-start | bytes 786440 | tf_op jit(solution)/shard_map/ppermute | solution.py:361
  39.2 4.1 %collective-permute-start.15 = (bf16[1,128,512]{2,1,0:T(8,128)(2,1)S(1)}, bf16[1,128,512]{2,1,0:T(8,128)(2,1)S(1)}, u32[]{:S(2)}, u32[]{:S(2)}) collective-permute-start(bf16[1,128,512]{2,1,0:T(8,128)(2,1)S(1)} %collective-permute-done.6.refs_8_), channel_id=1, source_target_pairs={{0,1},{1,0},{2,3},{3,2},{4,5},{5,4},{6,7},{7,6},{8,9},{9,8},{10,11... | collective-permute-start | bytes 393224 | tf_op jit(solution)/shard_map/ppermute | solution.py:361
  41.2 2.8 %collective-permute-start.16 = (bf16[1,128,512]{2,1,0:T(8,128)(2,1)S(1)}, bf16[1,128,512]{2,1,0:T(8,128)(2,1)S(1)}, u32[]{:S(2)}, u32[]{:S(2)}) collective-permute-start(bf16[1,128,512]{2,1,0:T(8,128)(2,1)S(1)} %collective-permute-done.7.refs_9_), channel_id=1, source_target_pairs={{0,1},{1,0},{2,3},{3,2},{4,5},{5,4},{6,7},{7,6},{8,9},{9,8},{10,11... | collective-permute-start | bytes 393224 | tf_op jit(solution)/shard_map/ppermute | solution.py:361
  (1 other events, 5.2 us)

commit v2 on v0

--- a/solution.py
+++ b/solution.py
@@ -1,6 +1,10 @@
+import functools
+
 import jax
 import jax.numpy as jnp
 from jax import lax
+from jax.experimental import pallas as pl
+from jax.experimental.pallas import tpu as pltpu
 from jax.sharding import PartitionSpec as P
 
 INTERP_LEN = 8
@@ -101,7 +105,7 @@
     )
 
 
-def shards(echoes, chirp_taps, steer_phase, ang_table, range_table, interp_taps, phase_twist):
+def level_by_level(echoes, chirp_taps, steer_phase, ang_table, range_table, interp_taps, phase_twist):
     tap_count = chirp_taps.shape[1]
     kernel = toeplitz_matrix(chirp_taps)
     upper_rim = from_behind(echoes[:, :, :tap_count], "range", -1)
@@ -145,9 +149,342 @@
     return images[None]
 
 
+LANES = 128
+SUBS = 8
+STEP = 16
+SPAN = 2 * RIM_CELLS
+NEAR = 2 * INTERP_LEN
+FAR = NEAR + 2 * STEP
+
+
+def table_kernel(meta, chirp, phase, ang, offset, taps, twist, near_mat, edge_mat, steer, *outs, total):
+    core, slot, column = meta[0], meta[1], meta[2]
+    bins = total // 2
+    pulses = phase.shape[0] // 2
+    beams = phase.shape[1]
+    shape = (LANES, 2 * LANES)
+    t_r, t_i = (
+        pltpu.roll(jnp.broadcast_to(chirp[i : i + 1, :], shape), 0, 1, stride=1, stride_axis=0)
+        for i in (0, 1)
+    )
+    for matrix, rows, cols in ((near_mat, LANES, 2 * LANES), (edge_mat, SPAN, LANES)):
+        real, imag = t_r[:rows, :cols].astype(jnp.bfloat16), t_i[:rows, :cols].astype(jnp.bfloat16)
+        matrix[:rows, :cols] = real
+        matrix[:rows, cols:] = imag
+        matrix[rows:, :cols] = -imag
+        matrix[rows:, cols:] = real
+    scale = phase.shape[0] ** (-0.5)
+    for x in (0, 1):
+        half = column ^ x
+        angle = phase[pl.ds(pl.multiple_of(half * pulses, pulses), pulses), :]
+        cos_part = (jnp.cos(angle) * scale).astype(jnp.bfloat16)
+        sin_part = (-jnp.sin(angle) * scale).astype(jnp.bfloat16)
+        low, high = x * pulses, (x + 1) * pulses
+        steer[low:high, :beams] = cos_part
+        steer[low:high, beams:] = sin_part
+        steer[2 * pulses + low : 2 * pulses + high, :beams] = -sin_part
+        steer[2 * pulses + low : 2 * pulses + high, beams:] = cos_part
+    sub = lax.broadcasted_iota(jnp.int32, (SUBS, LANES), 0)
+
+    def rows(line):
+        return jnp.where((sub & 1) == 0, line[:, :LANES], line[:, LANES:])
+
+    sign = jnp.where(sub < SUBS // 2, 1.0, -1.0)
+    ang_out, shift_out = outs[0], outs[1]
+    todo = []
+    for level in (0, 1):
+        table = outs[2 + level]
+        own = (slot >> level) & 1
+        for order in (0, 1):
+            child = own if order == 0 else 1 - own
+            ang_out[level, order] = ang[level, own, pl.ds(child, 1), :]
+            shift_out[level, order] = rows(offset[level, own, pl.ds(child, 1), :]) + (
+                RIM_CELLS - INTERP_LEN // 2 + 1
+            )
+            for t in range(INTERP_LEN):
+                table[order, t] = rows(taps[level, own, child, 0, t : t + 1, :])
+                table[order, INTERP_LEN + t] = sign * rows(taps[level, own, child, 1, t : t + 1, :])
+            rate = sign * rows(twist[level, own, pl.ds(child, 1), :])
+            half_bins = (bins + SPAN) // 2 if level == 0 else bins // 2
+            first = core * bins + ((sub >> 1) & 1) * half_bins
+            first = first - RIM_CELLS if level == 0 else first
+            todo.append((table, order, rate, first, half_bins // STEP))
+
+    def turn(step, carry):
+        for table, order, rate, first, steps in todo:
+            near = rate * (step.astype(jnp.float32) / total)
+            table[order, NEAR + step] = jnp.cos(near)
+            table[order, NEAR + STEP + step] = jnp.sin(near)
+            far = rate * ((first + STEP * step).astype(jnp.float32) / total)
+            table[order, FAR + step] = jnp.cos(far)
+            table[order, FAR + steps + step] = jnp.sin(far)
+        return carry
+
+    lax.fori_loop(0, STEP, turn, 0)
+    for table, order, rate, first, steps in todo:
+        for step in range(STEP, steps):
+            far = rate * ((first + STEP * step).astype(jnp.float32) / total)
+            table[order, FAR + step] = jnp.cos(far)
+            table[order, FAR + steps + step] = jnp.sin(far)
+
+
+def squeeze(piece, rim, core, near_mat, edge_mat, c_ref, index):
+    bins = piece.shape[-1]
+
+    def columns(low, high):
+        found = []
+        for ri in (0, 1):
+            tiles = []
+            for tile in range(low, high):
+                if tile == 0:
+                    other = rim[ri, :, bins - LANES :]
+                    tiles.append(jnp.where(core == 1, other, jnp.zeros_like(other)))
+                elif tile == bins // LANES + 1:
+                    other = rim[ri, :, :LANES]
+                    tiles.append(jnp.where(core == 0, other, jnp.zeros_like(other)))
+                else:
+                    tiles.append(piece[ri, :, (tile - 1) * LANES : tile * LANES])
+            found += tiles
+        return jnp.concatenate(found, axis=1)
+
+    def times(matrix, cols):
+        return lax.dot_general(
+            matrix, cols, (((1,), (1,)), ((), ())), preferred_element_type=jnp.float32
+        )
+
+    for block in range(bins // LANES + 2):
+        if block == 0:
+            rows = jnp.concatenate([near_mat[LANES - SPAN : LANES], near_mat[2 * LANES - SPAN :]], 0)
+            result = times(rows, columns(0, 2))
+            result = jnp.where(core == 1, result, 0.0).astype(jnp.bfloat16)
+            place, count = 0, SPAN
+        elif block <= bins // LANES:
+            result = times(near_mat[...], columns(block, block + 2)).astype(jnp.bfloat16)
+            place, count = SPAN + (block - 1) * LANES, LANES
+        else:
+            result = times(edge_mat[...], columns(block, block + 1)).astype(jnp.bfloat16)
+            place, count = SPAN + bins, SPAN
+        c_ref[index, 0, place : place + count] = result[:count]
+        c_ref[index, 1, place : place + count] = result[count:]
+
+
+def form(c_ref, steer, x_ref):
+    pieces = [c_ref[i, ri] for ri in (0, 1) for i in (0, 1)]
+    image = jnp.dot(
+        jnp.concatenate(pieces, axis=1), steer[...], preferred_element_type=jnp.float32
+    ).astype(jnp.bfloat16)
+    beams = x_ref.shape[2]
+    x_ref[0] = image[:, :beams]
+    x_ref[1] = image[:, beams:]
+
+
+def merge_child(x_ref, ang, shift, table, s_ref, y_ref, base_ref, o_ref, half_bins):
+    beams = x_ref.shape[2]
+    beam_index = lax.broadcasted_iota(jnp.int32, (beams, beams), 0)
+    hits = jnp.where(beam_index == ang[...], 1.0, 0.0).astype(jnp.bfloat16)
+    length = half_bins + SPAN
+    for ri in (0, 1):
+        picked = jnp.dot(x_ref[ri], hits, preferred_element_type=jnp.float32)
+        for half in (0, 1):
+            for part in (0, 1):
+                s_ref[pl.ds(ri * 4 + half * 2 + part, length, stride=SUBS), :] = picked[
+                    half * half_bins : half * half_bins + length, part * LANES : (part + 1) * LANES
+                ]
+    offset = shift[...]
+    bits = [(offset & (1 << b)) != 0 for b in range(5)]
+    steps = half_bins // STEP
+    for step in range(steps + 1):
+        base = step * STEP
+        row = [s_ref[pl.ds((base + k) * SUBS, SUBS), :] for k in range(STEP + 31)]
+        for b in (4, 3, 2, 1, 0):
+            d = 1 << b
+            row = [jnp.where(bits[b], row[k + d], row[k]) for k in range(len(row) - d)]
+        for k in range(STEP):
+            y_ref[pl.ds((base + k) * SUBS, SUBS), :] = row[k]
+    taps = INTERP_LEN
+    for step in range(steps):
+        far_r, far_i = table[FAR + step], table[FAR + steps + step]
+        w_r, w_i = [], []
+        for t in range(taps):
+            a, b = table[t], table[taps + t]
+            w_r.append(a * far_r - b * far_i)
+            w_i.append(a * far_i + b * far_r)
+        for low in range(0, STEP, SUBS):
+            base = step * STEP + low
+            row = [y_ref[pl.ds((base + k) * SUBS, SUBS), :] for k in range(SUBS + taps - 1)]
+            for k in range(SUBS):
+                a, b = row[k] * w_r[0], row[k] * w_i[0]
+                for t in range(1, taps):
+                    a = a + row[k + t] * w_r[t]
+                    b = b + row[k + t] * w_i[t]
+                e_r, e_i = table[NEAR + low + k], table[NEAR + STEP + low + k]
+                value = (e_r * a - e_i * b) + pltpu.roll(e_i * a + e_r * b, SUBS // 2, 0)
+                place = pl.ds((base + k) * SUBS, SUBS)
+                o_ref[place, :] = value if base_ref is None else base_ref[place, :] + value
+
+
+def merged_image(o_ref, x_ref, half_bins, first_bin, total):
+    for half in (0, 1):
+        bin_index = lax.broadcasted_iota(jnp.int32, (half_bins, 2 * LANES), 0)
+        bin_index = bin_index + (first_bin + half * half_bins)
+        inside = (bin_index >= 0) & (bin_index < total)
+        for ri in (0, 1):
+            value = jnp.concatenate(
+                [
+                    o_ref[pl.ds(ri * 4 + half * 2 + part, half_bins, stride=SUBS), :]
+                    for part in (0, 1)
+                ],
+                axis=1,
+            )
+            x_ref[ri, half * half_bins : (half + 1) * half_bins] = jnp.where(
+                inside, value, 0.0
+            ).astype(jnp.bfloat16)
+
+
+def finished(o_ref, out_ref, half_bins):
+    for ri in (0, 1):
+        for half in (0, 1):
+            for part in (0, 1):
+                value = o_ref[pl.ds(ri * 4 + half * 2 + part, half_bins, stride=SUBS), :]
+                out_ref[
+                    0, ri, part * LANES : (part + 1) * LANES, half * half_bins : (half + 1) * half_bins
+                ] = value.T
+
+
+def stage_kernel(stage, total, *refs):
+    (meta, first, first_rim, second, second_rim, near_mat, edge_mat, steer, ang, shift, table0) = refs[:11]
+    refs = refs[11:]
+    core = meta[0]
+    bins = total // 2
+    half0, half1 = (bins + SPAN) // 2, bins // 2
+    order = stage & 1
+    table1 = base0 = base1 = None
+    if order == 1:
+        table1, base0, refs = refs[0], refs[1], refs[2:]
+    if stage == 3:
+        base1, refs = refs[0], refs[1:]
+    out_ref, c_ref, x0_ref, s_ref, y_ref = refs[:5]
+    squeeze(first, first_rim, core, near_mat, edge_mat, c_ref, 0)
+    squeeze(second, second_rim, core, near_mat, edge_mat, c_ref, 1)
+    form(c_ref, steer, x0_ref)
+    o_ref = out_ref if order == 0 else refs[5]
+    merge_child(
+        x0_ref, ang.at[0, order], shift.at[0, order], table0.at[order], s_ref, y_ref, base0, o_ref, half0
+    )
+    if order == 0:
+        return
+    x1_ref = refs[6]
+    merged_image(o_ref, x1_ref, half0, core * bins - RIM_CELLS, total)
+    which = stage >> 1
+    final = out_ref if stage == 1 else refs[7]
+    merge_child(
+        x1_ref, ang.at[1, which], shift.at[1, which], table1.at[which], s_ref, y_ref, base1, final, half1
+    )
+    if stage == 3:
+        finished(final, out_ref, half1)
+
+
+def ring_of_chips(echoes, chirp_taps, steer_phase, ang_table, range_table, interp_taps, phase_twist):
+    pulses, bins = echoes.shape[1:]
+    beams = steer_phase.shape[1]
+    total = bins * lax.axis_size("range")
+    slots = lax.axis_size("aperture")
+    slot, column, core = (lax.axis_index(a) for a in ("aperture", "beam", "range"))
+    axes = ("aperture", "beam")
+    order = [z * 2 for z in range(slots)] + [z * 2 + 1 for z in reversed(range(slots))]
+    ahead = [(order[i], order[(i + 1) % len(order)]) for i in range(len(order))]
+    behind = [(b, a) for a, b in ahead]
+    across = [(2 * z + x, 2 * z + 1 - x) for z in range(1, slots - 1) for x in (0, 1)]
+    kind = jnp.where(column == 0, slot, slots - 1 - slot)
+    half0, half1 = (bins + SPAN) // 2, bins // 2
+    window = bins + 2 * SPAN
+    meta = jnp.stack([core, slot, column]).astype(jnp.int32)
+
+    def other_core(x):
+        return lax.ppermute(x, "range", [(0, 1), (1, 0)])
+
+    def choose(*options):
+        picked = options[-1]
+        for value, option in enumerate(options[:-1]):
+            if option is not picked:
+                picked = jnp.where(kind == value, option, picked)
+        return picked
+
+    smem, vmem = pl.BlockSpec(memory_space=pltpu.SMEM), pl.BlockSpec(memory_space=pltpu.VMEM)
+    f32, bf16, i32 = jnp.float32, jnp.bfloat16, jnp.int32
+    rows0 = NEAR + 2 * STEP + 2 * (half0 // STEP)
+    rows1 = NEAR + 2 * STEP + 2 * (half1 // STEP)
+    chirp = jnp.pad(chirp_taps.astype(f32), ((0, 0), (0, 2 * LANES - chirp_taps.shape[1])))
+    tables = pl.pallas_call(
+        functools.partial(table_kernel, total=total),
+        out_shape=[
+            jax.ShapeDtypeStruct((2 * LANES, 4 * LANES), bf16),
+            jax.ShapeDtypeStruct((2 * SPAN, 2 * LANES), bf16),
+            jax.ShapeDtypeStruct((4 * pulses, 2 * beams), bf16),
+            jax.ShapeDtypeStruct((2, 2, 1, beams), i32),
+            jax.ShapeDtypeStruct((2, 2, SUBS, LANES), i32),
+            jax.ShapeDtypeStruct((2, rows0, SUBS, LANES), f32),
+            jax.ShapeDtypeStruct((2, rows1, SUBS, LANES), f32),
+        ],
+        in_specs=[smem] + [vmem] * 6,
+        out_specs=[vmem] * 7,
+        compiler_params=pltpu.CompilerParams(vmem_limit_bytes=16 * 1024 * 1024),
+        cost_estimate=pl.CostEstimate(flops=10**9, bytes_accessed=4 * 2**20, transcendentals=0),
+        name="tables",
+    )(meta, chirp, steer_phase, ang_table, range_table, interp_taps, phase_twist)
+    shared, table0, table1 = tables[:5], tables[5], tables[6]
+
+    def run(stage, first, second, *carried):
+        rows = (half0 + SPAN + 32) * SUBS
+        if stage == 3:
+            out = jax.ShapeDtypeStruct((1, 2, beams, bins), f32)
+        else:
+            out = jax.ShapeDtypeStruct(((half1 if stage == 1 else half0) * SUBS, LANES), f32)
+        scratch = [
+            pltpu.VMEM((2, 2, window, pulses), bf16),
+            pltpu.VMEM((2, window, beams), bf16),
+            pltpu.VMEM((rows, LANES), f32),
+            pltpu.VMEM((rows, LANES), f32),
+        ]
+        if stage & 1:
+            scratch.append(pltpu.VMEM((half0 * SUBS, LANES), f32))
+            scratch.append(pltpu.VMEM((2, window - SPAN, beams), bf16))
+        if stage == 3:
+            scratch.append(pltpu.VMEM((half1 * SUBS, LANES), f32))
+        given = [meta, first[0], first[1], second[0], second[1], *shared, table0, *carried]
+        return pl.pallas_call(
+            functools.partial(stage_kernel, stage, total),
+            out_shape=out,
+            in_specs=[smem] + [vmem] * (len(given) - 1),
+            out_specs=vmem,
+            scratch_shapes=scratch,
+            compiler_params=pltpu.CompilerParams(vmem_limit_bytes=24 * 1024 * 1024),
+            cost_estimate=pl.CostEstimate(
+                flops=3 * 10**9, bytes_accessed=4 * 2**20, transcendentals=0
+            ),
+            name=f"stage{stage}",
+        )(*given)
+
+    up1, down1 = lax.ppermute(echoes, axes, ahead), lax.ppermute(echoes, axes, behind)
+    side = lax.ppermute(echoes, axes, across)
+    up2, down2 = lax.ppermute(up1, axes, ahead), lax.ppermute(down1, axes, behind)
+    up3, down3 = lax.ppermute(up2, axes, ahead), lax.ppermute(down2, axes, behind)
+    far = jnp.concatenate(
+        [lax.ppermute(up3[:1], axes, ahead), lax.ppermute(down3[1:], axes, behind)], axis=0
+    )
+    pair = lambda x: (x, other_core(x))
+    part = run(0, pair(echoes), pair(choose(up1, side, side, down1)))
+    near = run(
+        1, pair(choose(down1, up1, down1, up1)), pair(choose(up2, up2, down2, down2)), table1, part
+    )
+    part = run(2, pair(choose(down2, down2, up2, up2)), pair(choose(up3, down3, up3, down3)))
+    return run(3, pair(choose(down3, down1, up1, up3)), pair(far), table1, part, near)
+
+
 def solution(mesh):
+    small = (mesh.shape["aperture"], mesh.shape["beam"], mesh.shape["range"]) == (4, 2, 2)
     return jax.shard_map(
-        shards,
+        ring_of_chips if small else level_by_level,
         mesh=mesh,
         in_specs=(
             P(None, ("groups", "aperture", "beam"), "range"),

time: 179 us -> 56.4 us (0.32)
  other arithmetic: 73.3 us -> 0.92 us
  waiting for transfers between devices: 42.3 us -> 11.8 us
  local copies, waits for them, and re-layouts: 30.1 us -> 3.99 us
  Pallas kernels: 0 us -> 23.4 us
  blocking collectives: 9.49 us -> 0 us
  matrix products: 4.57 us -> 0 us
  between operations: 2.16 us -> 0.17 us
    ppermute x7 -> x17, waiting for transfers between devices: 42.3 us -> 11.8 us  [the longest x1 6.24 us: ring_of_chips(): lax.ppermute(echoes, axes, behind)]
    another operation x4 -> x1, other arithmetic: 29.5 us -> 0.08 us  [ring_of_chips(): meta = jnp.stack([core, slot, column]).astype(jnp.int32)]
    sub x6 -> x0, other arithmetic: 28.8 us -> none  [the longest x2 28.7 us: contribute(): real_part * cosine - imag_part * sine_value]
    pallas_call x0 -> x5, Pallas kernels: none -> 23.4 us  [the longest x4 19.6 us: run(): pl.pallas_call(functools.partial(stage_kernel, stage, total), out_shape=o...]
    all_gather x1 -> x0, blocking collectives: 9.49 us -> none  [shards(): shard_rows = lax.all_gather(compressed, 'beam', axis=1, tiled=True)]
    gather x4 -> x0, local copies, waits for them, and re-layouts: 8.64 us -> none  [contribute(): picked = jnp.take(extended, angles, axis=1)]
    slice x20 -> x2, local copies, waits for them, and re-layouts: 6.83 us -> 0.02 us  [the longest x1 0.01 us: ring_of_chips(): up3[:1]]
    add x3 -> x0, other arithmetic: 5.5 us -> none  [the longest x1 4.11 us: contribute(): real_part * sine_value + imag_part * cosine]
  transfers between devices with their start and end apart: 7 -> 17, of which waited for: 4 -> 4; matrix products, arithmetic and copies ran while one was open for 26% -> 2% of each run, Pallas kernels for 0% -> 29%
where the time goes in v2:
time: 56.4 us; the launch traced here: 55.7 us
  Pallas kernels  23.4 us (41%)
  starting transfers between devices  15.4 us (27%)
  waiting for transfers between devices  11.8 us (21%)
  local copies, waits for them, and re-layouts  3.99 us (7%)
  other arithmetic  0.92 us (2%)
    pallas_call x4, Pallas kernels, run(): pl.pallas_call(functools.partial(stage_kernel, stage, total), out_shape=o...  19.6 us
    ppermute x8, starting transfers between devices, other_core(): return lax.ppermute(x, 'range', [(0, 1), (1, 0)])  7.7 us
    ppermute x1, waiting for transfers between devices, ring_of_chips(): lax.ppermute(echoes, axes, behind)  6.24 us
    unnamed x13, local copies, waits for them, and re-layouts  3.96 us
    pallas_call x1, Pallas kernels, ring_of_chips(): pl.pallas_call(functools.partial(table_kernel, total=total), out_shape=[j...  3.83 us
    ppermute x1, waiting for transfers between devices, ring_of_chips(): lax.ppermute(up3[:1], axes, ahead)  2.69 us
    ppermute x1, waiting for transfers between devices, ring_of_chips(): lax.ppermute(down1, axes, behind)  2.57 us
    ppermute x1, starting transfers between devices, ring_of_chips(): lax.ppermute(echoes, axes, behind)  2.04 us
  transfers between devices with their start and end apart: 17, of which 4 were waited for; matrix products, arithmetic and copies ran while one was open for 2% of the time, Pallas kernels for 29%

profile of v2, /device:TPU:1, one launch (start us, length us, event | category | flops | bytes accessed | tf_op | source)
XLA Modules:
  0.0 55.7 jit_solution(4745451787883055955)
XLA Ops:
  0.0 2.0 %collective-permute-start.1 = (bf16[2,128,512]{2,1,0:T(8,128)(2,1)}, bf16[2,128,512]{2,1,0:T(8,128)(2,1)S(1)}, u32[]{:S(2)}, u32[]{:S(2)}) collective-permute-start(bf16[2,128,512]{2,1,0:T(8,128)(2,1)} %refs_1_.1), channel_id=1, source_target_pairs={{4,0},{8,4},{12,8},{14,12},{10,14},{6,10},{2,6},{0,2},{5,1},{9,5},... | collective-permute-start | bytes 786440 | tf_op jit(solution)/shard_map/ppermute | solution.py:468
  2.1 6.2 %collective-permute-done.1 = bf16[2,128,512]{2,1,0:T(8,128)(2,1)S(1)} collective-permute-done((bf16[2,128,512]{2,1,0:T(8,128)(2,1)}, bf16[2,128,512]{2,1,0:T(8,128)(2,1)S(1)}, u32[]{:S(2)}, u32[]{:S(2)}) %collective-permute-start.1) | collective-permute-done | bytes 262176 | tf_op jit(solution)/shard_map/ppermute | solution.py:468
  8.4 1.1 %collective-permute-start.2 = (bf16[2,128,512]{2,1,0:T(8,128)(2,1)S(1)}, bf16[2,128,512]{2,1,0:T(8,128)(2,1)S(1)}, u32[]{:S(2)}, u32[]{:S(2)}) collective-permute-start(bf16[2,128,512]{2,1,0:T(8,128)(2,1)S(1)} %collective-permute-done.1), channel_id=1, source_target_pairs={{4,0},{8,4},{12,8},{14,12},{10,14},{6,10},{2,6},{0,2},{5,1},{9,5},... | collective-permute-start | bytes 786440 | tf_op jit(solution)/shard_map/ppermute | solution.py:470
  9.8 0.7 %collective-permute-start.15 = (bf16[2,128,512]{2,1,0:T(8,128)(2,1)}, bf16[2,128,512]{2,1,0:T(8,128)(2,1)S(1)}, u32[]{:S(2)}, u32[]{:S(2)}) collective-permute-start(bf16[2,128,512]{2,1,0:T(8,128)(2,1)} %refs_1_.1), channel_id=1, source_target_pairs={{4,6},{6,4},{8,10},{10,8},{5,7},{7,5},{9,11},{11,9},{20,22},{22,20... | collective-permute-start | bytes 786440 | tf_op jit(solution)/shard_map/ppermute | solution.py:469
  10.5 1.9 %collective-permute-start.14 = (bf16[2,128,512]{2,1,0:T(8,128)(2,1)}, bf16[2,128,512]{2,1,0:T(8,128)(2,1)S(1)}, u32[]{:S(2)}, u32[]{:S(2)}) collective-permute-start(bf16[2,128,512]{2,1,0:T(8,128)(2,1)} %refs_1_.1), channel_id=1, source_target_pairs={{0,1},{1,0},{2,3},{3,2},{4,5},{5,4},{6,7},{7,6},{8,9},{9,8},{10,11... | collective-permute-start | bytes 786440 | tf_op jit(solution)/shard_map/ppermute | solution.py:404
  12.4 2.6 %collective-permute-done.2 = bf16[2,128,512]{2,1,0:T(8,128)(2,1)S(1)} collective-permute-done((bf16[2,128,512]{2,1,0:T(8,128)(2,1)S(1)}, bf16[2,128,512]{2,1,0:T(8,128)(2,1)S(1)}, u32[]{:S(2)}, u32[]{:S(2)}) %collective-permute-start.2) | collective-permute-done | bytes 262176 | tf_op jit(solution)/shard_map/ppermute | solution.py:470
  14.9 0.7 %collective-permute-start.3 = (bf16[2,128,512]{2,1,0:T(8,128)(2,1)S(1)}, bf16[2,128,512]{2,1,0:T(8,128)(2,1)S(1)}, u32[]{:S(2)}, u32[]{:S(2)}) collective-permute-start(bf16[2,128,512]{2,1,0:T(8,128)(2,1)S(1)} %collective-permute-done.2), channel_id=1, source_target_pairs={{4,0},{8,4},{12,8},{14,12},{10,14},{6,10},{2,6},{0,2},{5,1},{9,5},... | collective-permute-start | bytes 786440 | tf_op jit(solution)/shard_map/ppermute | solution.py:471
  15.7 0.9 %collective-permute-start.5 = (bf16[2,128,512]{2,1,0:T(8,128)(2,1)S(1)}, bf16[2,128,512]{2,1,0:T(8,128)(2,1)S(1)}, u32[]{:S(2)}, u32[]{:S(2)}) collective-permute-start(bf16[2,128,512]{2,1,0:T(8,128)(2,1)S(1)} %collective-permute-done.4), channel_id=1, source_target_pairs={{0,4},{4,8},{8,12},{12,14},{14,10},{10,6},{6,2},{2,0},{1,5},{5,9},... | collective-permute-start | bytes 786440 | tf_op jit(solution)/shard_map/ppermute | solution.py:471
  16.7 0.7 %pad_convert_fusion.chirp = f32[2,256]{1,0:T(2,128)S(1)} fusion(bf16[2,64]{1,0:T(2,128)(2,1)} %param.8), kind=kLoop, calls=%fused_computation.12 | loop fusion | flops 512 | bytes 2304 | tf_op jit(solution)/shard_map/jit(_pad)/pad | solution.py:417
  17.4 0.9 %copy-done = f32[256,256]{1,0:T(8,128)S(1)} copy-done((f32[256,256]{1,0:T(8,128)S(1)}, f32[256,256]{1,0:T(8,128)}, u32[]{:S(2)}) %copy-start) | copy-done | bytes 262168
  18.3 0.9 %copy-done.2 = f32[2,2,2,2,8,256]{5,4,3,2,1,0:T(8,128)S(1)} copy-done((f32[2,2,2,2,8,256]{5,4,3,2,1,0:T(8,128)S(1)}, f32[2,2,2,2,8,256]{5,4,3,2,1,0:T(8,128)}, u32[]{:S(2)}) %copy-start.2) | copy-done | bytes 131096
  19.2 0.7 %copy-done.3 = s32[2,2,2,256]{3,2,1,0:T(2,128)S(1)} copy-done((s32[2,2,2,256]{3,2,1,0:T(2,128)S(1)}, s32[2,2,2,256]{3,2,1,0:T(2,128)}, u32[]{:S(2)}) %copy-start.3) | copy-done | bytes 8216
  19.9 0.7 %copy-done.4 = s32[2,2,2,256]{3,2,1,0:T(2,128)S(1)} copy-done((s32[2,2,2,256]{3,2,1,0:T(2,128)S(1)}, s32[2,2,2,256]{3,2,1,0:T(2,128)}, u32[]{:S(2)}) %copy-start.4) | copy-done | bytes 8216
  20.6 0.7 %copy-done.5 = f32[2,2,2,256]{3,2,1,0:T(2,128)S(1)} copy-done((f32[2,2,2,256]{3,2,1,0:T(2,128)S(1)}, f32[2,2,2,256]{3,2,1,0:T(2,128)}, u32[]{:S(2)}) %copy-start.5) | copy-done | bytes 8216
  21.3 3.8 %tables.1 = (bf16[256,512]{1,0:T(8,128)(2,1)S(1)}, bf16[64,256]{1,0:T(8,128)(2,1)S(1)}, bf16[512,512]{1,0:T(8,128)(2,1)S(1)}, s32[2,2,1,256]{3,2,1,0:T(1,128)S(1...) custom-call(s32[3]{0:T(128)S(1)} %pad_add_fusion.meta.refs_0_, ...), custom_call_target="tpu_custom_call" | custom-call | flops 1000000000 | bytes 4194304 | tf_op jit(solution)/shard_map/tables/pallas_call | solution.py:418
  25.3 2.6 %collective-permute-start.16 = (bf16[2,128,512]{2,1,0:T(8,128)(2,1)S(1)}, bf16[2,128,512]{2,1,0:T(8,128)(2,1)S(1)}, u32[]{:S(2)}, u32[]{:S(2)}) collective-permute-start(bf16[2,128,512]{2,1,0:T(8,128)(2,1)S(1)} %get-tuple-element.19.refs_3_), channel_id=1, source_target_pairs={{0,1},{1,0},{2,3},{3,2},{4,5},{5,4},{6,7},{7,6},{8,9},{9,8},{10,11... | collective-permute-start | bytes 786440 | tf_op jit(solution)/shard_map/ppermute | solution.py:404
  27.9 1.2 %collective-permute-start.7 = (bf16[1,128,512]{2,1,0:T(8,128)(2,1)S(1)}, bf16[1,128,512]{2,1,0:T(8,128)(2,1)S(1)}, u32[]{:S(2)}, u32[]{:S(2)}) collective-permute-start(bf16[1,128,512]{2,1,0:T(8,128)(2,1)S(1)} %slice.8), channel_id=1, source_target_pairs={{0,4},{4,8},{8,12},{12,14},{14,10},{10,6},{6,2},{2,0},{1,5},{5,9},... | collective-permute-start | bytes 393224 | tf_op jit(solution)/shard_map/ppermute | solution.py:473
  30.4 2.7 %collective-permute-done.7 = bf16[1,128,512]{2,1,0:T(8,128)(2,1)S(1)} collective-permute-done((bf16[1,128,512]{2,1,0:T(8,128)(2,1)S(1)}, bf16[1,128,512]{2,1,0:T(8,128)(2,1)S(1)}, u32[]{:S(2)}, u32[]{:S(2)}) %collective-permute-start.7) | collective-permute-done | bytes 131104 | tf_op jit(solution)/shard_map/ppermute | solution.py:473
  33.1 0.8 %collective-permute-start.10 = (bf16[2,128,512]{2,1,0:T(8,128)(2,1)S(1)}, bf16[2,128,512]{2,1,0:T(8,128)(2,1)S(1)}, u32[]{:S(2)}, u32[]{:S(2)}) collective-permute-start(bf16[2,128,512]{2,1,0:T(8,128)(2,1)S(1)} %get-tuple-element.24.refs_1_), channel_id=1, source_target_pairs={{0,1},{1,0},{2,3},{3,2},{4,5},{5,4},{6,7},{7,6},{8,9},{9,8},{10,11... | collective-permute-start | bytes 786440 | tf_op jit(solution)/shard_map/ppermute | solution.py:404
  34.1 1.1 %collective-permute-start.12 = (bf16[2,128,512]{2,1,0:T(8,128)(2,1)S(1)}, bf16[2,128,512]{2,1,0:T(8,128)(2,1)S(1)}, u32[]{:S(2)}, u32[]{:S(2)}) collective-permute-start(bf16[2,128,512]{2,1,0:T(8,128)(2,1)S(1)} %get-tuple-element.20.refs_1_), channel_id=1, source_target_pairs={{0,1},{1,0},{2,3},{3,2},{4,5},{5,4},{6,7},{7,6},{8,9},{9,8},{10,11... | collective-permute-start | bytes 786440 | tf_op jit(solution)/shard_map/ppermute | solution.py:404
  35.9 3.5 %stage0.1.refs_12_ = f32[2176,128]{1,0:T(8,128)S(1)} custom-call(s32[3]{0:T(128)S(1)} %pad_add_fusion.meta.refs_0_, bf16[2,128,512]{2,1,0:T(8,128)(2,1)S(1)} %copy-done.1, bf16[2,128,512]{2,1,0:T(8,128)(2,1)S(1)} %collective-permute-done.14.refs_2_, bf16[2,128,512]{2,1,0:T(8,128)(2,1)S(1)} %get-tuple-element.19.refs_3_, ...), custom_call_target="tpu_custom_call" | custom-call | flops 3000000000 | bytes 4194304 | tf_op jit(solution)/shard_map/stage0/pallas_call | solution.py:455
  39.5 3.5 %stage2.1.refs_12_ = f32[2176,128]{1,0:T(8,128)S(1)} custom-call(s32[3]{0:T(128)S(1)} %pad_add_fusion.meta.refs_0_, bf16[2,128,512]{2,1,0:T(8,128)(2,1)S(1)} %get-tuple-element.24.refs_1_, bf16[2,128,512]{2,1,0:T(8,128)(2,1)S(1)} %collective-permute-done.10.refs_2_, bf16[2,128,512]{2,1,0:T(8,128)(2,1)S(1)} %get-tuple-element.22.refs_3_, ...), custom_call_target="tpu_custom_call" | custom-call | flops 3000000000 | bytes 4194304 | tf_op jit(solution)/shard_map/stage2/pallas_call | solution.py:455
  43.0 5.5 %stage1.1.refs_13_ = f32[2048,128]{1,0:T(8,128)S(1)} custom-call(s32[3]{0:T(128)S(1)} %pad_add_fusion.meta.refs_0_, bf16[2,128,512]{2,1,0:T(8,128)(2,1)S(1)} %get-tuple-element.20.refs_1_, bf16[2,128,512]{2,1,0:T(8,128)(2,1)S(1)} %collective-permute-done.12.refs_2_, bf16[2,128,512]{2,1,0:T(8,128)(2,1)S(1)} %get-tuple-element.23.refs_3_, ...), custom_call_target="tpu_custom_call" | custom-call | flops 3000000000 | bytes 4194304 | tf_op jit(solution)/shard_map/stage1/pallas_call | solution.py:455
  48.5 7.1 %stage3.1 = f32[1,2,256,512]{3,2,1,0:T(8,128)} custom-call(s32[3]{0:T(128)S(1)} %pad_add_fusion.meta.refs_0_, bf16[2,128,512]{2,1,0:T(8,128)(2,1)S(1)} %get-tuple-element.21.refs_1_, bf16[2,128,512]{2,1,0:T(8,128)(2,1)S(1)} %collective-permute-done.6.refs_2_, bf16[2,128,512]{2,1,0:T(8,128)(2,1)S(1)} %constant_dynamic-update-slice_fusion.refs_3_, ...), custom_call_target="tpu_custom_call" | custom-call | flops 3000000000 | bytes 4194304 | tf_op jit(solution)/shard_map/stage3/pallas_call | solution.py:455
  (35 shorter events, 3.0 us)
Async XLA Ops:
  0.0 8.4 %collective-permute-start.1 = (bf16[2,128,512]{2,1,0:T(8,128)(2,1)}, bf16[2,128,512]{2,1,0:T(8,128)(2,1)S(1)}, u32[]{:S(2)}, u32[]{:S(2)}) collective-permute-start(bf16[2,128,512]{2,1,0:T(8,128)(2,1)} %refs_1_.1), channel_id=1, source_target_pairs={{4,0},{8,4},{12,8},{14,12},{10,14},{6,10},{2,6},{0,2},{5,1},{9,5},... | collective-permute-start | bytes 786440 | tf_op jit(solution)/shard_map/ppermute | solution.py:468
  2.0 7.4 %collective-permute-start = (bf16[2,128,512]{2,1,0:T(8,128)(2,1)}, bf16[2,128,512]{2,1,0:T(8,128)(2,1)S(1)}, u32[]{:S(2)}, u32[]{:S(2)}) collective-permute-start(bf16[2,128,512]{2,1,0:T(8,128)(2,1)} %refs_1_.1), channel_id=1, source_target_pairs={{0,4},{4,8},{8,12},{12,14},{14,10},{10,6},{6,2},{2,0},{1,5},{5,9},... | collective-permute-start | bytes 786440 | tf_op jit(solution)/shard_map/ppermute | solution.py:468
  8.4 6.6 %collective-permute-start.2 = (bf16[2,128,512]{2,1,0:T(8,128)(2,1)S(1)}, bf16[2,128,512]{2,1,0:T(8,128)(2,1)S(1)}, u32[]{:S(2)}, u32[]{:S(2)}) collective-permute-start(bf16[2,128,512]{2,1,0:T(8,128)(2,1)S(1)} %collective-permute-done.1), channel_id=1, source_target_pairs={{4,0},{8,4},{12,8},{14,12},{10,14},{6,10},{2,6},{0,2},{5,1},{9,5},... | collective-permute-start | bytes 786440 | tf_op jit(solution)/shard_map/ppermute | solution.py:470
  9.4 6.3 %collective-permute-start.4 = (bf16[2,128,512]{2,1,0:T(8,128)(2,1)S(1)}, bf16[2,128,512]{2,1,0:T(8,128)(2,1)S(1)}, u32[]{:S(2)}, u32[]{:S(2)}) collective-permute-start(bf16[2,128,512]{2,1,0:T(8,128)(2,1)S(1)} %collective-permute-done), channel_id=1, source_target_pairs={{0,4},{4,8},{8,12},{12,14},{14,10},{10,6},{6,2},{2,0},{1,5},{5,9},... | collective-permute-start | bytes 786440 | tf_op jit(solution)/shard_map/ppermute | solution.py:470
  9.8 15.3 %collective-permute-start.15 = (bf16[2,128,512]{2,1,0:T(8,128)(2,1)}, bf16[2,128,512]{2,1,0:T(8,128)(2,1)S(1)}, u32[]{:S(2)}, u32[]{:S(2)}) collective-permute-start(bf16[2,128,512]{2,1,0:T(8,128)(2,1)} %refs_1_.1), channel_id=1, source_target_pairs={{4,6},{6,4},{8,10},{10,8},{5,7},{7,5},{9,11},{11,9},{20,22},{22,20... | collective-permute-start | bytes 786440 | tf_op jit(solution)/shard_map/ppermute | solution.py:469
  10.5 24.8 %collective-permute-start.14 = (bf16[2,128,512]{2,1,0:T(8,128)(2,1)}, bf16[2,128,512]{2,1,0:T(8,128)(2,1)S(1)}, u32[]{:S(2)}, u32[]{:S(2)}) collective-permute-start(bf16[2,128,512]{2,1,0:T(8,128)(2,1)} %refs_1_.1), channel_id=1, source_target_pairs={{0,1},{1,0},{2,3},{3,2},{4,5},{5,4},{6,7},{7,6},{8,9},{9,8},{10,11... | collective-permute-start | bytes 786440 | tf_op jit(solution)/shard_map/ppermute | solution.py:404
  14.9 10.2 %collective-permute-start.3 = (bf16[2,128,512]{2,1,0:T(8,128)(2,1)S(1)}, bf16[2,128,512]{2,1,0:T(8,128)(2,1)S(1)}, u32[]{:S(2)}, u32[]{:S(2)}) collective-permute-start(bf16[2,128,512]{2,1,0:T(8,128)(2,1)S(1)} %collective-permute-done.2), channel_id=1, source_target_pairs={{4,0},{8,4},{12,8},{14,12},{10,14},{6,10},{2,6},{0,2},{5,1},{9,5},... | collective-permute-start | bytes 786440 | tf_op jit(solution)/shard_map/ppermute | solution.py:471
  15.7 9.5 %collective-permute-start.5 = (bf16[2,128,512]{2,1,0:T(8,128)(2,1)S(1)}, bf16[2,128,512]{2,1,0:T(8,128)(2,1)S(1)}, u32[]{:S(2)}, u32[]{:S(2)}) collective-permute-start(bf16[2,128,512]{2,1,0:T(8,128)(2,1)S(1)} %collective-permute-done.4), channel_id=1, source_target_pairs={{0,4},{4,8},{8,12},{12,14},{14,10},{10,6},{6,2},{2,0},{1,5},{5,9},... | collective-permute-start | bytes 786440 | tf_op jit(solution)/shard_map/ppermute | solution.py:471
  17.4 0.9 %copy-start = (f32[256,256]{1,0:T(8,128)S(1)}, f32[256,256]{1,0:T(8,128)}, u32[]{:S(2)}) copy-start(f32[256,256]{1,0:T(8,128)} %phase.1) | copy-start | bytes 786436
  18.3 0.9 %copy-start.2 = (f32[2,2,2,2,8,256]{5,4,3,2,1,0:T(8,128)S(1)}, f32[2,2,2,2,8,256]{5,4,3,2,1,0:T(8,128)}, u32[]{:S(2)}) copy-start(f32[2,2,2,2,8,256]{5,4,3,2,1,0:T(8,128)} %taps.1) | copy-start | bytes 393220
  19.2 0.7 %copy-start.3 = (s32[2,2,2,256]{3,2,1,0:T(2,128)S(1)}, s32[2,2,2,256]{3,2,1,0:T(2,128)}, u32[]{:S(2)}) copy-start(s32[2,2,2,256]{3,2,1,0:T(2,128)} %ang.1) | copy-start | bytes 24580
  19.9 0.7 %copy-start.4 = (s32[2,2,2,256]{3,2,1,0:T(2,128)S(1)}, s32[2,2,2,256]{3,2,1,0:T(2,128)}, u32[]{:S(2)}) copy-start(s32[2,2,2,256]{3,2,1,0:T(2,128)} %offset.1) | copy-start | bytes 24580
  20.6 0.7 %copy-start.5 = (f32[2,2,2,256]{3,2,1,0:T(2,128)S(1)}, f32[2,2,2,256]{3,2,1,0:T(2,128)}, u32[]{:S(2)}) copy-start(f32[2,2,2,256]{3,2,1,0:T(2,128)} %twist.1) | copy-start | bytes 24580
  25.3 10.6 %copy-start.1 = (bf16[2,128,512]{2,1,0:T(8,128)(2,1)S(1)}, bf16[2,128,512]{2,1,0:T(8,128)(2,1)}, u32[]{:S(2)}) copy-start(bf16[2,128,512]{2,1,0:T(8,128)(2,1)} %refs_1_.1) | copy-start | bytes 786436
  25.3 10.0 %collective-permute-start.16 = (bf16[2,128,512]{2,1,0:T(8,128)(2,1)S(1)}, bf16[2,128,512]{2,1,0:T(8,128)(2,1)S(1)}, u32[]{:S(2)}, u32[]{:S(2)}) collective-permute-start(bf16[2,128,512]{2,1,0:T(8,128)(2,1)S(1)} %get-tuple-element.19.refs_3_), channel_id=1, source_target_pairs={{0,1},{1,0},{2,3},{3,2},{4,5},{5,4},{6,7},{7,6},{8,9},{9,8},{10,11... | collective-permute-start | bytes 786440 | tf_op jit(solution)/shard_map/ppermute | solution.py:404
  27.9 5.2 %collective-permute-start.7 = (bf16[1,128,512]{2,1,0:T(8,128)(2,1)S(1)}, bf16[1,128,512]{2,1,0:T(8,128)(2,1)S(1)}, u32[]{:S(2)}, u32[]{:S(2)}) collective-permute-start(bf16[1,128,512]{2,1,0:T(8,128)(2,1)S(1)} %slice.8), channel_id=1, source_target_pairs={{0,4},{4,8},{8,12},{12,14},{14,10},{10,6},{6,2},{2,0},{1,5},{5,9},... | collective-permute-start | bytes 393224 | tf_op jit(solution)/shard_map/ppermute | solution.py:473
  29.1 5.0 %collective-permute-start.8 = (bf16[1,128,512]{2,1,0:T(8,128)(2,1)S(1)}, bf16[1,128,512]{2,1,0:T(8,128)(2,1)S(1)}, u32[]{:S(2)}, u32[]{:S(2)}) collective-permute-start(bf16[1,128,512]{2,1,0:T(8,128)(2,1)S(1)} %slice.9), channel_id=1, source_target_pairs={{4,0},{8,4},{12,8},{14,12},{10,14},{6,10},{2,6},{0,2},{5,1},{9,5},... | collective-permute-start | bytes 393224 | tf_op jit(solution)/shard_map/ppermute | solution.py:473
  29.7 13.3 %collective-permute-start.13 = (bf16[2,128,512]{2,1,0:T(8,128)(2,1)S(1)}, bf16[2,128,512]{2,1,0:T(8,128)(2,1)S(1)}, u32[]{:S(2)}, u32[]{:S(2)}) collective-permute-start(bf16[2,128,512]{2,1,0:T(8,128)(2,1)S(1)} %get-tuple-element.23.refs_3_), channel_id=1, source_target_pairs={{0,1},{1,0},{2,3},{3,2},{4,5},{5,4},{6,7},{7,6},{8,9},{9,8},{10,11... | collective-permute-start | bytes 786440 | tf_op jit(solution)/shard_map/ppermute | solution.py:404
  33.1 6.3 %collective-permute-start.10 = (bf16[2,128,512]{2,1,0:T(8,128)(2,1)S(1)}, bf16[2,128,512]{2,1,0:T(8,128)(2,1)S(1)}, u32[]{:S(2)}, u32[]{:S(2)}) collective-permute-start(bf16[2,128,512]{2,1,0:T(8,128)(2,1)S(1)} %get-tuple-element.24.refs_1_), channel_id=1, source_target_pairs={{0,1},{1,0},{2,3},{3,2},{4,5},{5,4},{6,7},{7,6},{8,9},{9,8},{10,11... | collective-permute-start | bytes 786440 | tf_op jit(solution)/shard_map/ppermute | solution.py:404
  34.1 8.9 %collective-permute-start.12 = (bf16[2,128,512]{2,1,0:T(8,128)(2,1)S(1)}, bf16[2,128,512]{2,1,0:T(8,128)(2,1)S(1)}, u32[]{:S(2)}, u32[]{:S(2)}) collective-permute-start(bf16[2,128,512]{2,1,0:T(8,128)(2,1)S(1)} %get-tuple-element.20.refs_1_), channel_id=1, source_target_pairs={{0,1},{1,0},{2,3},{3,2},{4,5},{5,4},{6,7},{7,6},{8,9},{9,8},{10,11... | collective-permute-start | bytes 786440 | tf_op jit(solution)/shard_map/ppermute | solution.py:404
  35.3 4.2 %collective-permute-start.11 = (bf16[2,128,512]{2,1,0:T(8,128)(2,1)S(1)}, bf16[2,128,512]{2,1,0:T(8,128)(2,1)S(1)}, u32[]{:S(2)}, u32[]{:S(2)}) collective-permute-start(bf16[2,128,512]{2,1,0:T(8,128)(2,1)S(1)} %get-tuple-element.22.refs_3_), channel_id=1, source_target_pairs={{0,1},{1,0},{2,3},{3,2},{4,5},{5,4},{6,7},{7,6},{8,9},{9,8},{10,11... | collective-permute-start | bytes 786440 | tf_op jit(solution)/shard_map/ppermute | solution.py:404
  35.4 13.2 %collective-permute-start.6 = (bf16[2,128,512]{2,1,0:T(8,128)(2,1)S(1)}, bf16[2,128,512]{2,1,0:T(8,128)(2,1)S(1)}, u32[]{:S(2)}, u32[]{:S(2)}) collective-permute-start(bf16[2,128,512]{2,1,0:T(8,128)(2,1)S(1)} %get-tuple-element.21.refs_1_), channel_id=1, source_target_pairs={{0,1},{1,0},{2,3},{3,2},{4,5},{5,4},{6,7},{7,6},{8,9},{9,8},{10,11... | collective-permute-start | bytes 786440 | tf_op jit(solution)/shard_map/ppermute | solution.py:404
  39.4 9.2 %collective-permute-start.9 = (bf16[2,128,512]{2,1,0:T(8,128)(2,1)S(1)}, bf16[2,128,512]{2,1,0:T(8,128)(2,1)S(1)}, u32[]{:S(2)}, u32[]{:S(2)}) collective-permute-start(bf16[2,128,512]{2,1,0:T(8,128)(2,1)S(1)} %constant_dynamic-update-slice_fusion.refs_3_), channel_id=1, source_target_pairs={{0,1},{1,0},{2,3},{3,2},{4,5},{5,4},{6,7},{7,6},{8,9},{9,8},{10,11... | collective-permute-start | bytes 786440 | tf_op jit(solution)/shard_map/ppermute | solution.py:404

commit v3 on v2

--- a/solution.py
+++ b/solution.py
@@ -157,14 +157,25 @@
 FAR = NEAR + 2 * STEP
 
 
-def table_kernel(meta, chirp, phase, ang, offset, taps, twist, near_mat, edge_mat, steer, *outs, total):
-    core, slot, column = meta[0], meta[1], meta[2]
+def table_kernel(*refs, total):
+    given, outs, local = refs[:6], refs[6:13], refs[13:19]
+    line, sems = refs[19:]
+    copies = [pltpu.make_async_copy(a, b, sems.at[i]) for i, (a, b) in enumerate(zip(given, local))]
+    for copy in copies:
+        copy.start()
+    core, slot, column = (lax.axis_index(a) for a in ("range", "aperture", "beam"))
+    for copy in copies:
+        copy.wait()
+    chirp, phase, ang, offset, taps, twist = local
+    (near_mat, edge_mat, steer), outs = outs[:3], outs[3:]
+    line[...] = jnp.zeros_like(line)
+    line[:2, : chirp.shape[1]] = chirp[...].astype(jnp.float32)
     bins = total // 2
     pulses = phase.shape[0] // 2
     beams = phase.shape[1]
     shape = (LANES, 2 * LANES)
     t_r, t_i = (
-        pltpu.roll(jnp.broadcast_to(chirp[i : i + 1, :], shape), 0, 1, stride=1, stride_axis=0)
+        pltpu.roll(jnp.broadcast_to(line[i : i + 1, :], shape), 0, 1, stride=1, stride_axis=0)
         for i in (0, 1)
     )
     for matrix, rows, cols in ((near_mat, LANES, 2 * LANES), (edge_mat, SPAN, LANES)):
@@ -210,25 +221,33 @@
             first = first - RIM_CELLS if level == 0 else first
             todo.append((table, order, rate, first, half_bins // STEP))
 
-    def turn(step, carry):
-        for table, order, rate, first, steps in todo:
-            near = rate * (step.astype(jnp.float32) / total)
-            table[order, NEAR + step] = jnp.cos(near)
-            table[order, NEAR + STEP + step] = jnp.sin(near)
-            far = rate * ((first + STEP * step).astype(jnp.float32) / total)
-            table[order, FAR + step] = jnp.cos(far)
-            table[order, FAR + steps + step] = jnp.sin(far)
-        return carry
-
-    lax.fori_loop(0, STEP, turn, 0)
     for table, order, rate, first, steps in todo:
-        for step in range(STEP, steps):
-            far = rate * ((first + STEP * step).astype(jnp.float32) / total)
-            table[order, FAR + step] = jnp.cos(far)
-            table[order, FAR + steps + step] = jnp.sin(far)
-
-
-def squeeze(piece, rim, core, near_mat, edge_mat, c_ref, index):
+        power = 1
+        near, far = {0: (jnp.ones_like(rate), jnp.zeros_like(rate))}, {0: phasor(rate, first, total)}
+        while power < STEP:
+            turn = phasor(rate, power, total)
+            near.update({n + power: product(near[n], turn) for n in list(near)})
+            power *= 2
+        count = 1
+        while count < steps:
+            turn = phasor(rate, count * STEP, total)
+            far.update({n + count: product(far[n], turn) for n in list(far) if n + count < steps})
+            count *= 2
+        for found, place, length in ((near, NEAR, STEP), (far, FAR, steps)):
+            for n in range(length):
+                table[order, place + n], table[order, place + length + n] = found[n]
+
+
+def phasor(rate, count, total):
+    angle = rate * (jnp.asarray(count, jnp.float32) / total)
+    return jnp.cos(angle), jnp.sin(angle)
+
+
+def product(x, y):
+    return x[0] * y[0] - x[1] * y[1], x[0] * y[1] + x[1] * y[0]
+
+
+def squeeze(piece, rim, core, near_mat, edge_mat, c_ref):
     bins = piece.shape[-1]
 
     def columns(low, high):
@@ -237,10 +256,10 @@
             tiles = []
             for tile in range(low, high):
                 if tile == 0:
-                    other = rim[ri, :, bins - LANES :]
+                    other = rim[ri]
                     tiles.append(jnp.where(core == 1, other, jnp.zeros_like(other)))
                 elif tile == bins // LANES + 1:
-                    other = rim[ri, :, :LANES]
+                    other = rim[ri]
                     tiles.append(jnp.where(core == 0, other, jnp.zeros_like(other)))
                 else:
                     tiles.append(piece[ri, :, (tile - 1) * LANES : tile * LANES])
@@ -264,12 +283,12 @@
         else:
             result = times(edge_mat[...], columns(block, block + 1)).astype(jnp.bfloat16)
             place, count = SPAN + bins, SPAN
-        c_ref[index, 0, place : place + count] = result[:count]
-        c_ref[index, 1, place : place + count] = result[count:]
-
-
-def form(c_ref, steer, x_ref):
-    pieces = [c_ref[i, ri] for ri in (0, 1) for i in (0, 1)]
+        c_ref[0, place : place + count] = result[:count]
+        c_ref[1, place : place + count] = result[count:]
+
+
+def form(halves, steer, x_ref):
+    pieces = [half[ri] for ri in (0, 1) for half in halves]
     image = jnp.dot(
         jnp.concatenate(pieces, axis=1), steer[...], preferred_element_type=jnp.float32
     ).astype(jnp.bfloat16)
@@ -351,37 +370,65 @@
                 ] = value.T
 
 
-def stage_kernel(stage, total, *refs):
-    (meta, first, first_rim, second, second_rim, near_mat, edge_mat, steer, ang, shift, table0) = refs[:11]
-    refs = refs[11:]
-    core = meta[0]
-    bins = total // 2
-    half0, half1 = (bins + SPAN) // 2, bins // 2
-    order = stage & 1
-    table1 = base0 = base1 = None
-    if order == 1:
-        table1, base0, refs = refs[0], refs[1], refs[2:]
-    if stage == 3:
-        base1, refs = refs[0], refs[1:]
-    out_ref, c_ref, x0_ref, s_ref, y_ref = refs[:5]
-    squeeze(first, first_rim, core, near_mat, edge_mat, c_ref, 0)
-    squeeze(second, second_rim, core, near_mat, edge_mat, c_ref, 1)
-    form(c_ref, steer, x0_ref)
-    o_ref = out_ref if order == 0 else refs[5]
+def merge_low(halves, order, shared, table0, x0_ref, s_ref, y_ref, base, out_ref, half_bins):
+    near_mat, edge_mat, steer, ang, shift = shared
+    form(halves, steer, x0_ref)
     merge_child(
-        x0_ref, ang.at[0, order], shift.at[0, order], table0.at[order], s_ref, y_ref, base0, o_ref, half0
-    )
-    if order == 0:
-        return
-    x1_ref = refs[6]
-    merged_image(o_ref, x1_ref, half0, core * bins - RIM_CELLS, total)
-    which = stage >> 1
-    final = out_ref if stage == 1 else refs[7]
+        x0_ref, ang.at[0, order], shift.at[0, order], table0.at[order], s_ref, y_ref, base, out_ref, half_bins
+    )
+
+
+def merge_top(o_ref, order, shared, table1, x1_ref, s_ref, y_ref, base, out_ref, half_bins, total):
+    near_mat, edge_mat, steer, ang, shift = shared
+    first = lax.axis_index("range") * (total // 2) - RIM_CELLS
+    merged_image(o_ref, x1_ref, x1_ref.shape[1] // 2, first, total)
     merge_child(
-        x1_ref, ang.at[1, which], shift.at[1, which], table1.at[which], s_ref, y_ref, base1, final, half1
-    )
-    if stage == 3:
-        finished(final, out_ref, half1)
+        x1_ref, ang.at[1, order], shift.at[1, order], table1.at[order], s_ref, y_ref, base, out_ref, half_bins
+    )
+
+
+def first_stage(total, *refs):
+    pieces, shared, table0, refs = refs[:8], refs[8:13], refs[13], refs[14:]
+    part, c_own, c_next, c_a, c_b, x0_ref, s_ref, y_ref = refs
+    core = lax.axis_index("range")
+    for i, c_ref in enumerate((c_a, c_b, c_own, c_next)):
+        squeeze(pieces[2 * i], pieces[2 * i + 1], core, shared[0], shared[1], c_ref)
+    half0 = part.shape[0] // (SUBS)
+    merge_low((c_a, c_b), 1, shared, table0, x0_ref, s_ref, y_ref, None, part, half0)
+
+
+def second_stage(total, *refs):
+    pieces, shared, table0, refs = refs[:4], refs[4:9], refs[9], refs[10:]
+    table1, part, c_own = refs[:3]
+    near, c_b, c_a, x0_ref, s_ref, y_ref, o_ref, x1_ref = refs[3:]
+    core = lax.axis_index("range")
+    for i, c_ref in enumerate((c_a, c_b)):
+        squeeze(pieces[2 * i], pieces[2 * i + 1], core, shared[0], shared[1], c_ref)
+    half0, half1 = o_ref.shape[0] // SUBS, near.shape[0] // SUBS
+    merge_low((c_own, c_a), 0, shared, table0, x0_ref, s_ref, y_ref, part, o_ref, half0)
+    merge_top(o_ref, 0, shared, table1, x1_ref, s_ref, y_ref, None, near, half1, total)
+
+
+def third_stage(total, *refs):
+    pieces, shared, table0, refs = refs[:2], refs[2:7], refs[7], refs[8:]
+    c_next, c_b = refs[:2]
+    other, c_last, x0_ref, s_ref, y_ref = refs[2:]
+    core = lax.axis_index("range")
+    squeeze(pieces[0], pieces[1], core, shared[0], shared[1], c_last)
+    half0 = other.shape[0] // SUBS
+    merge_low((c_next, c_b), 0, shared, table0, x0_ref, s_ref, y_ref, None, other, half0)
+
+
+def last_stage(total, *refs):
+    pieces, shared, table0, refs = refs[:2], refs[2:7], refs[7], refs[8:]
+    table1, near, other, c_last = refs[:4]
+    out_ref, c_a, x0_ref, s_ref, y_ref, o_ref, x1_ref, final = refs[4:]
+    core = lax.axis_index("range")
+    squeeze(pieces[0], pieces[1], core, shared[0], shared[1], c_a)
+    half0, half1 = o_ref.shape[0] // SUBS, final.shape[0] // SUBS
+    merge_low((c_last, c_a), 1, shared, table0, x0_ref, s_ref, y_ref, other, o_ref, half0)
+    merge_top(o_ref, 1, shared, table1, x1_ref, s_ref, y_ref, near, final, half1, total)
+    finished(final, out_ref, half1)
 
 
 def ring_of_chips(echoes, chirp_taps, steer_phase, ang_table, range_table, interp_taps, phase_twist):
@@ -389,19 +436,20 @@
     beams = steer_phase.shape[1]
     total = bins * lax.axis_size("range")
     slots = lax.axis_size("aperture")
-    slot, column, core = (lax.axis_index(a) for a in ("aperture", "beam", "range"))
+    slot, column = lax.axis_index("aperture"), lax.axis_index("beam")
     axes = ("aperture", "beam")
     order = [z * 2 for z in range(slots)] + [z * 2 + 1 for z in reversed(range(slots))]
     ahead = [(order[i], order[(i + 1) % len(order)]) for i in range(len(order))]
     behind = [(b, a) for a, b in ahead]
-    across = [(2 * z + x, 2 * z + 1 - x) for z in range(1, slots - 1) for x in (0, 1)]
     kind = jnp.where(column == 0, slot, slots - 1 - slot)
     half0, half1 = (bins + SPAN) // 2, bins // 2
     window = bins + 2 * SPAN
-    meta = jnp.stack([core, slot, column]).astype(jnp.int32)
+
+    core = lax.axis_index("range")
 
     def other_core(x):
-        return lax.ppermute(x, "range", [(0, 1), (1, 0)])
+        rim = jnp.where(core == 0, x[:, :, bins - LANES :], x[:, :, :LANES])
+        return lax.ppermute(rim, "range", [(0, 1), (1, 0)])
 
     def choose(*options):
         picked = options[-1]
@@ -410,11 +458,11 @@
                 picked = jnp.where(kind == value, option, picked)
         return picked
 
-    smem, vmem = pl.BlockSpec(memory_space=pltpu.SMEM), pl.BlockSpec(memory_space=pltpu.VMEM)
+    vmem = pl.BlockSpec(memory_space=pltpu.VMEM)
     f32, bf16, i32 = jnp.float32, jnp.bfloat16, jnp.int32
     rows0 = NEAR + 2 * STEP + 2 * (half0 // STEP)
     rows1 = NEAR + 2 * STEP + 2 * (half1 // STEP)
-    chirp = jnp.pad(chirp_taps.astype(f32), ((0, 0), (0, 2 * LANES - chirp_taps.shape[1])))
+    arguments = (chirp_taps, steer_phase, ang_table, range_table, interp_taps, phase_twist)
     tables = pl.pallas_call(
         functools.partial(table_kernel, total=total),
         out_shape=[
@@ -426,59 +474,85 @@
             jax.ShapeDtypeStruct((2, rows0, SUBS, LANES), f32),
             jax.ShapeDtypeStruct((2, rows1, SUBS, LANES), f32),
         ],
-        in_specs=[smem] + [vmem] * 6,
+        in_specs=[pl.BlockSpec(memory_space=pltpu.HBM)] * 6,
         out_specs=[vmem] * 7,
-        compiler_params=pltpu.CompilerParams(vmem_limit_bytes=16 * 1024 * 1024),
+        scratch_shapes=[
+            *(pltpu.VMEM(x.shape, x.dtype) for x in arguments),
+            pltpu.VMEM((SUBS, 2 * LANES), f32),
+            pltpu.SemaphoreType.DMA((len(arguments),)),
+        ],
+        compiler_params=pltpu.CompilerParams(vmem_limit_bytes=60 * 2**20),
         cost_estimate=pl.CostEstimate(flops=10**9, bytes_accessed=4 * 2**20, transcendentals=0),
         name="tables",
-    )(meta, chirp, steer_phase, ang_table, range_table, interp_taps, phase_twist)
+    )(*arguments)
     shared, table0, table1 = tables[:5], tables[5], tables[6]
 
-    def run(stage, first, second, *carried):
-        rows = (half0 + SPAN + 32) * SUBS
-        if stage == 3:
-            out = jax.ShapeDtypeStruct((1, 2, beams, bins), f32)
-        else:
-            out = jax.ShapeDtypeStruct(((half1 if stage == 1 else half0) * SUBS, LANES), f32)
-        scratch = [
-            pltpu.VMEM((2, 2, window, pulses), bf16),
-            pltpu.VMEM((2, window, beams), bf16),
-            pltpu.VMEM((rows, LANES), f32),
-            pltpu.VMEM((rows, LANES), f32),
-        ]
-        if stage & 1:
-            scratch.append(pltpu.VMEM((half0 * SUBS, LANES), f32))
-            scratch.append(pltpu.VMEM((2, window - SPAN, beams), bf16))
-        if stage == 3:
-            scratch.append(pltpu.VMEM((half1 * SUBS, LANES), f32))
-        given = [meta, first[0], first[1], second[0], second[1], *shared, table0, *carried]
+    rows = (half0 + SPAN + 32) * SUBS
+    squeezed = ((2, window, pulses), bf16)
+    sums0, sums1 = ((half0 * SUBS, LANES), f32), ((half1 * SUBS, LANES), f32)
+    image0, image1 = ((2, window, beams), bf16), ((2, window - SPAN, beams), bf16)
+    room = ((rows, LANES), f32)
+
+    def run(kernel, pieces, carried, out, scratch):
+        given = [x for piece in pieces for x in piece] + [*shared, table0, *carried]
         return pl.pallas_call(
-            functools.partial(stage_kernel, stage, total),
-            out_shape=out,
-            in_specs=[smem] + [vmem] * (len(given) - 1),
-            out_specs=vmem,
-            scratch_shapes=scratch,
+            functools.partial(kernel, total),
+            out_shape=[jax.ShapeDtypeStruct(*x) for x in out],
+            in_specs=[vmem] * len(given),
+            out_specs=[vmem] * len(out),
+            scratch_shapes=[pltpu.VMEM(*x) for x in scratch],
             compiler_params=pltpu.CompilerParams(vmem_limit_bytes=24 * 1024 * 1024),
             cost_estimate=pl.CostEstimate(
                 flops=3 * 10**9, bytes_accessed=4 * 2**20, transcendentals=0
             ),
-            name=f"stage{stage}",
+            name=kernel.__name__,
         )(*given)
 
+    def after(value, result):
+        return lax.optimization_barrier((value, result))[0]
+
+    def pair(x):
+        return (x, other_core(x))
+
     up1, down1 = lax.ppermute(echoes, axes, ahead), lax.ppermute(echoes, axes, behind)
-    side = lax.ppermute(echoes, axes, across)
+    own = pair(echoes)
+    up1, down1 = after(up1, shared[0]), after(down1, shared[0])
     up2, down2 = lax.ppermute(up1, axes, ahead), lax.ppermute(down1, axes, behind)
+    beside = pair(choose(down1, up1, down1, up1))
     up3, down3 = lax.ppermute(up2, axes, ahead), lax.ppermute(down2, axes, behind)
-    far = jnp.concatenate(
-        [lax.ppermute(up3[:1], axes, ahead), lax.ppermute(down3[1:], axes, behind)], axis=0
-    )
-    pair = lambda x: (x, other_core(x))
-    part = run(0, pair(echoes), pair(choose(up1, side, side, down1)))
-    near = run(
-        1, pair(choose(down1, up1, down1, up1)), pair(choose(up2, up2, down2, down2)), table1, part
-    )
-    part = run(2, pair(choose(down2, down2, up2, up2)), pair(choose(up3, down3, up3, down3)))
-    return run(3, pair(choose(down3, down1, up1, up3)), pair(far), table1, part, near)
+    part, c_own, c_next = run(
+        first_stage,
+        [
+            beside,
+            pair(choose(up2, up2, down2, down2)),
+            own,
+            pair(choose(down2, down2, up2, up2)),
+        ],
+        [],
+        [sums0, squeezed, squeezed],
+        [squeezed, squeezed, image0, room, room],
+    )
+    up3, down3 = after(up3, part), after(down3, part)
+    far_up, far_down = lax.ppermute(up3[:1], axes, ahead), lax.ppermute(down3[1:], axes, behind)
+    last = pair(choose(down3, down1, up1, up3))
+    near, c_b = run(
+        second_stage,
+        [pair(choose(up1, up3, down3, down1)), pair(choose(up3, down3, up3, down3))],
+        [table1, part, c_own],
+        [sums1, squeezed],
+        [squeezed, image0, room, room, sums0, image1],
+    )
+    far = pair(jnp.concatenate([after(far_up, near), after(far_down, near)], axis=0))
+    other, c_last = run(
+        third_stage, [last], [c_next, c_b], [sums0, squeezed], [image0, room, room]
+    )
+    return run(
+        last_stage,
+        [(far[0], after(far[1], other))],
+        [table1, near, other, c_last],
+        [((1, 2, beams, bins), f32)],
+        [squeezed, image0, room, room, sums0, image1, sums1],
+    )[0]
 
 
 def solution(mesh):

time: 56.4 us -> 45.5 us (0.81); the launches traced: 55.7 us -> 45.4 us
  waiting for transfers between devices: 11.8 us -> 7.09 us
  local copies, waits for them, and re-layouts: 3.99 us -> 0.07 us
  Pallas kernels: 23.4 us -> 21 us
    ppermute x1, waiting for transfers between devices: 6.24 us -> 0.59 us  [ring_of_chips(): lax.ppermute(echoes, axes, behind)]
    unnamed x13 -> x17, local copies, waits for them, and re-layouts: 3.96 us -> 0.04 us
    ppermute x1, waiting for transfers between devices: 0.01 us -> 3.21 us  [ring_of_chips(): lax.ppermute(down2, axes, behind)]
    ppermute x1, waiting for transfers between devices: 2.69 us -> 0.01 us  [ring_of_chips(): lax.ppermute(up3[:1], axes, ahead)]
    pallas_call x4, Pallas kernels: 19.6 us -> 17.2 us  [run(): pl.pallas_call(functools.partial(kernel, total), out_shape=[jax.ShapeDtyp...]
    ppermute x1, waiting for transfers between devices: 2.57 us -> 0.65 us  [ring_of_chips(): lax.ppermute(down1, axes, behind)]
    ppermute x1, waiting for transfers between devices: 0.01 us -> 1.92 us  [ring_of_chips(): lax.ppermute(up1, axes, ahead)]
    select_n x0 -> x8, other arithmetic: none -> 0.96 us  [other_core(): rim = jnp.where(core == 0, x[:, :, bins - LANES:], x[:, :, :LANES])]
  transfers between devices with their start and end apart: 17 -> 16, of which waited for: 4 -> 5; matrix products, arithmetic and copies ran while one was open for 2% -> 2% of each run, Pallas kernels for 29% -> 33%
where the time goes in v3:
time: 45.5 us; the launch traced here: 45.4 us
  Pallas kernels  21 us (46%)
  starting transfers between devices  15.8 us (35%)
  waiting for transfers between devices  7.09 us (16%)
  other arithmetic  1.15 us (3%)
    pallas_call x4, Pallas kernels, run(): pl.pallas_call(functools.partial(kernel, total), out_shape=[jax.ShapeDtyp...  17.2 us
    ppermute x8, starting transfers between devices, other_core(): return lax.ppermute(rim, 'range', [(0, 1), (1, 0)])  9.27 us
    pallas_call x1, Pallas kernels, ring_of_chips(): pl.pallas_call(functools.partial(table_kernel, total=total), out_shape=[j...  3.73 us
    ppermute x1, waiting for transfers between devices, ring_of_chips(): lax.ppermute(down2, axes, behind)  3.21 us
    ppermute x1, starting transfers between devices, ring_of_chips(): lax.ppermute(echoes, axes, behind)  2.04 us
    ppermute x1, waiting for transfers between devices, ring_of_chips(): lax.ppermute(up1, axes, ahead)  1.92 us
    ppermute x1, starting transfers between devices, ring_of_chips(): lax.ppermute(up3[:1], axes, ahead)  1.3 us
    ppermute x1, starting transfers between devices, ring_of_chips(): lax.ppermute(up2, axes, ahead)  1.3 us
  transfers between devices with their start and end apart: 16, of which 5 were waited for; matrix products, arithmetic and copies ran while one was open for 2% of the time, Pallas kernels for 33%

profile of v3, /device:TPU:1, one launch (start us, length us, event | category | flops | bytes accessed | tf_op | source)
XLA Modules:
  0.0 45.4 jit_solution(16632240979864755753)
XLA Ops:
  0.0 2.0 %collective-permute-start.3 = (bf16[2,128,512]{2,1,0:T(8,128)(2,1)}, bf16[2,128,512]{2,1,0:T(8,128)(2,1)S(1)}, u32[]{:S(2)}, u32[]{:S(2)}) collective-permute-start(bf16[2,128,512]{2,1,0:T(8,128)(2,1)} %refs_4_.3), channel_id=1, source_target_pairs={{4,0},{8,4},{12,8},{14,12},{10,14},{6,10},{2,6},{0,2},{5,1},{9,5},... | collective-permute-start | bytes 786440 | tf_op jit(solution)/shard_map/ppermute | solution.py:517
  2.1 0.9 %slice_select_fusion.7 = bf16[2,128,128]{2,1,0:T(8,128)(2,1)S(1)} fusion(bf16[2,128,512]{2,1,0:T(8,128)(2,1)} %refs_4_.3, pred[]{:T(512)S(6)} %eq.14), kind=kLoop, calls=%fused_computation.17 | loop fusion | flops 32768 | bytes 196609 | tf_op jit(solution)/shard_map/jit(_where)/select_n | solution.py:451
  3.0 1.0 %collective-permute-start.7 = (bf16[2,128,128]{2,1,0:T(8,128)(2,1)S(1)}, bf16[2,128,128]{2,1,0:T(8,128)(2,1)S(1)}, u32[]{:S(2)}, u32[]{:S(2)}) collective-permute-start(bf16[2,128,128]{2,1,0:T(8,128)(2,1)S(1)} %slice_select_fusion.7), channel_id=1, source_target_pairs={{0,1},{1,0},{2,3},{3,2},{4,5},{5,4},{6,7},{7,6},{8,9},{9,8},{10,11... | collective-permute-start | bytes 196616 | tf_op jit(solution)/shard_map/ppermute | solution.py:452
  4.0 3.7 %tables.1 = (bf16[256,512]{1,0:T(8,128)(2,1)}, bf16[64,256]{1,0:T(8,128)(2,1)}, bf16[512,512]{1,0:T(8,128)(2,1)}, s32[2,2,1,256]{3,2,1,0:T(1,128)}, s32[2,2,8,12...) custom-call(bf16[2,64]{1,0:T(2,128)(2,1)} %refs_0_.1, f32[256,256]{1,0:T(8,128)} %refs_1_.1, ...), custom_call_target="tpu_custom_call" | custom-call | flops 1000000000 | bytes 4194304 | tf_op jit(solution)/shard_map/tables/pallas_call | solution.py:466
  7.8 0.6 %collective-permute-done.3 = bf16[2,128,512]{2,1,0:T(8,128)(2,1)S(1)} collective-permute-done((bf16[2,128,512]{2,1,0:T(8,128)(2,1)}, bf16[2,128,512]{2,1,0:T(8,128)(2,1)S(1)}, u32[]{:S(2)}, u32[]{:S(2)}) %collective-permute-start.3) | collective-permute-done | bytes 262176 | tf_op jit(solution)/shard_map/ppermute | solution.py:517
  8.4 0.7 %collective-permute-done = bf16[2,128,512]{2,1,0:T(8,128)(2,1)S(1)} collective-permute-done((bf16[2,128,512]{2,1,0:T(8,128)(2,1)}, bf16[2,128,512]{2,1,0:T(8,128)(2,1)S(1)}, u32[]{:S(2)}, u32[]{:S(2)}) %collective-permute-start) | collective-permute-done | bytes 262176 | tf_op jit(solution)/shard_map/ppermute | solution.py:517
  9.1 0.6 %collective-permute-start.1 = (bf16[2,128,512]{2,1,0:T(8,128)(2,1)S(1)}, bf16[2,128,512]{2,1,0:T(8,128)(2,1)S(1)}, u32[]{:S(2)}, u32[]{:S(2)}) collective-permute-start(bf16[2,128,512]{2,1,0:T(8,128)(2,1)S(1)} %collective-permute-done), channel_id=1, source_target_pairs={{0,4},{4,8},{8,12},{12,14},{14,10},{10,6},{6,2},{2,0},{1,5},{5,9},... | collective-permute-start | bytes 786440 | tf_op jit(solution)/shard_map/ppermute | solution.py:520
  9.7 0.9 %collective-permute-start.5 = (bf16[2,128,512]{2,1,0:T(8,128)(2,1)S(1)}, bf16[2,128,512]{2,1,0:T(8,128)(2,1)S(1)}, u32[]{:S(2)}, u32[]{:S(2)}) collective-permute-start(bf16[2,128,512]{2,1,0:T(8,128)(2,1)S(1)} %collective-permute-done.3), channel_id=1, source_target_pairs={{4,0},{8,4},{12,8},{14,12},{10,14},{6,10},{2,6},{0,2},{5,1},{9,5},... | collective-permute-start | bytes 786440 | tf_op jit(solution)/shard_map/ppermute | solution.py:520
  10.6 2.5 %collective-permute-start.4 = (bf16[2,128,128]{2,1,0:T(8,128)(2,1)S(1)}, bf16[2,128,128]{2,1,0:T(8,128)(2,1)S(1)}, u32[]{:S(2)}, u32[]{:S(2)}) collective-permute-start(bf16[2,128,128]{2,1,0:T(8,128)(2,1)S(1)} %slice_select_fusion.6), channel_id=1, source_target_pairs={{0,1},{1,0},{2,3},{3,2},{4,5},{5,4},{6,7},{7,6},{8,9},{9,8},{10,11... | collective-permute-start | bytes 196616 | tf_op jit(solution)/shard_map/ppermute | solution.py:452
  13.1 1.9 %collective-permute-done.1 = bf16[2,128,512]{2,1,0:T(8,128)(2,1)S(1)} collective-permute-done((bf16[2,128,512]{2,1,0:T(8,128)(2,1)S(1)}, bf16[2,128,512]{2,1,0:T(8,128)(2,1)S(1)}, u32[]{:S(2)}, u32[]{:S(2)}) %collective-permute-start.1) | collective-permute-done | bytes 262176 | tf_op jit(solution)/shard_map/ppermute | solution.py:520
  15.0 0.6 %collective-permute-done.5 = bf16[2,128,512]{2,1,0:T(8,128)(2,1)S(1)} collective-permute-done((bf16[2,128,512]{2,1,0:T(8,128)(2,1)S(1)}, bf16[2,128,512]{2,1,0:T(8,128)(2,1)S(1)}, u32[]{:S(2)}, u32[]{:S(2)}) %collective-permute-start.5) | collective-permute-done | bytes 262176 | tf_op jit(solution)/shard_map/ppermute | solution.py:520
  15.8 2.8 %collective-permute-start.6 = (bf16[2,128,128]{2,1,0:T(8,128)(2,1)S(1)}, bf16[2,128,128]{2,1,0:T(8,128)(2,1)S(1)}, u32[]{:S(2)}, u32[]{:S(2)}) collective-permute-start(bf16[2,128,128]{2,1,0:T(8,128)(2,1)S(1)} %slice_select_fusion.5), channel_id=1, source_target_pairs={{0,1},{1,0},{2,3},{3,2},{4,5},{5,4},{6,7},{7,6},{8,9},{9,8},{10,11... | collective-permute-start | bytes 196616 | tf_op jit(solution)/shard_map/ppermute | solution.py:452
  18.6 1.3 %collective-permute-start.2 = (bf16[2,128,512]{2,1,0:T(8,128)(2,1)S(1)}, bf16[2,128,512]{2,1,0:T(8,128)(2,1)S(1)}, u32[]{:S(2)}, u32[]{:S(2)}) collective-permute-start(bf16[2,128,512]{2,1,0:T(8,128)(2,1)S(1)} %collective-permute-done.1), channel_id=1, source_target_pairs={{0,4},{4,8},{8,12},{12,14},{14,10},{10,6},{6,2},{2,0},{1,5},{5,9},... | collective-permute-start | bytes 786440 | tf_op jit(solution)/shard_map/ppermute | solution.py:522
  19.9 0.2 collective-permute-start.10
  20.2 3.7 %first_stage.1 = (f32[2176,128]{1,0:T(8,128)S(1)}, bf16[2,576,128]{2,1,0:T(8,128)(2,1)S(1)}, bf16[2,576,128]{2,1,0:T(8,128)(2,1)S(1)}) custom-call(bf16[2,128,512]{2,1,0:T(8,128)(2,1)S(1)} %fusion.3.refs_0_, bf16[2,128,128]{2,1,0:T(8,128)(2,1)S(1)} %collective-permute-done.4.refs_1_, bf16[2,128,512]{2,1,0:T(8,128)(2,1)S(1)} %get-tuple-element.51.refs_2_, ...), custom_call_target="tpu_custom_call" | custom-call | flops 3000000000 | bytes 4194304 | tf_op jit(solution)/shard_map/first_stage/pallas_call | solution.py:498
  23.9 3.2 %collective-permute-done.10 = bf16[2,128,512]{2,1,0:T(8,128)(2,1)S(1)} collective-permute-done((bf16[2,128,512]{2,1,0:T(8,128)(2,1)S(1)}, bf16[2,128,512]{2,1,0:T(8,128)(2,1)S(1)}, u32[]{:S(2)}, u32[]{:S(2)}) %collective-permute-start.10) | collective-permute-done | bytes 262176 | tf_op jit(solution)/shard_map/ppermute | solution.py:522
  27.2 1.7 %collective-permute-start.12 = (bf16[2,128,128]{2,1,0:T(8,128)(2,1)S(1)}, bf16[2,128,128]{2,1,0:T(8,128)(2,1)S(1)}, u32[]{:S(2)}, u32[]{:S(2)}) collective-permute-start(bf16[2,128,128]{2,1,0:T(8,128)(2,1)S(1)} %slice_select_fusion.2), channel_id=1, source_target_pairs={{0,1},{1,0},{2,3},{3,2},{4,5},{5,4},{6,7},{7,6},{8,9},{9,8},{10,11... | collective-permute-start | bytes 196616 | tf_op jit(solution)/shard_map/ppermute | solution.py:452
  29.0 0.5 %collective-permute-start.15 = (bf16[2,128,128]{2,1,0:T(8,128)(2,1)S(1)}, bf16[2,128,128]{2,1,0:T(8,128)(2,1)S(1)}, u32[]{:S(2)}, u32[]{:S(2)}) collective-permute-start(bf16[2,128,128]{2,1,0:T(8,128)(2,1)S(1)} %slice_select_fusion), channel_id=1, source_target_pairs={{0,1},{1,0},{2,3},{3,2},{4,5},{5,4},{6,7},{7,6},{8,9},{9,8},{10,11... | collective-permute-start | bytes 196616 | tf_op jit(solution)/shard_map/ppermute | solution.py:452
  29.5 0.2 collective-permute-start.13
  29.7 1.3 %collective-permute-start.9 = (bf16[1,128,512]{2,1,0:T(8,128)(2,1)S(1)}, bf16[1,128,512]{2,1,0:T(8,128)(2,1)S(1)}, u32[]{:S(2)}, u32[]{:S(2)}) collective-permute-start(bf16[1,128,512]{2,1,0:T(8,128)(2,1)S(1)} %slice.62), channel_id=1, source_target_pairs={{0,4},{4,8},{8,12},{12,14},{14,10},{10,6},{6,2},{2,0},{1,5},{5,9},... | collective-permute-start | bytes 393224 | tf_op jit(solution)/shard_map/ppermute | solution.py:536
  31.0 4.9 %second_stage.1 = (f32[2048,128]{1,0:T(8,128)S(1)}, bf16[2,576,128]{2,1,0:T(8,128)(2,1)S(1)}) custom-call(bf16[2,128,512]{2,1,0:T(8,128)(2,1)S(1)} %get-tuple-element.48.refs_0_, bf16[2,128,128]{2,1,0:T(8,128)(2,1)S(1)} %collective-permute-done.11.refs_1_, bf16[2,128,512]{2,1,0:T(8,128)(2,1)S(1)} %get-tuple-element.49.refs_2_, ...), custom_call_target="tpu_custom_call" | custom-call | flops 3000000000 | bytes 4194304 | tf_op jit(solution)/shard_map/second_stage/pallas_call | solution.py:498
  36.0 0.7 %collective-permute-start.14 = (bf16[2,128,128]{2,1,0:T(8,128)(2,1)S(1)}, bf16[2,128,128]{2,1,0:T(8,128)(2,1)S(1)}, u32[]{:S(2)}, u32[]{:S(2)}) collective-permute-start(bf16[2,128,128]{2,1,0:T(8,128)(2,1)S(1)} %slice_select_fusion.1), channel_id=1, source_target_pairs={{0,1},{1,0},{2,3},{3,2},{4,5},{5,4},{6,7},{7,6},{8,9},{9,8},{10,11... | collective-permute-start | bytes 196616 | tf_op jit(solution)/shard_map/ppermute | solution.py:452
  36.7 2.6 %third_stage.1 = (f32[2176,128]{1,0:T(8,128)S(1)}, bf16[2,576,128]{2,1,0:T(8,128)(2,1)S(1)}) custom-call(bf16[2,128,512]{2,1,0:T(8,128)(2,1)S(1)} %get-tuple-element.47.refs_0_, bf16[2,128,128]{2,1,0:T(8,128)(2,1)S(1)} %collective-permute-done.15.refs_1_, bf16[256,512]{1,0:T(8,128)(2,1)S(1)} %copy-done.4, bf16[64,256]{1,0:T(8,128)(2,1)S(1)} %copy-done.5, ...), custom_call_target="tpu_custom_call" | custom-call | flops 3000000000 | bytes 4194304 | tf_op jit(solution)/shard_map/third_stage/pallas_call | solution.py:498
  39.3 6.0 %last_stage.1 = f32[1,2,256,512]{3,2,1,0:T(8,128)} custom-call(bf16[2,128,512]{2,1,0:T(8,128)(2,1)S(1)} %constant_dynamic-update-slice_fusion.refs_0_, bf16[2,128,128]{2,1,0:T(8,128)(2,1)S(1)} %collective-permute-done.14.refs_1_, bf16[256,512]{1,0:T(8,128)(2,1)S(1)} %copy-done.4, bf16[64,256]{1,0:T(8,128)(2,1)S(1)} %copy-done.5, ...), custom_call_target="tpu_custom_call" | custom-call | flops 3000000000 | bytes 4194304 | tf_op jit(solution)/shard_map/last_stage/pallas_call | solution.py:498
  (44 shorter events, 0.6 us)
Async XLA Ops:
  0.0 8.4 %collective-permute-start.3 = (bf16[2,128,512]{2,1,0:T(8,128)(2,1)}, bf16[2,128,512]{2,1,0:T(8,128)(2,1)S(1)}, u32[]{:S(2)}, u32[]{:S(2)}) collective-permute-start(bf16[2,128,512]{2,1,0:T(8,128)(2,1)} %refs_4_.3), channel_id=1, source_target_pairs={{4,0},{8,4},{12,8},{14,12},{10,14},{6,10},{2,6},{0,2},{5,1},{9,5},... | collective-permute-start | bytes 786440 | tf_op jit(solution)/shard_map/ppermute | solution.py:517
  2.0 7.1 %collective-permute-start = (bf16[2,128,512]{2,1,0:T(8,128)(2,1)}, bf16[2,128,512]{2,1,0:T(8,128)(2,1)S(1)}, u32[]{:S(2)}, u32[]{:S(2)}) collective-permute-start(bf16[2,128,512]{2,1,0:T(8,128)(2,1)} %refs_4_.3), channel_id=1, source_target_pairs={{0,4},{4,8},{8,12},{12,14},{14,10},{10,6},{6,2},{2,0},{1,5},{5,9},... | collective-permute-start | bytes 786440 | tf_op jit(solution)/shard_map/ppermute | solution.py:517
  3.0 16.9 %collective-permute-start.7 = (bf16[2,128,128]{2,1,0:T(8,128)(2,1)S(1)}, bf16[2,128,128]{2,1,0:T(8,128)(2,1)S(1)}, u32[]{:S(2)}, u32[]{:S(2)}) collective-permute-start(bf16[2,128,128]{2,1,0:T(8,128)(2,1)S(1)} %slice_select_fusion.7), channel_id=1, source_target_pairs={{0,1},{1,0},{2,3},{3,2},{4,5},{5,4},{6,7},{7,6},{8,9},{9,8},{10,11... | collective-permute-start | bytes 196616 | tf_op jit(solution)/shard_map/ppermute | solution.py:452
  8.4 11.8 %copy-start = (bf16[2,128,512]{2,1,0:T(8,128)(2,1)S(1)}, bf16[2,128,512]{2,1,0:T(8,128)(2,1)}, u32[]{:S(2)}) copy-start(bf16[2,128,512]{2,1,0:T(8,128)(2,1)} %refs_4_.3) | copy-start | bytes 786436
  8.4 11.8 %copy-start.1 = (f32[2,82,8,128]{3,2,1,0:T(8,128)S(1)}, f32[2,82,8,128]{3,2,1,0:T(8,128)}, u32[]{:S(2)}) copy-start(f32[2,82,8,128]{3,2,1,0:T(8,128)} %get-tuple-element.33.refs_13_.refs_9_.refs_7_) | copy-start | bytes 2015236
  8.4 11.8 %copy-start.3 = (bf16[512,512]{1,0:T(8,128)(2,1)S(1)}, bf16[512,512]{1,0:T(8,128)(2,1)}, u32[]{:S(2)}) copy-start(bf16[512,512]{1,0:T(8,128)(2,1)} %get-tuple-element.30.refs_10_.refs_6_.refs_4_) | copy-start | bytes 1572868
  8.4 11.8 %copy-start.4 = (bf16[256,512]{1,0:T(8,128)(2,1)S(1)}, bf16[256,512]{1,0:T(8,128)(2,1)}, u32[]{:S(2)}) copy-start(bf16[256,512]{1,0:T(8,128)(2,1)} %get-tuple-element.26.refs_8_.refs_4_.refs_2_) | copy-start | bytes 786436
  8.4 11.8 %copy-start.5 = (bf16[64,256]{1,0:T(8,128)(2,1)S(1)}, bf16[64,256]{1,0:T(8,128)(2,1)}, u32[]{:S(2)}) copy-start(bf16[64,256]{1,0:T(8,128)(2,1)} %get-tuple-element.29.refs_9_.refs_5_.refs_3_) | copy-start | bytes 98308
  8.4 11.8 %copy-start.6 = (s32[2,2,8,128]{3,2,1,0:T(8,128)S(1)}, s32[2,2,8,128]{3,2,1,0:T(8,128)}, u32[]{:S(2)}) copy-start(s32[2,2,8,128]{3,2,1,0:T(8,128)} %get-tuple-element.32.refs_12_.refs_8_.refs_6_) | copy-start | bytes 49156
  8.4 11.8 %copy-start.7 = (s32[2,2,1,256]{3,2,1,0:T(1,128)S(1)}, s32[2,2,1,256]{3,2,1,0:T(1,128)}, u32[]{:S(2)}) copy-start(s32[2,2,1,256]{3,2,1,0:T(1,128)} %get-tuple-element.31.refs_11_.refs_7_.refs_5_) | copy-start | bytes 12292
  9.1 5.9 %collective-permute-start.1 = (bf16[2,128,512]{2,1,0:T(8,128)(2,1)S(1)}, bf16[2,128,512]{2,1,0:T(8,128)(2,1)S(1)}, u32[]{:S(2)}, u32[]{:S(2)}) collective-permute-start(bf16[2,128,512]{2,1,0:T(8,128)(2,1)S(1)} %collective-permute-done), channel_id=1, source_target_pairs={{0,4},{4,8},{8,12},{12,14},{14,10},{10,6},{6,2},{2,0},{1,5},{5,9},... | collective-permute-start | bytes 786440 | tf_op jit(solution)/shard_map/ppermute | solution.py:520
  9.7 6.0 %collective-permute-start.5 = (bf16[2,128,512]{2,1,0:T(8,128)(2,1)S(1)}, bf16[2,128,512]{2,1,0:T(8,128)(2,1)S(1)}, u32[]{:S(2)}, u32[]{:S(2)}) collective-permute-start(bf16[2,128,512]{2,1,0:T(8,128)(2,1)S(1)} %collective-permute-done.3), channel_id=1, source_target_pairs={{4,0},{8,4},{12,8},{14,12},{10,14},{6,10},{2,6},{0,2},{5,1},{9,5},... | collective-permute-start | bytes 786440 | tf_op jit(solution)/shard_map/ppermute | solution.py:520
  10.6 9.5 %collective-permute-start.4 = (bf16[2,128,128]{2,1,0:T(8,128)(2,1)S(1)}, bf16[2,128,128]{2,1,0:T(8,128)(2,1)S(1)}, u32[]{:S(2)}, u32[]{:S(2)}) collective-permute-start(bf16[2,128,128]{2,1,0:T(8,128)(2,1)S(1)} %slice_select_fusion.6), channel_id=1, source_target_pairs={{0,1},{1,0},{2,3},{3,2},{4,5},{5,4},{6,7},{7,6},{8,9},{9,8},{10,11... | collective-permute-start | bytes 196616 | tf_op jit(solution)/shard_map/ppermute | solution.py:452
  15.8 4.3 %collective-permute-start.6 = (bf16[2,128,128]{2,1,0:T(8,128)(2,1)S(1)}, bf16[2,128,128]{2,1,0:T(8,128)(2,1)S(1)}, u32[]{:S(2)}, u32[]{:S(2)}) collective-permute-start(bf16[2,128,128]{2,1,0:T(8,128)(2,1)S(1)} %slice_select_fusion.5), channel_id=1, source_target_pairs={{0,1},{1,0},{2,3},{3,2},{4,5},{5,4},{6,7},{7,6},{8,9},{9,8},{10,11... | collective-permute-start | bytes 196616 | tf_op jit(solution)/shard_map/ppermute | solution.py:452
  18.6 1.6 %collective-permute-start.8 = (bf16[2,128,128]{2,1,0:T(8,128)(2,1)S(1)}, bf16[2,128,128]{2,1,0:T(8,128)(2,1)S(1)}, u32[]{:S(2)}, u32[]{:S(2)}) collective-permute-start(bf16[2,128,128]{2,1,0:T(8,128)(2,1)S(1)} %slice_select_fusion.4), channel_id=1, source_target_pairs={{0,1},{1,0},{2,3},{3,2},{4,5},{5,4},{6,7},{7,6},{8,9},{9,8},{10,11... | collective-permute-start | bytes 196616 | tf_op jit(solution)/shard_map/ppermute | solution.py:452
  18.6 8.4 %collective-permute-start.2 = (bf16[2,128,512]{2,1,0:T(8,128)(2,1)S(1)}, bf16[2,128,512]{2,1,0:T(8,128)(2,1)S(1)}, u32[]{:S(2)}, u32[]{:S(2)}) collective-permute-start(bf16[2,128,512]{2,1,0:T(8,128)(2,1)S(1)} %collective-permute-done.1), channel_id=1, source_target_pairs={{0,4},{4,8},{8,12},{12,14},{14,10},{10,6},{6,2},{2,0},{1,5},{5,9},... | collective-permute-start | bytes 786440 | tf_op jit(solution)/shard_map/ppermute | solution.py:522
  19.9 7.1 %collective-permute-start.10 = (bf16[2,128,512]{2,1,0:T(8,128)(2,1)S(1)}, bf16[2,128,512]{2,1,0:T(8,128)(2,1)S(1)}, u32[]{:S(2)}, u32[]{:S(2)}) collective-permute-start(bf16[2,128,512]{2,1,0:T(8,128)(2,1)S(1)} %collective-permute-done.5), channel_id=1, source_target_pairs={{4,0},{8,4},{12,8},{14,12},{10,14},{6,10},{2,6},{0,2},{5,1},{9,5},... | collective-permute-start | bytes 786440 | tf_op jit(solution)/shard_map/ppermute | solution.py:522
  27.1 3.9 %copy-start.2 = (f32[2,80,8,128]{3,2,1,0:T(8,128)S(1)}, f32[2,80,8,128]{3,2,1,0:T(8,128)}, u32[]{:S(2)}) copy-start(f32[2,80,8,128]{3,2,1,0:T(8,128)} %get-tuple-element.37.refs_10_.refs_8_) | copy-start | bytes 1966084
  27.2 3.8 %collective-permute-start.12 = (bf16[2,128,128]{2,1,0:T(8,128)(2,1)S(1)}, bf16[2,128,128]{2,1,0:T(8,128)(2,1)S(1)}, u32[]{:S(2)}, u32[]{:S(2)}) collective-permute-start(bf16[2,128,128]{2,1,0:T(8,128)(2,1)S(1)} %slice_select_fusion.2), channel_id=1, source_target_pairs={{0,1},{1,0},{2,3},{3,2},{4,5},{5,4},{6,7},{7,6},{8,9},{9,8},{10,11... | collective-permute-start | bytes 196616 | tf_op jit(solution)/shard_map/ppermute | solution.py:452
  28.9 2.1 %collective-permute-start.11 = (bf16[2,128,128]{2,1,0:T(8,128)(2,1)S(1)}, bf16[2,128,128]{2,1,0:T(8,128)(2,1)S(1)}, u32[]{:S(2)}, u32[]{:S(2)}) collective-permute-start(bf16[2,128,128]{2,1,0:T(8,128)(2,1)S(1)} %slice_select_fusion.3), channel_id=1, source_target_pairs={{0,1},{1,0},{2,3},{3,2},{4,5},{5,4},{6,7},{7,6},{8,9},{9,8},{10,11... | collective-permute-start | bytes 196616 | tf_op jit(solution)/shard_map/ppermute | solution.py:452
  29.0 7.7 %collective-permute-start.15 = (bf16[2,128,128]{2,1,0:T(8,128)(2,1)S(1)}, bf16[2,128,128]{2,1,0:T(8,128)(2,1)S(1)}, u32[]{:S(2)}, u32[]{:S(2)}) collective-permute-start(bf16[2,128,128]{2,1,0:T(8,128)(2,1)S(1)} %slice_select_fusion), channel_id=1, source_target_pairs={{0,1},{1,0},{2,3},{3,2},{4,5},{5,4},{6,7},{7,6},{8,9},{9,8},{10,11... | collective-permute-start | bytes 196616 | tf_op jit(solution)/shard_map/ppermute | solution.py:452
  29.5 6.4 %collective-permute-start.13 = (bf16[1,128,512]{2,1,0:T(8,128)(2,1)S(1)}, bf16[1,128,512]{2,1,0:T(8,128)(2,1)S(1)}, u32[]{:S(2)}, u32[]{:S(2)}) collective-permute-start(bf16[1,128,512]{2,1,0:T(8,128)(2,1)S(1)} %slice.67), channel_id=1, source_target_pairs={{4,0},{8,4},{12,8},{14,12},{10,14},{6,10},{2,6},{0,2},{5,1},{9,5},... | collective-permute-start | bytes 393224 | tf_op jit(solution)/shard_map/ppermute | solution.py:536
  29.7 6.3 %collective-permute-start.9 = (bf16[1,128,512]{2,1,0:T(8,128)(2,1)S(1)}, bf16[1,128,512]{2,1,0:T(8,128)(2,1)S(1)}, u32[]{:S(2)}, u32[]{:S(2)}) collective-permute-start(bf16[1,128,512]{2,1,0:T(8,128)(2,1)S(1)} %slice.62), channel_id=1, source_target_pairs={{0,4},{4,8},{8,12},{12,14},{14,10},{10,6},{6,2},{2,0},{1,5},{5,9},... | collective-permute-start | bytes 393224 | tf_op jit(solution)/shard_map/ppermute | solution.py:536
  36.0 3.3 %collective-permute-start.14 = (bf16[2,128,128]{2,1,0:T(8,128)(2,1)S(1)}, bf16[2,128,128]{2,1,0:T(8,128)(2,1)S(1)}, u32[]{:S(2)}, u32[]{:S(2)}) collective-permute-start(bf16[2,128,128]{2,1,0:T(8,128)(2,1)S(1)} %slice_select_fusion.1), channel_id=1, source_target_pairs={{0,1},{1,0},{2,3},{3,2},{4,5},{5,4},{6,7},{7,6},{8,9},{9,8},{10,11... | collective-permute-start | bytes 196616 | tf_op jit(solution)/shard_map/ppermute | solution.py:452

commit v4 on v3

--- a/solution.py
+++ b/solution.py
@@ -297,7 +297,7 @@
     x_ref[1] = image[:, beams:]
 
 
-def merge_child(x_ref, ang, shift, table, s_ref, y_ref, base_ref, o_ref, half_bins):
+def merge_child(x_ref, ang, shift, table, s_ref, y_ref, z_ref, base_ref, o_ref, half_bins):
     beams = x_ref.shape[2]
     beam_index = lax.broadcasted_iota(jnp.int32, (beams, beams), 0)
     hits = jnp.where(beam_index == ang[...], 1.0, 0.0).astype(jnp.bfloat16)
@@ -311,34 +311,50 @@
                 ]
     offset = shift[...]
     bits = [(offset & (1 << b)) != 0 for b in range(5)]
+    taps, middle = INTERP_LEN, SUBS // 2
+    n = STEP // 2
+    width = n + taps - 1
     steps = half_bins // STEP
-    for step in range(steps + 1):
-        base = step * STEP
-        row = [s_ref[pl.ds((base + k) * SUBS, SUBS), :] for k in range(STEP + 31)]
+    last = half_bins + taps - 1
+    for start in range(0, last, 2 * STEP):
+        count = min(2 * STEP, last - start)
+        row = [s_ref[pl.ds((start + k) * SUBS, SUBS), :] for k in range(count + 31)]
         for b in (4, 3, 2, 1, 0):
             d = 1 << b
             row = [jnp.where(bits[b], row[k + d], row[k]) for k in range(len(row) - d)]
-        for k in range(STEP):
-            y_ref[pl.ds((base + k) * SUBS, SUBS), :] = row[k]
-    taps = INTERP_LEN
+        for k in range(count):
+            y_ref[pl.ds((start + k) * SUBS, SUBS), :] = row[k]
+            both = row[k] + pltpu.roll(row[k], middle, 0)
+            for group in range(2 * steps):
+                index = start + k - group * n
+                if 0 <= index < width:
+                    place, side = (group // 2) * width + index, (group % 2) * middle
+                    z_ref[pl.ds(place * SUBS + side, middle), :] = both[side : side + middle]
+    first_part = lax.broadcasted_iota(jnp.int32, (SUBS, LANES), 0) < middle
+
+    def filtered(ref, start, weights):
+        total = ref[pl.ds(start * SUBS, SUBS), :] * weights[0]
+        for t in range(1, taps):
+            total = total + ref[pl.ds((start + t) * SUBS, SUBS), :] * weights[t]
+        return total
+
     for step in range(steps):
-        far_r, far_i = table[FAR + step], table[FAR + steps + step]
-        w_r, w_i = [], []
-        for t in range(taps):
-            a, b = table[t], table[taps + t]
-            w_r.append(a * far_r - b * far_i)
-            w_i.append(a * far_i + b * far_r)
-        for low in range(0, STEP, SUBS):
-            base = step * STEP + low
-            row = [y_ref[pl.ds((base + k) * SUBS, SUBS), :] for k in range(SUBS + taps - 1)]
-            for k in range(SUBS):
-                a, b = row[k] * w_r[0], row[k] * w_i[0]
-                for t in range(1, taps):
-                    a = a + row[k + t] * w_r[t]
-                    b = b + row[k + t] * w_i[t]
-                e_r, e_i = table[NEAR + low + k], table[NEAR + STEP + low + k]
-                value = (e_r * a - e_i * b) + pltpu.roll(e_i * a + e_r * b, SUBS // 2, 0)
-                place = pl.ds((base + k) * SUBS, SUBS)
+        far = table[FAR + step], table[FAR + steps + step]
+        turned_taps = [product((table[t], table[taps + t]), far) for t in range(taps)]
+        w_sum = [real for real, imag in turned_taps]
+        w_one = [imag - real for real, imag in turned_taps]
+        for k in range(n):
+            shared = filtered(z_ref, step * width + k, w_sum)
+            turned = pltpu.roll(shared, middle, 0)
+            for low, sums in (
+                (k, jnp.where(first_part, shared, turned)),
+                (n + k, jnp.where(first_part, turned, shared)),
+            ):
+                bin_index = step * STEP + low
+                value = sums + pltpu.roll(filtered(y_ref, bin_index, w_one), middle, 0)
+                e_r, e_i = table[NEAR + low], table[NEAR + STEP + low]
+                value = value * e_r + pltpu.roll(value * e_i, middle, 0)
+                place = pl.ds(bin_index * SUBS, SUBS)
                 o_ref[place, :] = value if base_ref is None else base_ref[place, :] + value
 
 
@@ -370,64 +386,64 @@
                 ] = value.T
 
 
-def merge_low(halves, order, shared, table0, x0_ref, s_ref, y_ref, base, out_ref, half_bins):
+def merge_low(halves, order, shared, table0, x0_ref, rooms, base, out_ref, half_bins):
     near_mat, edge_mat, steer, ang, shift = shared
     form(halves, steer, x0_ref)
     merge_child(
-        x0_ref, ang.at[0, order], shift.at[0, order], table0.at[order], s_ref, y_ref, base, out_ref, half_bins
-    )
-
-
-def merge_top(o_ref, order, shared, table1, x1_ref, s_ref, y_ref, base, out_ref, half_bins, total):
+        x0_ref, ang.at[0, order], shift.at[0, order], table0.at[order], *rooms, base, out_ref, half_bins
+    )
+
+
+def merge_top(o_ref, order, shared, table1, x1_ref, rooms, base, out_ref, half_bins, total):
     near_mat, edge_mat, steer, ang, shift = shared
     first = lax.axis_index("range") * (total // 2) - RIM_CELLS
     merged_image(o_ref, x1_ref, x1_ref.shape[1] // 2, first, total)
     merge_child(
-        x1_ref, ang.at[1, order], shift.at[1, order], table1.at[order], s_ref, y_ref, base, out_ref, half_bins
+        x1_ref, ang.at[1, order], shift.at[1, order], table1.at[order], *rooms, base, out_ref, half_bins
     )
 
 
 def first_stage(total, *refs):
     pieces, shared, table0, refs = refs[:8], refs[8:13], refs[13], refs[14:]
-    part, c_own, c_next, c_a, c_b, x0_ref, s_ref, y_ref = refs
+    part, c_own, c_next, c_a, c_b, x0_ref, *rooms = refs
     core = lax.axis_index("range")
     for i, c_ref in enumerate((c_a, c_b, c_own, c_next)):
         squeeze(pieces[2 * i], pieces[2 * i + 1], core, shared[0], shared[1], c_ref)
     half0 = part.shape[0] // (SUBS)
-    merge_low((c_a, c_b), 1, shared, table0, x0_ref, s_ref, y_ref, None, part, half0)
+    merge_low((c_a, c_b), 1, shared, table0, x0_ref, rooms, None, part, half0)
 
 
 def second_stage(total, *refs):
     pieces, shared, table0, refs = refs[:4], refs[4:9], refs[9], refs[10:]
     table1, part, c_own = refs[:3]
-    near, c_b, c_a, x0_ref, s_ref, y_ref, o_ref, x1_ref = refs[3:]
+    near, c_b, c_a, x0_ref, o_ref, x1_ref, *rooms = refs[3:]
     core = lax.axis_index("range")
     for i, c_ref in enumerate((c_a, c_b)):
         squeeze(pieces[2 * i], pieces[2 * i + 1], core, shared[0], shared[1], c_ref)
     half0, half1 = o_ref.shape[0] // SUBS, near.shape[0] // SUBS
-    merge_low((c_own, c_a), 0, shared, table0, x0_ref, s_ref, y_ref, part, o_ref, half0)
-    merge_top(o_ref, 0, shared, table1, x1_ref, s_ref, y_ref, None, near, half1, total)
+    merge_low((c_own, c_a), 0, shared, table0, x0_ref, rooms, part, o_ref, half0)
+    merge_top(o_ref, 0, shared, table1, x1_ref, rooms, None, near, half1, total)
 
 
 def third_stage(total, *refs):
     pieces, shared, table0, refs = refs[:2], refs[2:7], refs[7], refs[8:]
     c_next, c_b = refs[:2]
-    other, c_last, x0_ref, s_ref, y_ref = refs[2:]
+    other, c_last, x0_ref, *rooms = refs[2:]
     core = lax.axis_index("range")
     squeeze(pieces[0], pieces[1], core, shared[0], shared[1], c_last)
     half0 = other.shape[0] // SUBS
-    merge_low((c_next, c_b), 0, shared, table0, x0_ref, s_ref, y_ref, None, other, half0)
+    merge_low((c_next, c_b), 0, shared, table0, x0_ref, rooms, None, other, half0)
 
 
 def last_stage(total, *refs):
     pieces, shared, table0, refs = refs[:2], refs[2:7], refs[7], refs[8:]
     table1, near, other, c_last = refs[:4]
-    out_ref, c_a, x0_ref, s_ref, y_ref, o_ref, x1_ref, final = refs[4:]
+    out_ref, c_a, x0_ref, o_ref, x1_ref, final, *rooms = refs[4:]
     core = lax.axis_index("range")
     squeeze(pieces[0], pieces[1], core, shared[0], shared[1], c_a)
     half0, half1 = o_ref.shape[0] // SUBS, final.shape[0] // SUBS
-    merge_low((c_last, c_a), 1, shared, table0, x0_ref, s_ref, y_ref, other, o_ref, half0)
-    merge_top(o_ref, 1, shared, table1, x1_ref, s_ref, y_ref, near, final, half1, total)
+    merge_low((c_last, c_a), 1, shared, table0, x0_ref, rooms, other, o_ref, half0)
+    merge_top(o_ref, 1, shared, table1, x1_ref, rooms, near, final, half1, total)
     finished(final, out_ref, half1)
 
 
@@ -491,7 +507,7 @@
     squeezed = ((2, window, pulses), bf16)
     sums0, sums1 = ((half0 * SUBS, LANES), f32), ((half1 * SUBS, LANES), f32)
     image0, image1 = ((2, window, beams), bf16), ((2, window - SPAN, beams), bf16)
-    room = ((rows, LANES), f32)
+    rooms = [((rows, LANES), f32)] * 3
 
     def run(kernel, pieces, carried, out, scratch):
         given = [x for piece in pieces for x in piece] + [*shared, table0, *carried]
@@ -530,7 +546,7 @@
         ],
         [],
         [sums0, squeezed, squeezed],
-        [squeezed, squeezed, image0, room, room],
+        [squeezed, squeezed, image0, *rooms],
     )
     up3, down3 = after(up3, part), after(down3, part)
     far_up, far_down = lax.ppermute(up3[:1], axes, ahead), lax.ppermute(down3[1:], axes, behind)
@@ -540,18 +556,18 @@
         [pair(choose(up1, up3, down3, down1)), pair(choose(up3, down3, up3, down3))],
         [table1, part, c_own],
         [sums1, squeezed],
-        [squeezed, image0, room, room, sums0, image1],
+        [squeezed, image0, sums0, image1, *rooms],
     )
     far = pair(jnp.concatenate([after(far_up, near), after(far_down, near)], axis=0))
     other, c_last = run(
-        third_stage, [last], [c_next, c_b], [sums0, squeezed], [image0, room, room]
+        third_stage, [last], [c_next, c_b], [sums0, squeezed], [image0, *rooms]
     )
     return run(
         last_stage,
         [(far[0], after(far[1], other))],
         [table1, near, other, c_last],
         [((1, 2, beams, bins), f32)],
-        [squeezed, image0, room, room, sums0, image1, sums1],
+        [squeezed, image0, sums0, image1, sums1, *rooms],
     )[0]
 
 

time: 45.5 us -> 44.9 us (0.987)
  Pallas kernels: 21 us -> 20.3 us
    pallas_call x4, Pallas kernels: 17.2 us -> 16.5 us  [run(): pl.pallas_call(functools.partial(kernel, total), out_shape=[jax.ShapeDtyp...]
  transfers between devices with their start and end apart: 16 -> 16, of which waited for: 5 -> 5; matrix products, arithmetic and copies ran while one was open for 2% -> 2% of each run, Pallas kernels for 33% -> 32%
where the time goes in v4:
time: 44.9 us; the launch traced here: 44.7 us
  Pallas kernels  20.3 us (45%)
  starting transfers between devices  15.8 us (35%)
  waiting for transfers between devices  7.16 us (16%)
  other arithmetic  1.15 us (3%)
    pallas_call x4, Pallas kernels, run(): pl.pallas_call(functools.partial(kernel, total), out_shape=[jax.ShapeDtyp...  16.5 us
    ppermute x8, starting transfers between devices, other_core(): return lax.ppermute(rim, 'range', [(0, 1), (1, 0)])  9.27 us
    pallas_call x1, Pallas kernels, ring_of_chips(): pl.pallas_call(functools.partial(table_kernel, total=total), out_shape=[j...  3.73 us
    ppermute x1, waiting for transfers between devices, ring_of_chips(): lax.ppermute(down2, axes, behind)  3.28 us
    ppermute x1, starting transfers between devices, ring_of_chips(): lax.ppermute(echoes, axes, behind)  2.04 us
    ppermute x1, waiting for transfers between devices, ring_of_chips(): lax.ppermute(up1, axes, ahead)  1.92 us
    ppermute x1, starting transfers between devices, ring_of_chips(): lax.ppermute(up3[:1], axes, ahead)  1.3 us
    ppermute x1, starting transfers between devices, ring_of_chips(): lax.ppermute(up2, axes, ahead)  1.3 us
  transfers between devices with their start and end apart: 16, of which 5 were waited for; matrix products, arithmetic and copies ran while one was open for 2% of the time, Pallas kernels for 32%

profile of v4, /device:TPU:1, one launch (start us, length us, event | category | flops | bytes accessed | tf_op | source)
XLA Modules:
  0.0 44.7 jit_solution(18335563859869693882)
XLA Ops:
  0.0 2.0 %collective-permute-start.3 = (bf16[2,128,512]{2,1,0:T(8,128)(2,1)}, bf16[2,128,512]{2,1,0:T(8,128)(2,1)S(1)}, u32[]{:S(2)}, u32[]{:S(2)}) collective-permute-start(bf16[2,128,512]{2,1,0:T(8,128)(2,1)} %refs_4_.3), channel_id=1, source_target_pairs={{4,0},{8,4},{12,8},{14,12},{10,14},{6,10},{2,6},{0,2},{5,1},{9,5},... | collective-permute-start | bytes 786440 | tf_op jit(solution)/shard_map/ppermute | solution.py:533
  2.1 0.9 %slice_select_fusion.7 = bf16[2,128,128]{2,1,0:T(8,128)(2,1)S(1)} fusion(bf16[2,128,512]{2,1,0:T(8,128)(2,1)} %refs_4_.3, pred[]{:T(512)S(6)} %eq.14), kind=kLoop, calls=%fused_computation.17 | loop fusion | flops 32768 | bytes 196609 | tf_op jit(solution)/shard_map/jit(_where)/select_n | solution.py:467
  3.0 1.0 %collective-permute-start.7 = (bf16[2,128,128]{2,1,0:T(8,128)(2,1)S(1)}, bf16[2,128,128]{2,1,0:T(8,128)(2,1)S(1)}, u32[]{:S(2)}, u32[]{:S(2)}) collective-permute-start(bf16[2,128,128]{2,1,0:T(8,128)(2,1)S(1)} %slice_select_fusion.7), channel_id=1, source_target_pairs={{0,1},{1,0},{2,3},{3,2},{4,5},{5,4},{6,7},{7,6},{8,9},{9,8},{10,11... | collective-permute-start | bytes 196616 | tf_op jit(solution)/shard_map/ppermute | solution.py:468
  4.0 3.7 %tables.1 = (bf16[256,512]{1,0:T(8,128)(2,1)}, bf16[64,256]{1,0:T(8,128)(2,1)}, bf16[512,512]{1,0:T(8,128)(2,1)}, s32[2,2,1,256]{3,2,1,0:T(1,128)}, s32[2,2,8,12...) custom-call(bf16[2,64]{1,0:T(2,128)(2,1)} %refs_0_.1, f32[256,256]{1,0:T(8,128)} %refs_1_.1, ...), custom_call_target="tpu_custom_call" | custom-call | flops 1000000000 | bytes 4194304 | tf_op jit(solution)/shard_map/tables/pallas_call | solution.py:482
  7.8 0.6 %collective-permute-done.3 = bf16[2,128,512]{2,1,0:T(8,128)(2,1)S(1)} collective-permute-done((bf16[2,128,512]{2,1,0:T(8,128)(2,1)}, bf16[2,128,512]{2,1,0:T(8,128)(2,1)S(1)}, u32[]{:S(2)}, u32[]{:S(2)}) %collective-permute-start.3) | collective-permute-done | bytes 262176 | tf_op jit(solution)/shard_map/ppermute | solution.py:533
  8.4 0.7 %collective-permute-done = bf16[2,128,512]{2,1,0:T(8,128)(2,1)S(1)} collective-permute-done((bf16[2,128,512]{2,1,0:T(8,128)(2,1)}, bf16[2,128,512]{2,1,0:T(8,128)(2,1)S(1)}, u32[]{:S(2)}, u32[]{:S(2)}) %collective-permute-start) | collective-permute-done | bytes 262176 | tf_op jit(solution)/shard_map/ppermute | solution.py:533
  9.1 0.6 %collective-permute-start.1 = (bf16[2,128,512]{2,1,0:T(8,128)(2,1)S(1)}, bf16[2,128,512]{2,1,0:T(8,128)(2,1)S(1)}, u32[]{:S(2)}, u32[]{:S(2)}) collective-permute-start(bf16[2,128,512]{2,1,0:T(8,128)(2,1)S(1)} %collective-permute-done), channel_id=1, source_target_pairs={{0,4},{4,8},{8,12},{12,14},{14,10},{10,6},{6,2},{2,0},{1,5},{5,9},... | collective-permute-start | bytes 786440 | tf_op jit(solution)/shard_map/ppermute | solution.py:536
  9.7 0.9 %collective-permute-start.5 = (bf16[2,128,512]{2,1,0:T(8,128)(2,1)S(1)}, bf16[2,128,512]{2,1,0:T(8,128)(2,1)S(1)}, u32[]{:S(2)}, u32[]{:S(2)}) collective-permute-start(bf16[2,128,512]{2,1,0:T(8,128)(2,1)S(1)} %collective-permute-done.3), channel_id=1, source_target_pairs={{4,0},{8,4},{12,8},{14,12},{10,14},{6,10},{2,6},{0,2},{5,1},{9,5},... | collective-permute-start | bytes 786440 | tf_op jit(solution)/shard_map/ppermute | solution.py:536
  10.6 2.5 %collective-permute-start.4 = (bf16[2,128,128]{2,1,0:T(8,128)(2,1)S(1)}, bf16[2,128,128]{2,1,0:T(8,128)(2,1)S(1)}, u32[]{:S(2)}, u32[]{:S(2)}) collective-permute-start(bf16[2,128,128]{2,1,0:T(8,128)(2,1)S(1)} %slice_select_fusion.6), channel_id=1, source_target_pairs={{0,1},{1,0},{2,3},{3,2},{4,5},{5,4},{6,7},{7,6},{8,9},{9,8},{10,11... | collective-permute-start | bytes 196616 | tf_op jit(solution)/shard_map/ppermute | solution.py:468
  13.1 1.9 %collective-permute-done.1 = bf16[2,128,512]{2,1,0:T(8,128)(2,1)S(1)} collective-permute-done((bf16[2,128,512]{2,1,0:T(8,128)(2,1)S(1)}, bf16[2,128,512]{2,1,0:T(8,128)(2,1)S(1)}, u32[]{:S(2)}, u32[]{:S(2)}) %collective-permute-start.1) | collective-permute-done | bytes 262176 | tf_op jit(solution)/shard_map/ppermute | solution.py:536
  15.0 0.6 %collective-permute-done.5 = bf16[2,128,512]{2,1,0:T(8,128)(2,1)S(1)} collective-permute-done((bf16[2,128,512]{2,1,0:T(8,128)(2,1)S(1)}, bf16[2,128,512]{2,1,0:T(8,128)(2,1)S(1)}, u32[]{:S(2)}, u32[]{:S(2)}) %collective-permute-start.5) | collective-permute-done | bytes 262176 | tf_op jit(solution)/shard_map/ppermute | solution.py:536
  15.8 2.8 %collective-permute-start.6 = (bf16[2,128,128]{2,1,0:T(8,128)(2,1)S(1)}, bf16[2,128,128]{2,1,0:T(8,128)(2,1)S(1)}, u32[]{:S(2)}, u32[]{:S(2)}) collective-permute-start(bf16[2,128,128]{2,1,0:T(8,128)(2,1)S(1)} %slice_select_fusion.5), channel_id=1, source_target_pairs={{0,1},{1,0},{2,3},{3,2},{4,5},{5,4},{6,7},{7,6},{8,9},{9,8},{10,11... | collective-permute-start | bytes 196616 | tf_op jit(solution)/shard_map/ppermute | solution.py:468
  18.6 1.3 %collective-permute-start.2 = (bf16[2,128,512]{2,1,0:T(8,128)(2,1)S(1)}, bf16[2,128,512]{2,1,0:T(8,128)(2,1)S(1)}, u32[]{:S(2)}, u32[]{:S(2)}) collective-permute-start(bf16[2,128,512]{2,1,0:T(8,128)(2,1)S(1)} %collective-permute-done.1), channel_id=1, source_target_pairs={{0,4},{4,8},{8,12},{12,14},{14,10},{10,6},{6,2},{2,0},{1,5},{5,9},... | collective-permute-start | bytes 786440 | tf_op jit(solution)/shard_map/ppermute | solution.py:538
  19.9 0.2 collective-permute-start.10
  20.2 3.6 %first_stage.1 = (f32[2176,128]{1,0:T(8,128)S(1)}, bf16[2,576,128]{2,1,0:T(8,128)(2,1)S(1)}, bf16[2,576,128]{2,1,0:T(8,128)(2,1)S(1)}) custom-call(bf16[2,128,512]{2,1,0:T(8,128)(2,1)S(1)} %fusion.3.refs_0_, bf16[2,128,128]{2,1,0:T(8,128)(2,1)S(1)} %collective-permute-done.4.refs_1_, bf16[2,128,512]{2,1,0:T(8,128)(2,1)S(1)} %get-tuple-element.51.refs_2_, ...), custom_call_target="tpu_custom_call" | custom-call | flops 3000000000 | bytes 4194304 | tf_op jit(solution)/shard_map/first_stage/pallas_call | solution.py:514
  23.8 3.3 %collective-permute-done.10 = bf16[2,128,512]{2,1,0:T(8,128)(2,1)S(1)} collective-permute-done((bf16[2,128,512]{2,1,0:T(8,128)(2,1)S(1)}, bf16[2,128,512]{2,1,0:T(8,128)(2,1)S(1)}, u32[]{:S(2)}, u32[]{:S(2)}) %collective-permute-start.10) | collective-permute-done | bytes 262176 | tf_op jit(solution)/shard_map/ppermute | solution.py:538
  27.2 1.7 %collective-permute-start.12 = (bf16[2,128,128]{2,1,0:T(8,128)(2,1)S(1)}, bf16[2,128,128]{2,1,0:T(8,128)(2,1)S(1)}, u32[]{:S(2)}, u32[]{:S(2)}) collective-permute-start(bf16[2,128,128]{2,1,0:T(8,128)(2,1)S(1)} %slice_select_fusion.2), channel_id=1, source_target_pairs={{0,1},{1,0},{2,3},{3,2},{4,5},{5,4},{6,7},{7,6},{8,9},{9,8},{10,11... | collective-permute-start | bytes 196616 | tf_op jit(solution)/shard_map/ppermute | solution.py:468
  29.0 0.5 %collective-permute-start.15 = (bf16[2,128,128]{2,1,0:T(8,128)(2,1)S(1)}, bf16[2,128,128]{2,1,0:T(8,128)(2,1)S(1)}, u32[]{:S(2)}, u32[]{:S(2)}) collective-permute-start(bf16[2,128,128]{2,1,0:T(8,128)(2,1)S(1)} %slice_select_fusion), channel_id=1, source_target_pairs={{0,1},{1,0},{2,3},{3,2},{4,5},{5,4},{6,7},{7,6},{8,9},{9,8},{10,11... | collective-permute-start | bytes 196616 | tf_op jit(solution)/shard_map/ppermute | solution.py:468
  29.5 0.2 collective-permute-start.13
  29.7 1.3 %collective-permute-start.9 = (bf16[1,128,512]{2,1,0:T(8,128)(2,1)S(1)}, bf16[1,128,512]{2,1,0:T(8,128)(2,1)S(1)}, u32[]{:S(2)}, u32[]{:S(2)}) collective-permute-start(bf16[1,128,512]{2,1,0:T(8,128)(2,1)S(1)} %slice.62), channel_id=1, source_target_pairs={{0,4},{4,8},{8,12},{12,14},{14,10},{10,6},{6,2},{2,0},{1,5},{5,9},... | collective-permute-start | bytes 393224 | tf_op jit(solution)/shard_map/ppermute | solution.py:552
  31.0 4.6 %second_stage.1 = (f32[2048,128]{1,0:T(8,128)S(1)}, bf16[2,576,128]{2,1,0:T(8,128)(2,1)S(1)}) custom-call(bf16[2,128,512]{2,1,0:T(8,128)(2,1)S(1)} %get-tuple-element.48.refs_0_, bf16[2,128,128]{2,1,0:T(8,128)(2,1)S(1)} %collective-permute-done.11.refs_1_, bf16[2,128,512]{2,1,0:T(8,128)(2,1)S(1)} %get-tuple-element.49.refs_2_, ...), custom_call_target="tpu_custom_call" | custom-call | flops 3000000000 | bytes 4194304 | tf_op jit(solution)/shard_map/second_stage/pallas_call | solution.py:514
  35.7 0.7 %collective-permute-start.14 = (bf16[2,128,128]{2,1,0:T(8,128)(2,1)S(1)}, bf16[2,128,128]{2,1,0:T(8,128)(2,1)S(1)}, u32[]{:S(2)}, u32[]{:S(2)}) collective-permute-start(bf16[2,128,128]{2,1,0:T(8,128)(2,1)S(1)} %slice_select_fusion.1), channel_id=1, source_target_pairs={{0,1},{1,0},{2,3},{3,2},{4,5},{5,4},{6,7},{7,6},{8,9},{9,8},{10,11... | collective-permute-start | bytes 196616 | tf_op jit(solution)/shard_map/ppermute | solution.py:468
  36.4 2.6 %third_stage.1 = (f32[2176,128]{1,0:T(8,128)S(1)}, bf16[2,576,128]{2,1,0:T(8,128)(2,1)S(1)}) custom-call(bf16[2,128,512]{2,1,0:T(8,128)(2,1)S(1)} %get-tuple-element.47.refs_0_, bf16[2,128,128]{2,1,0:T(8,128)(2,1)S(1)} %collective-permute-done.15.refs_1_, bf16[256,512]{1,0:T(8,128)(2,1)S(1)} %copy-done.4, bf16[64,256]{1,0:T(8,128)(2,1)S(1)} %copy-done.5, ...), custom_call_target="tpu_custom_call" | custom-call | flops 3000000000 | bytes 4194304 | tf_op jit(solution)/shard_map/third_stage/pallas_call | solution.py:514
  39.0 5.7 %last_stage.1 = f32[1,2,256,512]{3,2,1,0:T(8,128)} custom-call(bf16[2,128,512]{2,1,0:T(8,128)(2,1)S(1)} %constant_dynamic-update-slice_fusion.refs_0_, bf16[2,128,128]{2,1,0:T(8,128)(2,1)S(1)} %collective-permute-done.14.refs_1_, bf16[256,512]{1,0:T(8,128)(2,1)S(1)} %copy-done.4, bf16[64,256]{1,0:T(8,128)(2,1)S(1)} %copy-done.5, ...), custom_call_target="tpu_custom_call" | custom-call | flops 3000000000 | bytes 4194304 | tf_op jit(solution)/shard_map/last_stage/pallas_call | solution.py:514
  (44 shorter events, 0.6 us)
Async XLA Ops:
  0.0 8.4 %collective-permute-start.3 = (bf16[2,128,512]{2,1,0:T(8,128)(2,1)}, bf16[2,128,512]{2,1,0:T(8,128)(2,1)S(1)}, u32[]{:S(2)}, u32[]{:S(2)}) collective-permute-start(bf16[2,128,512]{2,1,0:T(8,128)(2,1)} %refs_4_.3), channel_id=1, source_target_pairs={{4,0},{8,4},{12,8},{14,12},{10,14},{6,10},{2,6},{0,2},{5,1},{9,5},... | collective-permute-start | bytes 786440 | tf_op jit(solution)/shard_map/ppermute | solution.py:533
  2.0 7.1 %collective-permute-start = (bf16[2,128,512]{2,1,0:T(8,128)(2,1)}, bf16[2,128,512]{2,1,0:T(8,128)(2,1)S(1)}, u32[]{:S(2)}, u32[]{:S(2)}) collective-permute-start(bf16[2,128,512]{2,1,0:T(8,128)(2,1)} %refs_4_.3), channel_id=1, source_target_pairs={{0,4},{4,8},{8,12},{12,14},{14,10},{10,6},{6,2},{2,0},{1,5},{5,9},... | collective-permute-start | bytes 786440 | tf_op jit(solution)/shard_map/ppermute | solution.py:533
  3.0 16.9 %collective-permute-start.7 = (bf16[2,128,128]{2,1,0:T(8,128)(2,1)S(1)}, bf16[2,128,128]{2,1,0:T(8,128)(2,1)S(1)}, u32[]{:S(2)}, u32[]{:S(2)}) collective-permute-start(bf16[2,128,128]{2,1,0:T(8,128)(2,1)S(1)} %slice_select_fusion.7), channel_id=1, source_target_pairs={{0,1},{1,0},{2,3},{3,2},{4,5},{5,4},{6,7},{7,6},{8,9},{9,8},{10,11... | collective-permute-start | bytes 196616 | tf_op jit(solution)/shard_map/ppermute | solution.py:468
  8.4 11.8 %copy-start = (bf16[2,128,512]{2,1,0:T(8,128)(2,1)S(1)}, bf16[2,128,512]{2,1,0:T(8,128)(2,1)}, u32[]{:S(2)}) copy-start(bf16[2,128,512]{2,1,0:T(8,128)(2,1)} %refs_4_.3) | copy-start | bytes 786436
  8.4 11.8 %copy-start.1 = (f32[2,82,8,128]{3,2,1,0:T(8,128)S(1)}, f32[2,82,8,128]{3,2,1,0:T(8,128)}, u32[]{:S(2)}) copy-start(f32[2,82,8,128]{3,2,1,0:T(8,128)} %get-tuple-element.33.refs_13_.refs_9_.refs_7_) | copy-start | bytes 2015236
  8.4 11.8 %copy-start.3 = (bf16[512,512]{1,0:T(8,128)(2,1)S(1)}, bf16[512,512]{1,0:T(8,128)(2,1)}, u32[]{:S(2)}) copy-start(bf16[512,512]{1,0:T(8,128)(2,1)} %get-tuple-element.30.refs_10_.refs_6_.refs_4_) | copy-start | bytes 1572868
  8.4 11.8 %copy-start.4 = (bf16[256,512]{1,0:T(8,128)(2,1)S(1)}, bf16[256,512]{1,0:T(8,128)(2,1)}, u32[]{:S(2)}) copy-start(bf16[256,512]{1,0:T(8,128)(2,1)} %get-tuple-element.26.refs_8_.refs_4_.refs_2_) | copy-start | bytes 786436
  8.4 11.8 %copy-start.5 = (bf16[64,256]{1,0:T(8,128)(2,1)S(1)}, bf16[64,256]{1,0:T(8,128)(2,1)}, u32[]{:S(2)}) copy-start(bf16[64,256]{1,0:T(8,128)(2,1)} %get-tuple-element.29.refs_9_.refs_5_.refs_3_) | copy-start | bytes 98308
  8.4 11.8 %copy-start.6 = (s32[2,2,8,128]{3,2,1,0:T(8,128)S(1)}, s32[2,2,8,128]{3,2,1,0:T(8,128)}, u32[]{:S(2)}) copy-start(s32[2,2,8,128]{3,2,1,0:T(8,128)} %get-tuple-element.32.refs_12_.refs_8_.refs_6_) | copy-start | bytes 49156
  8.4 11.8 %copy-start.7 = (s32[2,2,1,256]{3,2,1,0:T(1,128)S(1)}, s32[2,2,1,256]{3,2,1,0:T(1,128)}, u32[]{:S(2)}) copy-start(s32[2,2,1,256]{3,2,1,0:T(1,128)} %get-tuple-element.31.refs_11_.refs_7_.refs_5_) | copy-start | bytes 12292
  9.1 5.9 %collective-permute-start.1 = (bf16[2,128,512]{2,1,0:T(8,128)(2,1)S(1)}, bf16[2,128,512]{2,1,0:T(8,128)(2,1)S(1)}, u32[]{:S(2)}, u32[]{:S(2)}) collective-permute-start(bf16[2,128,512]{2,1,0:T(8,128)(2,1)S(1)} %collective-permute-done), channel_id=1, source_target_pairs={{0,4},{4,8},{8,12},{12,14},{14,10},{10,6},{6,2},{2,0},{1,5},{5,9},... | collective-permute-start | bytes 786440 | tf_op jit(solution)/shard_map/ppermute | solution.py:536
  9.7 6.0 %collective-permute-start.5 = (bf16[2,128,512]{2,1,0:T(8,128)(2,1)S(1)}, bf16[2,128,512]{2,1,0:T(8,128)(2,1)S(1)}, u32[]{:S(2)}, u32[]{:S(2)}) collective-permute-start(bf16[2,128,512]{2,1,0:T(8,128)(2,1)S(1)} %collective-permute-done.3), channel_id=1, source_target_pairs={{4,0},{8,4},{12,8},{14,12},{10,14},{6,10},{2,6},{0,2},{5,1},{9,5},... | collective-permute-start | bytes 786440 | tf_op jit(solution)/shard_map/ppermute | solution.py:536
  10.6 9.5 %collective-permute-start.4 = (bf16[2,128,128]{2,1,0:T(8,128)(2,1)S(1)}, bf16[2,128,128]{2,1,0:T(8,128)(2,1)S(1)}, u32[]{:S(2)}, u32[]{:S(2)}) collective-permute-start(bf16[2,128,128]{2,1,0:T(8,128)(2,1)S(1)} %slice_select_fusion.6), channel_id=1, source_target_pairs={{0,1},{1,0},{2,3},{3,2},{4,5},{5,4},{6,7},{7,6},{8,9},{9,8},{10,11... | collective-permute-start | bytes 196616 | tf_op jit(solution)/shard_map/ppermute | solution.py:468
  15.8 4.3 %collective-permute-start.6 = (bf16[2,128,128]{2,1,0:T(8,128)(2,1)S(1)}, bf16[2,128,128]{2,1,0:T(8,128)(2,1)S(1)}, u32[]{:S(2)}, u32[]{:S(2)}) collective-permute-start(bf16[2,128,128]{2,1,0:T(8,128)(2,1)S(1)} %slice_select_fusion.5), channel_id=1, source_target_pairs={{0,1},{1,0},{2,3},{3,2},{4,5},{5,4},{6,7},{7,6},{8,9},{9,8},{10,11... | collective-permute-start | bytes 196616 | tf_op jit(solution)/shard_map/ppermute | solution.py:468
  18.6 1.6 %collective-permute-start.8 = (bf16[2,128,128]{2,1,0:T(8,128)(2,1)S(1)}, bf16[2,128,128]{2,1,0:T(8,128)(2,1)S(1)}, u32[]{:S(2)}, u32[]{:S(2)}) collective-permute-start(bf16[2,128,128]{2,1,0:T(8,128)(2,1)S(1)} %slice_select_fusion.4), channel_id=1, source_target_pairs={{0,1},{1,0},{2,3},{3,2},{4,5},{5,4},{6,7},{7,6},{8,9},{9,8},{10,11... | collective-permute-start | bytes 196616 | tf_op jit(solution)/shard_map/ppermute | solution.py:468
  18.6 8.4 %collective-permute-start.2 = (bf16[2,128,512]{2,1,0:T(8,128)(2,1)S(1)}, bf16[2,128,512]{2,1,0:T(8,128)(2,1)S(1)}, u32[]{:S(2)}, u32[]{:S(2)}) collective-permute-start(bf16[2,128,512]{2,1,0:T(8,128)(2,1)S(1)} %collective-permute-done.1), channel_id=1, source_target_pairs={{0,4},{4,8},{8,12},{12,14},{14,10},{10,6},{6,2},{2,0},{1,5},{5,9},... | collective-permute-start | bytes 786440 | tf_op jit(solution)/shard_map/ppermute | solution.py:538
  19.9 7.1 %collective-permute-start.10 = (bf16[2,128,512]{2,1,0:T(8,128)(2,1)S(1)}, bf16[2,128,512]{2,1,0:T(8,128)(2,1)S(1)}, u32[]{:S(2)}, u32[]{:S(2)}) collective-permute-start(bf16[2,128,512]{2,1,0:T(8,128)(2,1)S(1)} %collective-permute-done.5), channel_id=1, source_target_pairs={{4,0},{8,4},{12,8},{14,12},{10,14},{6,10},{2,6},{0,2},{5,1},{9,5},... | collective-permute-start | bytes 786440 | tf_op jit(solution)/shard_map/ppermute | solution.py:538
  27.1 3.9 %copy-start.2 = (f32[2,80,8,128]{3,2,1,0:T(8,128)S(1)}, f32[2,80,8,128]{3,2,1,0:T(8,128)}, u32[]{:S(2)}) copy-start(f32[2,80,8,128]{3,2,1,0:T(8,128)} %get-tuple-element.37.refs_10_.refs_8_) | copy-start | bytes 1966084
  27.2 3.8 %collective-permute-start.12 = (bf16[2,128,128]{2,1,0:T(8,128)(2,1)S(1)}, bf16[2,128,128]{2,1,0:T(8,128)(2,1)S(1)}, u32[]{:S(2)}, u32[]{:S(2)}) collective-permute-start(bf16[2,128,128]{2,1,0:T(8,128)(2,1)S(1)} %slice_select_fusion.2), channel_id=1, source_target_pairs={{0,1},{1,0},{2,3},{3,2},{4,5},{5,4},{6,7},{7,6},{8,9},{9,8},{10,11... | collective-permute-start | bytes 196616 | tf_op jit(solution)/shard_map/ppermute | solution.py:468
  28.9 2.1 %collective-permute-start.11 = (bf16[2,128,128]{2,1,0:T(8,128)(2,1)S(1)}, bf16[2,128,128]{2,1,0:T(8,128)(2,1)S(1)}, u32[]{:S(2)}, u32[]{:S(2)}) collective-permute-start(bf16[2,128,128]{2,1,0:T(8,128)(2,1)S(1)} %slice_select_fusion.3), channel_id=1, source_target_pairs={{0,1},{1,0},{2,3},{3,2},{4,5},{5,4},{6,7},{7,6},{8,9},{9,8},{10,11... | collective-permute-start | bytes 196616 | tf_op jit(solution)/shard_map/ppermute | solution.py:468
  29.0 7.4 %collective-permute-start.15 = (bf16[2,128,128]{2,1,0:T(8,128)(2,1)S(1)}, bf16[2,128,128]{2,1,0:T(8,128)(2,1)S(1)}, u32[]{:S(2)}, u32[]{:S(2)}) collective-permute-start(bf16[2,128,128]{2,1,0:T(8,128)(2,1)S(1)} %slice_select_fusion), channel_id=1, source_target_pairs={{0,1},{1,0},{2,3},{3,2},{4,5},{5,4},{6,7},{7,6},{8,9},{9,8},{10,11... | collective-permute-start | bytes 196616 | tf_op jit(solution)/shard_map/ppermute | solution.py:468
  29.5 6.1 %collective-permute-start.13 = (bf16[1,128,512]{2,1,0:T(8,128)(2,1)S(1)}, bf16[1,128,512]{2,1,0:T(8,128)(2,1)S(1)}, u32[]{:S(2)}, u32[]{:S(2)}) collective-permute-start(bf16[1,128,512]{2,1,0:T(8,128)(2,1)S(1)} %slice.67), channel_id=1, source_target_pairs={{4,0},{8,4},{12,8},{14,12},{10,14},{6,10},{2,6},{0,2},{5,1},{9,5},... | collective-permute-start | bytes 393224 | tf_op jit(solution)/shard_map/ppermute | solution.py:552
  29.7 6.0 %collective-permute-start.9 = (bf16[1,128,512]{2,1,0:T(8,128)(2,1)S(1)}, bf16[1,128,512]{2,1,0:T(8,128)(2,1)S(1)}, u32[]{:S(2)}, u32[]{:S(2)}) collective-permute-start(bf16[1,128,512]{2,1,0:T(8,128)(2,1)S(1)} %slice.62), channel_id=1, source_target_pairs={{0,4},{4,8},{8,12},{12,14},{14,10},{10,6},{6,2},{2,0},{1,5},{5,9},... | collective-permute-start | bytes 393224 | tf_op jit(solution)/shard_map/ppermute | solution.py:552
  35.7 3.3 %collective-permute-start.14 = (bf16[2,128,128]{2,1,0:T(8,128)(2,1)S(1)}, bf16[2,128,128]{2,1,0:T(8,128)(2,1)S(1)}, u32[]{:S(2)}, u32[]{:S(2)}) collective-permute-start(bf16[2,128,128]{2,1,0:T(8,128)(2,1)S(1)} %slice_select_fusion.1), channel_id=1, source_target_pairs={{0,1},{1,0},{2,3},{3,2},{4,5},{5,4},{6,7},{7,6},{8,9},{9,8},{10,11... | collective-permute-start | bytes 196616 | tf_op jit(solution)/shard_map/ppermute | solution.py:468

commit v5 on v4

--- a/solution.py
+++ b/solution.py
@@ -288,7 +288,11 @@
 
 
 def form(halves, steer, x_ref):
-    pieces = [half[ri] for ri in (0, 1) for half in halves]
+    pieces = [
+        jnp.where(half[0], half[1][ri], half[2][ri]) if isinstance(half, tuple) else half[ri]
+        for ri in (0, 1)
+        for half in halves
+    ]
     image = jnp.dot(
         jnp.concatenate(pieces, axis=1), steer[...], preferred_element_type=jnp.float32
     ).astype(jnp.bfloat16)
@@ -376,14 +380,22 @@
             ).astype(jnp.bfloat16)
 
 
-def finished(o_ref, out_ref, half_bins):
+def finished(o_ref, image, out_ref, sems, half_bins):
+    copies = []
     for ri in (0, 1):
-        for half in (0, 1):
-            for part in (0, 1):
+        for part in (0, 1):
+            beams = pl.ds(part * LANES, LANES)
+            for half in (0, 1):
                 value = o_ref[pl.ds(ri * 4 + half * 2 + part, half_bins, stride=SUBS), :]
-                out_ref[
-                    0, ri, part * LANES : (part + 1) * LANES, half * half_bins : (half + 1) * half_bins
-                ] = value.T
+                image[ri, beams, half * half_bins : (half + 1) * half_bins] = value.T
+            copies.append(
+                pltpu.make_async_copy(
+                    image.at[ri, beams], out_ref.at[0, ri, beams], sems.at[len(copies)]
+                )
+            )
+            copies[-1].start()
+    for copy in copies:
+        copy.wait()
 
 
 def merge_low(halves, order, shared, table0, x0_ref, rooms, base, out_ref, half_bins):
@@ -403,11 +415,16 @@
     )
 
 
+def outer():
+    slot = lax.axis_index("aperture")
+    return (slot == 0) | (slot == lax.axis_size("aperture") - 1)
+
+
 def first_stage(total, *refs):
-    pieces, shared, table0, refs = refs[:8], refs[8:13], refs[13], refs[14:]
-    part, c_own, c_next, c_a, c_b, x0_ref, *rooms = refs
+    pieces, shared, table0, refs = refs[:10], refs[10:15], refs[15], refs[16:]
+    part, c_own, c_next, c_early, c_a, c_b, x0_ref, *rooms = refs
     core = lax.axis_index("range")
-    for i, c_ref in enumerate((c_a, c_b, c_own, c_next)):
+    for i, c_ref in enumerate((c_a, c_b, c_own, c_next, c_early)):
         squeeze(pieces[2 * i], pieces[2 * i + 1], core, shared[0], shared[1], c_ref)
     half0 = part.shape[0] // (SUBS)
     merge_low((c_a, c_b), 1, shared, table0, x0_ref, rooms, None, part, half0)
@@ -415,36 +432,35 @@
 
 def second_stage(total, *refs):
     pieces, shared, table0, refs = refs[:4], refs[4:9], refs[9], refs[10:]
-    table1, part, c_own = refs[:3]
-    near, c_b, c_a, x0_ref, o_ref, x1_ref, *rooms = refs[3:]
+    table1, part, c_own, c_early = refs[:4]
+    near, c_b, c_late, x0_ref, o_ref, x1_ref, *rooms = refs[4:]
     core = lax.axis_index("range")
-    for i, c_ref in enumerate((c_a, c_b)):
+    for i, c_ref in enumerate((c_late, c_b)):
         squeeze(pieces[2 * i], pieces[2 * i + 1], core, shared[0], shared[1], c_ref)
     half0, half1 = o_ref.shape[0] // SUBS, near.shape[0] // SUBS
-    merge_low((c_own, c_a), 0, shared, table0, x0_ref, rooms, part, o_ref, half0)
+    second = (outer(), c_early, c_late)
+    merge_low((c_own, second), 0, shared, table0, x0_ref, rooms, part, o_ref, half0)
     merge_top(o_ref, 0, shared, table1, x1_ref, rooms, None, near, half1, total)
 
 
 def third_stage(total, *refs):
-    pieces, shared, table0, refs = refs[:2], refs[2:7], refs[7], refs[8:]
-    c_next, c_b = refs[:2]
-    other, c_last, x0_ref, *rooms = refs[2:]
-    core = lax.axis_index("range")
-    squeeze(pieces[0], pieces[1], core, shared[0], shared[1], c_last)
+    shared, table0, c_next, c_b = refs[:5], refs[5], refs[6], refs[7]
+    other, x0_ref, *rooms = refs[8:]
     half0 = other.shape[0] // SUBS
     merge_low((c_next, c_b), 0, shared, table0, x0_ref, rooms, None, other, half0)
 
 
 def last_stage(total, *refs):
     pieces, shared, table0, refs = refs[:2], refs[2:7], refs[7], refs[8:]
-    table1, near, other, c_last = refs[:4]
-    out_ref, c_a, x0_ref, o_ref, x1_ref, final, *rooms = refs[4:]
+    table1, near, other, c_early, c_late = refs[:5]
+    out_ref, c_a, x0_ref, o_ref, x1_ref, final, image, sems, *rooms = refs[5:]
     core = lax.axis_index("range")
     squeeze(pieces[0], pieces[1], core, shared[0], shared[1], c_a)
     half0, half1 = o_ref.shape[0] // SUBS, final.shape[0] // SUBS
-    merge_low((c_last, c_a), 1, shared, table0, x0_ref, rooms, other, o_ref, half0)
+    first = (outer(), c_late, c_early)
+    merge_low((first, c_a), 1, shared, table0, x0_ref, rooms, other, o_ref, half0)
     merge_top(o_ref, 1, shared, table1, x1_ref, rooms, near, final, half1, total)
-    finished(final, out_ref, half1)
+    finished(final, image, out_ref, sems, half1)
 
 
 def ring_of_chips(echoes, chirp_taps, steer_phase, ang_table, range_table, interp_taps, phase_twist):
@@ -463,9 +479,10 @@
 
     core = lax.axis_index("range")
 
-    def other_core(x):
-        rim = jnp.where(core == 0, x[:, :, bins - LANES :], x[:, :, :LANES])
-        return lax.ppermute(rim, "range", [(0, 1), (1, 0)])
+    def pairs(*pieces):
+        rims = [jnp.where(core == 0, x[:, :, bins - LANES :], x[:, :, :LANES]) for x in pieces]
+        rims = lax.ppermute(jnp.concatenate(rims, axis=0), "range", [(0, 1), (1, 0)])
+        return [(x, rims[2 * i : 2 * i + 2]) for i, x in enumerate(pieces)]
 
     def choose(*options):
         picked = options[-1]
@@ -509,14 +526,14 @@
     image0, image1 = ((2, window, beams), bf16), ((2, window - SPAN, beams), bf16)
     rooms = [((rows, LANES), f32)] * 3
 
-    def run(kernel, pieces, carried, out, scratch):
+    def run(kernel, pieces, carried, out, scratch, place=vmem):
         given = [x for piece in pieces for x in piece] + [*shared, table0, *carried]
         return pl.pallas_call(
             functools.partial(kernel, total),
             out_shape=[jax.ShapeDtypeStruct(*x) for x in out],
             in_specs=[vmem] * len(given),
-            out_specs=[vmem] * len(out),
-            scratch_shapes=[pltpu.VMEM(*x) for x in scratch],
+            out_specs=[place] * len(out),
+            scratch_shapes=[pltpu.VMEM(*x) if isinstance(x, tuple) else x for x in scratch],
             compiler_params=pltpu.CompilerParams(vmem_limit_bytes=24 * 1024 * 1024),
             cost_estimate=pl.CostEstimate(
                 flops=3 * 10**9, bytes_accessed=4 * 2**20, transcendentals=0
@@ -527,47 +544,47 @@
     def after(value, result):
         return lax.optimization_barrier((value, result))[0]
 
-    def pair(x):
-        return (x, other_core(x))
-
     up1, down1 = lax.ppermute(echoes, axes, ahead), lax.ppermute(echoes, axes, behind)
-    own = pair(echoes)
+    own = pairs(echoes)
     up1, down1 = after(up1, shared[0]), after(down1, shared[0])
     up2, down2 = lax.ppermute(up1, axes, ahead), lax.ppermute(down1, axes, behind)
-    beside = pair(choose(down1, up1, down1, up1))
+    ready = pairs(choose(down1, up1, down1, up1), choose(up1, down1, up1, down1))
     up3, down3 = lax.ppermute(up2, axes, ahead), lax.ppermute(down2, axes, behind)
-    part, c_own, c_next = run(
+    fresh = pairs(choose(up2, up2, down2, down2), choose(down2, down2, up2, up2))
+    part, c_own, c_next, c_early = run(
         first_stage,
-        [
-            beside,
-            pair(choose(up2, up2, down2, down2)),
-            own,
-            pair(choose(down2, down2, up2, up2)),
-        ],
+        [ready[0], fresh[0], *own, fresh[1], ready[1]],
         [],
-        [sums0, squeezed, squeezed],
+        [sums0, squeezed, squeezed, squeezed],
         [squeezed, squeezed, image0, *rooms],
     )
     up3, down3 = after(up3, part), after(down3, part)
     far_up, far_down = lax.ppermute(up3[:1], axes, ahead), lax.ppermute(down3[1:], axes, behind)
-    last = pair(choose(down3, down1, up1, up3))
-    near, c_b = run(
+    near, c_b, c_late = run(
         second_stage,
-        [pair(choose(up1, up3, down3, down1)), pair(choose(up3, down3, up3, down3))],
-        [table1, part, c_own],
-        [sums1, squeezed],
-        [squeezed, image0, sums0, image1, *rooms],
-    )
-    far = pair(jnp.concatenate([after(far_up, near), after(far_down, near)], axis=0))
-    other, c_last = run(
-        third_stage, [last], [c_next, c_b], [sums0, squeezed], [image0, *rooms]
-    )
+        pairs(choose(down3, up3, down3, up3), choose(up3, down3, up3, down3)),
+        [table1, part, c_own, c_early],
+        [sums1, squeezed, squeezed],
+        [image0, sums0, image1, *rooms],
+    )
+    far = pairs(jnp.concatenate([after(far_up, near), after(far_down, near)], axis=0))[0]
+    other = run(third_stage, [], [c_next, c_b], [sums0], [image0, *rooms])[0]
     return run(
         last_stage,
         [(far[0], after(far[1], other))],
-        [table1, near, other, c_last],
+        [table1, near, other, c_early, c_late],
         [((1, 2, beams, bins), f32)],
-        [squeezed, image0, sums0, image1, sums1, *rooms],
+        [
+            squeezed,
+            image0,
+            sums0,
+            image1,
+            sums1,
+            ((2, beams, bins), f32),
+            pltpu.SemaphoreType.DMA((4,)),
+            *rooms,
+        ],
+        pl.BlockSpec(memory_space=pl.ANY),
     )[0]
 
 

time: 44.9 us -> 43.9 us (0.978)
  starting transfers between devices: 15.8 us -> 14.7 us
    ppermute x8 -> x5, starting transfers between devices: 9.27 us -> 8.02 us  [pairs(): lax.ppermute(jnp.concatenate(rims, axis=0), 'range', [(0, 1), (1, 0)])]
    select_n x8 -> x6, other arithmetic: 0.96 us -> 0.96 us  [pairs(): jnp.where(core == 0, x[:, :, bins - LANES:], x[:, :, :LANES])]
  transfers between devices with their start and end apart: 16 -> 13, of which waited for: 5 -> 5; matrix products, arithmetic and copies ran while one was open for 2% -> 3% of each run, Pallas kernels for 32% -> 33%
where the time goes in v5:
time: 43.9 us; the launch traced here: 43.7 us
  Pallas kernels  20.2 us (46%)
  starting transfers between devices  14.7 us (33%)
  waiting for transfers between devices  7.09 us (16%)
  other arithmetic  1.19 us (3%)
  between operations  0.46 us (1%)
    pallas_call x4, Pallas kernels, run(): pl.pallas_call(functools.partial(kernel, total), out_shape=[jax.ShapeDtyp...  16.4 us
    ppermute x5, starting transfers between devices, pairs(): lax.ppermute(jnp.concatenate(rims, axis=0), 'range', [(0, 1), (1, 0)])  8.02 us
    pallas_call x1, Pallas kernels, ring_of_chips(): pl.pallas_call(functools.partial(table_kernel, total=total), out_shape=[j...  3.73 us
    ppermute x1, waiting for transfers between devices, ring_of_chips(): lax.ppermute(down2, axes, behind)  3.35 us
    ppermute x1, starting transfers between devices, ring_of_chips(): lax.ppermute(echoes, axes, behind)  2.04 us
    ppermute x1, waiting for transfers between devices, ring_of_chips(): lax.ppermute(up1, axes, ahead)  1.79 us
    ppermute x1, starting transfers between devices, ring_of_chips(): lax.ppermute(up3[:1], axes, ahead)  1.37 us
    ppermute x1, starting transfers between devices, ring_of_chips(): lax.ppermute(up2, axes, ahead)  1.35 us
  transfers between devices with their start and end apart: 13, of which 5 were waited for; matrix products, arithmetic and copies ran while one was open for 3% of the time, Pallas kernels for 33%

profile of v5, /device:TPU:1, one launch (start us, length us, event | category | flops | bytes accessed | tf_op | source)
XLA Modules:
  0.0 43.7 jit_solution(14219988836194256287)
XLA Ops:
  0.0 2.0 %collective-permute-start.3 = (bf16[2,128,512]{2,1,0:T(8,128)(2,1)}, bf16[2,128,512]{2,1,0:T(8,128)(2,1)S(1)}, u32[]{:S(2)}, u32[]{:S(2)}) collective-permute-start(bf16[2,128,512]{2,1,0:T(8,128)(2,1)} %refs_4_.3), channel_id=1, source_target_pairs={{4,0},{8,4},{12,8},{14,12},{10,14},{6,10},{2,6},{0,2},{5,1},{9,5},... | collective-permute-start | bytes 786440 | tf_op jit(solution)/shard_map/ppermute | solution.py:547
  2.0 0.1 collective-permute-start
  2.1 0.9 %slice_select_fusion.7 = bf16[2,128,128]{2,1,0:T(8,128)(2,1)S(1)} fusion(bf16[2,128,512]{2,1,0:T(8,128)(2,1)} %refs_4_.3, pred[]{:T(512)S(6)} %eq.14), kind=kLoop, calls=%fused_computation.22 | loop fusion | flops 32768 | bytes 196609 | tf_op jit(solution)/shard_map/jit(_where)/select_n | solution.py:483
  3.0 1.0 %collective-permute-start.7 = (bf16[2,128,128]{2,1,0:T(8,128)(2,1)S(1)}, bf16[2,128,128]{2,1,0:T(8,128)(2,1)S(1)}, u32[]{:S(2)}, u32[]{:S(2)}) collective-permute-start(bf16[2,128,128]{2,1,0:T(8,128)(2,1)S(1)} %slice_select_fusion.7), channel_id=1, source_target_pairs={{0,1},{1,0},{2,3},{3,2},{4,5},{5,4},{6,7},{7,6},{8,9},{9,8},{10,11... | collective-permute-start | bytes 196616 | tf_op jit(solution)/shard_map/ppermute | solution.py:484
  4.0 3.7 %tables.1 = (bf16[256,512]{1,0:T(8,128)(2,1)}, bf16[64,256]{1,0:T(8,128)(2,1)}, bf16[512,512]{1,0:T(8,128)(2,1)}, s32[2,2,1,256]{3,2,1,0:T(1,128)}, s32[2,2,8,12...) custom-call(bf16[2,64]{1,0:T(2,128)(2,1)} %refs_0_.1, f32[256,256]{1,0:T(8,128)} %refs_1_.1, ...), custom_call_target="tpu_custom_call" | custom-call | flops 1000000000 | bytes 4194304 | tf_op jit(solution)/shard_map/tables/pallas_call | solution.py:499
  7.8 0.6 %collective-permute-done.3 = bf16[2,128,512]{2,1,0:T(8,128)(2,1)S(1)} collective-permute-done((bf16[2,128,512]{2,1,0:T(8,128)(2,1)}, bf16[2,128,512]{2,1,0:T(8,128)(2,1)S(1)}, u32[]{:S(2)}, u32[]{:S(2)}) %collective-permute-start.3) | collective-permute-done | bytes 262176 | tf_op jit(solution)/shard_map/ppermute | solution.py:547
  8.4 0.7 %collective-permute-done = bf16[2,128,512]{2,1,0:T(8,128)(2,1)S(1)} collective-permute-done((bf16[2,128,512]{2,1,0:T(8,128)(2,1)}, bf16[2,128,512]{2,1,0:T(8,128)(2,1)S(1)}, u32[]{:S(2)}, u32[]{:S(2)}) %collective-permute-start) | collective-permute-done | bytes 262176 | tf_op jit(solution)/shard_map/ppermute | solution.py:547
  9.1 0.5 %collective-permute-start.1 = (bf16[2,128,512]{2,1,0:T(8,128)(2,1)S(1)}, bf16[2,128,512]{2,1,0:T(8,128)(2,1)S(1)}, u32[]{:S(2)}, u32[]{:S(2)}) collective-permute-start(bf16[2,128,512]{2,1,0:T(8,128)(2,1)S(1)} %collective-permute-done), channel_id=1, source_target_pairs={{0,4},{4,8},{8,12},{12,14},{14,10},{10,6},{6,2},{2,0},{1,5},{5,9},... | collective-permute-start | bytes 786440 | tf_op jit(solution)/shard_map/ppermute | solution.py:550
  9.6 1.0 %collective-permute-start.5 = (bf16[2,128,512]{2,1,0:T(8,128)(2,1)S(1)}, bf16[2,128,512]{2,1,0:T(8,128)(2,1)S(1)}, u32[]{:S(2)}, u32[]{:S(2)}) collective-permute-start(bf16[2,128,512]{2,1,0:T(8,128)(2,1)S(1)} %collective-permute-done.3), channel_id=1, source_target_pairs={{4,0},{8,4},{12,8},{14,12},{10,14},{6,10},{2,6},{0,2},{5,1},{9,5},... | collective-permute-start | bytes 786440 | tf_op jit(solution)/shard_map/ppermute | solution.py:550
  10.8 2.5 %collective-permute-start.4 = (bf16[4,128,128]{2,1,0:T(8,128)(2,1)S(1)}, bf16[4,128,128]{2,1,0:T(8,128)(2,1)S(1)}, u32[]{:S(2)}, u32[]{:S(2)}) collective-permute-start(bf16[4,128,128]{2,1,0:T(8,128)(2,1)S(1)} %pad_maximum_fusion), channel_id=1, source_target_pairs={{0,1},{1,0},{2,3},{3,2},{4,5},{5,4},{6,7},{7,6},{8,9},{9,8},{10,11... | collective-permute-start | bytes 393224 | tf_op jit(solution)/shard_map/ppermute | solution.py:484
  13.3 1.8 %collective-permute-done.1 = bf16[2,128,512]{2,1,0:T(8,128)(2,1)S(1)} collective-permute-done((bf16[2,128,512]{2,1,0:T(8,128)(2,1)S(1)}, bf16[2,128,512]{2,1,0:T(8,128)(2,1)S(1)}, u32[]{:S(2)}, u32[]{:S(2)}) %collective-permute-start.1) | collective-permute-done | bytes 262176 | tf_op jit(solution)/shard_map/ppermute | solution.py:550
  15.0 0.6 %collective-permute-done.5 = bf16[2,128,512]{2,1,0:T(8,128)(2,1)S(1)} collective-permute-done((bf16[2,128,512]{2,1,0:T(8,128)(2,1)S(1)}, bf16[2,128,512]{2,1,0:T(8,128)(2,1)S(1)}, u32[]{:S(2)}, u32[]{:S(2)}) %collective-permute-start.5) | collective-permute-done | bytes 262176 | tf_op jit(solution)/shard_map/ppermute | solution.py:550
  15.8 2.7 %collective-permute-start.6 = (bf16[4,128,128]{2,1,0:T(8,128)(2,1)S(1)}, bf16[4,128,128]{2,1,0:T(8,128)(2,1)S(1)}, u32[]{:S(2)}, u32[]{:S(2)}) collective-permute-start(bf16[4,128,128]{2,1,0:T(8,128)(2,1)S(1)} %pad_maximum_fusion.1), channel_id=1, source_target_pairs={{0,1},{1,0},{2,3},{3,2},{4,5},{5,4},{6,7},{7,6},{8,9},{9,8},{10,11... | collective-permute-start | bytes 393224 | tf_op jit(solution)/shard_map/ppermute | solution.py:484
  18.5 1.3 %collective-permute-start.2 = (bf16[2,128,512]{2,1,0:T(8,128)(2,1)S(1)}, bf16[2,128,512]{2,1,0:T(8,128)(2,1)S(1)}, u32[]{:S(2)}, u32[]{:S(2)}) collective-permute-start(bf16[2,128,512]{2,1,0:T(8,128)(2,1)S(1)} %collective-permute-done.1), channel_id=1, source_target_pairs={{0,4},{4,8},{8,12},{12,14},{14,10},{10,6},{6,2},{2,0},{1,5},{5,9},... | collective-permute-start | bytes 786440 | tf_op jit(solution)/shard_map/ppermute | solution.py:552
  19.9 0.2 collective-permute-start.9
  20.1 4.0 %first_stage.1 = (f32[2176,128]{1,0:T(8,128)S(1)}, bf16[2,576,128]{2,1,0:T(8,128)(2,1)S(1)}, bf16[2,576,128]{2,1,0:T(8,128)(2,1)S(1)}, bf16[2,576,128]{2,1,0:T(8,128)(2,1)S(1)}) custom-call(bf16[2,128,512]{2,1,0:T(8,128)(2,1)S(1)} %get-tuple-element.52.refs_0_, bf16[2,128,128]{2,1,0:T(8,128)(2,1)S(1)} %get-tuple-element.56.refs_1_, ...), custom_call_target="tpu_custom_call" | custom-call | flops 3000000000 | bytes 4194304 | tf_op jit(solution)/shard_map/first_stage/pallas_call | solution.py:531
  24.1 3.4 %collective-permute-done.9 = bf16[2,128,512]{2,1,0:T(8,128)(2,1)S(1)} collective-permute-done((bf16[2,128,512]{2,1,0:T(8,128)(2,1)S(1)}, bf16[2,128,512]{2,1,0:T(8,128)(2,1)S(1)}, u32[]{:S(2)}, u32[]{:S(2)}) %collective-permute-start.9) | collective-permute-done | bytes 262176 | tf_op jit(solution)/shard_map/ppermute | solution.py:552
  27.6 1.2 %collective-permute-start.10 = (bf16[4,128,128]{2,1,0:T(8,128)(2,1)S(1)}, bf16[4,128,128]{2,1,0:T(8,128)(2,1)S(1)}, u32[]{:S(2)}, u32[]{:S(2)}) collective-permute-start(bf16[4,128,128]{2,1,0:T(8,128)(2,1)S(1)} %pad_maximum_fusion.2), channel_id=1, source_target_pairs={{0,1},{1,0},{2,3},{3,2},{4,5},{5,4},{6,7},{7,6},{8,9},{9,8},{10,11... | collective-permute-start | bytes 393224 | tf_op jit(solution)/shard_map/ppermute | solution.py:484
  28.8 0.2 collective-permute-start.11
  29.0 1.4 %collective-permute-start.8 = (bf16[1,128,512]{2,1,0:T(8,128)(2,1)S(1)}, bf16[1,128,512]{2,1,0:T(8,128)(2,1)S(1)}, u32[]{:S(2)}, u32[]{:S(2)}) collective-permute-start(bf16[1,128,512]{2,1,0:T(8,128)(2,1)S(1)} %slice.86), channel_id=1, source_target_pairs={{0,4},{4,8},{8,12},{12,14},{14,10},{10,6},{6,2},{2,0},{1,5},{5,9},... | collective-permute-start | bytes 393224 | tf_op jit(solution)/shard_map/ppermute | solution.py:562
  30.4 4.7 %second_stage.1 = (f32[2048,128]{1,0:T(8,128)S(1)}, bf16[2,576,128]{2,1,0:T(8,128)(2,1)S(1)}, bf16[2,576,128]{2,1,0:T(8,128)(2,1)S(1)}) custom-call(bf16[2,128,512]{2,1,0:T(8,128)(2,1)S(1)} %get-tuple-element.48.refs_0_, bf16[2,128,128]{2,1,0:T(8,128)(2,1)S(1)} %get-tuple-element.54.refs_1_, bf16[2,128,512]{2,1,0:T(8,128)(2,1)S(1)} %get-tuple-element.47.refs_2_, ...), custom_call_target="tpu_custom_call" | custom-call | flops 3000000000 | bytes 4194304 | tf_op jit(solution)/shard_map/second_stage/pallas_call | solution.py:531
  35.2 0.6 %collective-permute-start.12 = (bf16[2,128,128]{2,1,0:T(8,128)(2,1)S(1)}, bf16[2,128,128]{2,1,0:T(8,128)(2,1)S(1)}, u32[]{:S(2)}, u32[]{:S(2)}) collective-permute-start(bf16[2,128,128]{2,1,0:T(8,128)(2,1)S(1)} %slice_select_fusion), channel_id=1, source_target_pairs={{0,1},{1,0},{2,3},{3,2},{4,5},{5,4},{6,7},{7,6},{8,9},{9,8},{10,11... | collective-permute-start | bytes 196616 | tf_op jit(solution)/shard_map/ppermute | solution.py:484
  35.8 2.2 %third_stage.1.refs_10_ = f32[2176,128]{1,0:T(8,128)S(1)} custom-call(bf16[256,512]{1,0:T(8,128)(2,1)S(1)} %copy-done.4, bf16[64,256]{1,0:T(8,128)(2,1)S(1)} %copy-done.5, bf16[512,512]{1,0:T(8,128)(2,1)S(1)} %copy-done.3, s32[2,2,1,256]{3,2,1,0:T(1,128)S(1)} %copy-done.7, s32[2,2,8,128]{3,2,1,0:T(8,128)S(1)} %copy-done.6, f32[2,82,8,128]{3,2,1,0:T(8,128)S(1)} %copy-done.1, ...), custom_call_target="tpu_custom_call" | custom-call | flops 3000000000 | bytes 4194304 | tf_op jit(solution)/shard_map/third_stage/pallas_call | solution.py:531
  38.0 5.6 %last_stage.1 = f32[1,2,256,512]{3,2,1,0:T(8,128)} custom-call(bf16[2,128,512]{2,1,0:T(8,128)(2,1)S(1)} %constant_dynamic-update-slice_fusion.refs_0_, bf16[2,128,128]{2,1,0:T(8,128)(2,1)S(1)} %collective-permute-done.12.refs_1_, bf16[256,512]{1,0:T(8,128)(2,1)S(1)} %copy-done.4, bf16[64,256]{1,0:T(8,128)(2,1)S(1)} %copy-done.5, ...), custom_call_target="tpu_custom_call" | custom-call | flops 3000000000 | bytes 4194304 | tf_op jit(solution)/shard_map/last_stage/pallas_call | solution.py:531
  (42 shorter events, 0.4 us)
Async XLA Ops:
  0.0 8.4 %collective-permute-start.3 = (bf16[2,128,512]{2,1,0:T(8,128)(2,1)}, bf16[2,128,512]{2,1,0:T(8,128)(2,1)S(1)}, u32[]{:S(2)}, u32[]{:S(2)}) collective-permute-start(bf16[2,128,512]{2,1,0:T(8,128)(2,1)} %refs_4_.3), channel_id=1, source_target_pairs={{4,0},{8,4},{12,8},{14,12},{10,14},{6,10},{2,6},{0,2},{5,1},{9,5},... | collective-permute-start | bytes 786440 | tf_op jit(solution)/shard_map/ppermute | solution.py:547
  2.0 7.1 %collective-permute-start = (bf16[2,128,512]{2,1,0:T(8,128)(2,1)}, bf16[2,128,512]{2,1,0:T(8,128)(2,1)S(1)}, u32[]{:S(2)}, u32[]{:S(2)}) collective-permute-start(bf16[2,128,512]{2,1,0:T(8,128)(2,1)} %refs_4_.3), channel_id=1, source_target_pairs={{0,4},{4,8},{8,12},{12,14},{14,10},{10,6},{6,2},{2,0},{1,5},{5,9},... | collective-permute-start | bytes 786440 | tf_op jit(solution)/shard_map/ppermute | solution.py:547
  3.0 17.0 %collective-permute-start.7 = (bf16[2,128,128]{2,1,0:T(8,128)(2,1)S(1)}, bf16[2,128,128]{2,1,0:T(8,128)(2,1)S(1)}, u32[]{:S(2)}, u32[]{:S(2)}) collective-permute-start(bf16[2,128,128]{2,1,0:T(8,128)(2,1)S(1)} %slice_select_fusion.7), channel_id=1, source_target_pairs={{0,1},{1,0},{2,3},{3,2},{4,5},{5,4},{6,7},{7,6},{8,9},{9,8},{10,11... | collective-permute-start | bytes 196616 | tf_op jit(solution)/shard_map/ppermute | solution.py:484
  9.1 5.9 %collective-permute-start.1 = (bf16[2,128,512]{2,1,0:T(8,128)(2,1)S(1)}, bf16[2,128,512]{2,1,0:T(8,128)(2,1)S(1)}, u32[]{:S(2)}, u32[]{:S(2)}) collective-permute-start(bf16[2,128,512]{2,1,0:T(8,128)(2,1)S(1)} %collective-permute-done), channel_id=1, source_target_pairs={{0,4},{4,8},{8,12},{12,14},{14,10},{10,6},{6,2},{2,0},{1,5},{5,9},... | collective-permute-start | bytes 786440 | tf_op jit(solution)/shard_map/ppermute | solution.py:550
  9.6 6.0 %collective-permute-start.5 = (bf16[2,128,512]{2,1,0:T(8,128)(2,1)S(1)}, bf16[2,128,512]{2,1,0:T(8,128)(2,1)S(1)}, u32[]{:S(2)}, u32[]{:S(2)}) collective-permute-start(bf16[2,128,512]{2,1,0:T(8,128)(2,1)S(1)} %collective-permute-done.3), channel_id=1, source_target_pairs={{4,0},{8,4},{12,8},{14,12},{10,14},{6,10},{2,6},{0,2},{5,1},{9,5},... | collective-permute-start | bytes 786440 | tf_op jit(solution)/shard_map/ppermute | solution.py:550
  10.7 9.4 %copy-start = (bf16[2,128,512]{2,1,0:T(8,128)(2,1)S(1)}, bf16[2,128,512]{2,1,0:T(8,128)(2,1)}, u32[]{:S(2)}) copy-start(bf16[2,128,512]{2,1,0:T(8,128)(2,1)} %refs_4_.3) | copy-start | bytes 786436
  10.7 9.4 %copy-start.1 = (f32[2,82,8,128]{3,2,1,0:T(8,128)S(1)}, f32[2,82,8,128]{3,2,1,0:T(8,128)}, u32[]{:S(2)}) copy-start(f32[2,82,8,128]{3,2,1,0:T(8,128)} %get-tuple-element.33.refs_15_.refs_9_.refs_5_.refs_7_) | copy-start | bytes 2015236
  10.7 9.4 %copy-start.3 = (bf16[512,512]{1,0:T(8,128)(2,1)S(1)}, bf16[512,512]{1,0:T(8,128)(2,1)}, u32[]{:S(2)}) copy-start(bf16[512,512]{1,0:T(8,128)(2,1)} %get-tuple-element.30.refs_12_.refs_6_.refs_2_.refs_4_) | copy-start | bytes 1572868
  10.7 9.4 %copy-start.4 = (bf16[256,512]{1,0:T(8,128)(2,1)S(1)}, bf16[256,512]{1,0:T(8,128)(2,1)}, u32[]{:S(2)}) copy-start(bf16[256,512]{1,0:T(8,128)(2,1)} %get-tuple-element.26.refs_10_.refs_4_.refs_0_.refs_2_) | copy-start | bytes 786436
  10.7 9.4 %copy-start.5 = (bf16[64,256]{1,0:T(8,128)(2,1)S(1)}, bf16[64,256]{1,0:T(8,128)(2,1)}, u32[]{:S(2)}) copy-start(bf16[64,256]{1,0:T(8,128)(2,1)} %get-tuple-element.29.refs_11_.refs_5_.refs_1_.refs_3_) | copy-start | bytes 98308
  10.7 9.4 %copy-start.6 = (s32[2,2,8,128]{3,2,1,0:T(8,128)S(1)}, s32[2,2,8,128]{3,2,1,0:T(8,128)}, u32[]{:S(2)}) copy-start(s32[2,2,8,128]{3,2,1,0:T(8,128)} %get-tuple-element.32.refs_14_.refs_8_.refs_4_.refs_6_) | copy-start | bytes 49156
  10.8 9.4 %copy-start.7 = (s32[2,2,1,256]{3,2,1,0:T(1,128)S(1)}, s32[2,2,1,256]{3,2,1,0:T(1,128)}, u32[]{:S(2)}) copy-start(s32[2,2,1,256]{3,2,1,0:T(1,128)} %get-tuple-element.31.refs_13_.refs_7_.refs_3_.refs_5_) | copy-start | bytes 12292
  10.8 7.7 %collective-permute-start.4 = (bf16[4,128,128]{2,1,0:T(8,128)(2,1)S(1)}, bf16[4,128,128]{2,1,0:T(8,128)(2,1)S(1)}, u32[]{:S(2)}, u32[]{:S(2)}) collective-permute-start(bf16[4,128,128]{2,1,0:T(8,128)(2,1)S(1)} %pad_maximum_fusion), channel_id=1, source_target_pairs={{0,1},{1,0},{2,3},{3,2},{4,5},{5,4},{6,7},{7,6},{8,9},{9,8},{10,11... | collective-permute-start | bytes 393224 | tf_op jit(solution)/shard_map/ppermute | solution.py:484
  15.8 4.3 %collective-permute-start.6 = (bf16[4,128,128]{2,1,0:T(8,128)(2,1)S(1)}, bf16[4,128,128]{2,1,0:T(8,128)(2,1)S(1)}, u32[]{:S(2)}, u32[]{:S(2)}) collective-permute-start(bf16[4,128,128]{2,1,0:T(8,128)(2,1)S(1)} %pad_maximum_fusion.1), channel_id=1, source_target_pairs={{0,1},{1,0},{2,3},{3,2},{4,5},{5,4},{6,7},{7,6},{8,9},{9,8},{10,11... | collective-permute-start | bytes 393224 | tf_op jit(solution)/shard_map/ppermute | solution.py:484
  18.5 8.9 %collective-permute-start.2 = (bf16[2,128,512]{2,1,0:T(8,128)(2,1)S(1)}, bf16[2,128,512]{2,1,0:T(8,128)(2,1)S(1)}, u32[]{:S(2)}, u32[]{:S(2)}) collective-permute-start(bf16[2,128,512]{2,1,0:T(8,128)(2,1)S(1)} %collective-permute-done.1), channel_id=1, source_target_pairs={{0,4},{4,8},{8,12},{12,14},{14,10},{10,6},{6,2},{2,0},{1,5},{5,9},... | collective-permute-start | bytes 786440 | tf_op jit(solution)/shard_map/ppermute | solution.py:552
  19.9 7.6 %collective-permute-start.9 = (bf16[2,128,512]{2,1,0:T(8,128)(2,1)S(1)}, bf16[2,128,512]{2,1,0:T(8,128)(2,1)S(1)}, u32[]{:S(2)}, u32[]{:S(2)}) collective-permute-start(bf16[2,128,512]{2,1,0:T(8,128)(2,1)S(1)} %collective-permute-done.5), channel_id=1, source_target_pairs={{4,0},{8,4},{12,8},{14,12},{10,14},{6,10},{2,6},{0,2},{5,1},{9,5},... | collective-permute-start | bytes 786440 | tf_op jit(solution)/shard_map/ppermute | solution.py:552
  27.5 3.0 %copy-start.2 = (f32[2,80,8,128]{3,2,1,0:T(8,128)S(1)}, f32[2,80,8,128]{3,2,1,0:T(8,128)}, u32[]{:S(2)}) copy-start(f32[2,80,8,128]{3,2,1,0:T(8,128)} %get-tuple-element.37.refs_10_.refs_8_) | copy-start | bytes 1966084
  27.6 2.8 %collective-permute-start.10 = (bf16[4,128,128]{2,1,0:T(8,128)(2,1)S(1)}, bf16[4,128,128]{2,1,0:T(8,128)(2,1)S(1)}, u32[]{:S(2)}, u32[]{:S(2)}) collective-permute-start(bf16[4,128,128]{2,1,0:T(8,128)(2,1)S(1)} %pad_maximum_fusion.2), channel_id=1, source_target_pairs={{0,1},{1,0},{2,3},{3,2},{4,5},{5,4},{6,7},{7,6},{8,9},{9,8},{10,11... | collective-permute-start | bytes 393224 | tf_op jit(solution)/shard_map/ppermute | solution.py:484
  28.8 6.3 %collective-permute-start.11 = (bf16[1,128,512]{2,1,0:T(8,128)(2,1)S(1)}, bf16[1,128,512]{2,1,0:T(8,128)(2,1)S(1)}, u32[]{:S(2)}, u32[]{:S(2)}) collective-permute-start(bf16[1,128,512]{2,1,0:T(8,128)(2,1)S(1)} %slice.93), channel_id=1, source_target_pairs={{4,0},{8,4},{12,8},{14,12},{10,14},{6,10},{2,6},{0,2},{5,1},{9,5},... | collective-permute-start | bytes 393224 | tf_op jit(solution)/shard_map/ppermute | solution.py:562
  29.0 6.1 %collective-permute-start.8 = (bf16[1,128,512]{2,1,0:T(8,128)(2,1)S(1)}, bf16[1,128,512]{2,1,0:T(8,128)(2,1)S(1)}, u32[]{:S(2)}, u32[]{:S(2)}) collective-permute-start(bf16[1,128,512]{2,1,0:T(8,128)(2,1)S(1)} %slice.86), channel_id=1, source_target_pairs={{0,4},{4,8},{8,12},{12,14},{14,10},{10,6},{6,2},{2,0},{1,5},{5,9},... | collective-permute-start | bytes 393224 | tf_op jit(solution)/shard_map/ppermute | solution.py:562
  35.2 2.8 %collective-permute-start.12 = (bf16[2,128,128]{2,1,0:T(8,128)(2,1)S(1)}, bf16[2,128,128]{2,1,0:T(8,128)(2,1)S(1)}, u32[]{:S(2)}, u32[]{:S(2)}) collective-permute-start(bf16[2,128,128]{2,1,0:T(8,128)(2,1)S(1)} %slice_select_fusion), channel_id=1, source_target_pairs={{0,1},{1,0},{2,3},{3,2},{4,5},{5,4},{6,7},{7,6},{8,9},{9,8},{10,11... | collective-permute-start | bytes 196616 | tf_op jit(solution)/shard_map/ppermute | solution.py:484

commit v6 on v5

--- a/solution.py
+++ b/solution.py
@@ -247,23 +247,22 @@
     return x[0] * y[0] - x[1] * y[1], x[0] * y[1] + x[1] * y[0]
 
 
-def squeeze(piece, rim, core, near_mat, edge_mat, c_ref):
-    bins = piece.shape[-1]
+def squeeze(pieces, core, near_mat, edge_mat, c_refs):
+    pulses, bins = pieces[0].shape[1:]
 
     def columns(low, high):
         found = []
         for ri in (0, 1):
-            tiles = []
             for tile in range(low, high):
-                if tile == 0:
-                    other = rim[ri]
-                    tiles.append(jnp.where(core == 1, other, jnp.zeros_like(other)))
-                elif tile == bins // LANES + 1:
-                    other = rim[ri]
-                    tiles.append(jnp.where(core == 0, other, jnp.zeros_like(other)))
-                else:
-                    tiles.append(piece[ri, :, (tile - 1) * LANES : tile * LANES])
-            found += tiles
+                parts = []
+                for piece, rim in zip(pieces[::2], pieces[1::2]):
+                    if tile in (0, bins // LANES + 1):
+                        other = rim[ri]
+                        here = core == (1 if tile == 0 else 0)
+                        parts.append(jnp.where(here, other, jnp.zeros_like(other)))
+                    else:
+                        parts.append(piece[ri, :, (tile - 1) * LANES : tile * LANES])
+                found.append(jnp.concatenate(parts, axis=0))
         return jnp.concatenate(found, axis=1)
 
     def times(matrix, cols):
@@ -283,8 +282,9 @@
         else:
             result = times(edge_mat[...], columns(block, block + 1)).astype(jnp.bfloat16)
             place, count = SPAN + bins, SPAN
-        c_ref[0, place : place + count] = result[:count]
-        c_ref[1, place : place + count] = result[count:]
+        for i, c_ref in enumerate(c_refs):
+            c_ref[0, place : place + count] = result[:count, i * pulses : (i + 1) * pulses]
+            c_ref[1, place : place + count] = result[count:, i * pulses : (i + 1) * pulses]
 
 
 def form(halves, steer, x_ref):
@@ -424,8 +424,9 @@
     pieces, shared, table0, refs = refs[:10], refs[10:15], refs[15], refs[16:]
     part, c_own, c_next, c_early, c_a, c_b, x0_ref, *rooms = refs
     core = lax.axis_index("range")
-    for i, c_ref in enumerate((c_a, c_b, c_own, c_next, c_early)):
-        squeeze(pieces[2 * i], pieces[2 * i + 1], core, shared[0], shared[1], c_ref)
+    squeeze(pieces[:4], core, shared[0], shared[1], (c_a, c_b))
+    squeeze(pieces[4:8], core, shared[0], shared[1], (c_own, c_next))
+    squeeze(pieces[8:], core, shared[0], shared[1], (c_early,))
     half0 = part.shape[0] // (SUBS)
     merge_low((c_a, c_b), 1, shared, table0, x0_ref, rooms, None, part, half0)
 
@@ -435,8 +436,7 @@
     table1, part, c_own, c_early = refs[:4]
     near, c_b, c_late, x0_ref, o_ref, x1_ref, *rooms = refs[4:]
     core = lax.axis_index("range")
-    for i, c_ref in enumerate((c_late, c_b)):
-        squeeze(pieces[2 * i], pieces[2 * i + 1], core, shared[0], shared[1], c_ref)
+    squeeze(pieces, core, shared[0], shared[1], (c_late, c_b))
     half0, half1 = o_ref.shape[0] // SUBS, near.shape[0] // SUBS
     second = (outer(), c_early, c_late)
     merge_low((c_own, second), 0, shared, table0, x0_ref, rooms, part, o_ref, half0)
@@ -455,7 +455,7 @@
     table1, near, other, c_early, c_late = refs[:5]
     out_ref, c_a, x0_ref, o_ref, x1_ref, final, image, sems, *rooms = refs[5:]
     core = lax.axis_index("range")
-    squeeze(pieces[0], pieces[1], core, shared[0], shared[1], c_a)
+    squeeze(pieces, core, shared[0], shared[1], (c_a,))
     half0, half1 = o_ref.shape[0] // SUBS, final.shape[0] // SUBS
     first = (outer(), c_late, c_early)
     merge_low((first, c_a), 1, shared, table0, x0_ref, rooms, other, o_ref, half0)

time: 43.9 us -> 43.7 us (level)
  Pallas kernels: 20.2 us -> 19.4 us
  waiting for transfers between devices: 7.09 us -> 7.68 us
    pallas_call x4, Pallas kernels: 16.4 us -> 15.6 us  [run(): pl.pallas_call(functools.partial(kernel, total), out_shape=[jax.ShapeDtyp...]
    ppermute x1, waiting for transfers between devices: 3.35 us -> 3.94 us  [ring_of_chips(): lax.ppermute(down2, axes, behind)]
  transfers between devices with their start and end apart: 13 -> 13, of which waited for: 5 -> 5; matrix products, arithmetic and copies ran while one was open for 3% -> 3% of each run, Pallas kernels for 33% -> 32%
where the time goes in v6:
time: 43.7 us; the launch traced here: 43.5 us
  Pallas kernels  19.4 us (44%)
  starting transfers between devices  14.7 us (34%)
  waiting for transfers between devices  7.68 us (18%)
  other arithmetic  1.19 us (3%)
  between operations  0.46 us (1%)
    pallas_call x4, Pallas kernels, run(): pl.pallas_call(functools.partial(kernel, total), out_shape=[jax.ShapeDtyp...  15.6 us
    ppermute x5, starting transfers between devices, pairs(): lax.ppermute(jnp.concatenate(rims, axis=0), 'range', [(0, 1), (1, 0)])  8.01 us
    ppermute x1, waiting for transfers between devices, ring_of_chips(): lax.ppermute(down2, axes, behind)  3.94 us
    pallas_call x1, Pallas kernels, ring_of_chips(): pl.pallas_call(functools.partial(table_kernel, total=total), out_shape=[j...  3.73 us
    ppermute x1, starting transfers between devices, ring_of_chips(): lax.ppermute(echoes, axes, behind)  2.04 us
    ppermute x1, waiting for transfers between devices, ring_of_chips(): lax.ppermute(up1, axes, ahead)  1.79 us
    ppermute x1, starting transfers between devices, ring_of_chips(): lax.ppermute(up3[:1], axes, ahead)  1.37 us
    ppermute x1, starting transfers between devices, ring_of_chips(): lax.ppermute(up2, axes, ahead)  1.35 us
  transfers between devices with their start and end apart: 13, of which 5 were waited for; matrix products, arithmetic and copies ran while one was open for 3% of the time, Pallas kernels for 32%

profile of v6, /device:TPU:1, one launch (start us, length us, event | category | flops | bytes accessed | tf_op | source)
XLA Modules:
  0.0 43.5 jit_solution(6438854280326159343)
XLA Ops:
  0.0 2.0 %collective-permute-start.3 = (bf16[2,128,512]{2,1,0:T(8,128)(2,1)}, bf16[2,128,512]{2,1,0:T(8,128)(2,1)S(1)}, u32[]{:S(2)}, u32[]{:S(2)}) collective-permute-start(bf16[2,128,512]{2,1,0:T(8,128)(2,1)} %refs_4_.3), channel_id=1, source_target_pairs={{4,0},{8,4},{12,8},{14,12},{10,14},{6,10},{2,6},{0,2},{5,1},{9,5},... | collective-permute-start | bytes 786440 | tf_op jit(solution)/shard_map/ppermute | solution.py:547
  2.0 0.1 collective-permute-start
  2.1 0.9 %slice_select_fusion.7 = bf16[2,128,128]{2,1,0:T(8,128)(2,1)S(1)} fusion(bf16[2,128,512]{2,1,0:T(8,128)(2,1)} %refs_4_.3, pred[]{:T(512)S(6)} %eq.14), kind=kLoop, calls=%fused_computation.22 | loop fusion | flops 32768 | bytes 196609 | tf_op jit(solution)/shard_map/jit(_where)/select_n | solution.py:483
  3.0 1.0 %collective-permute-start.7 = (bf16[2,128,128]{2,1,0:T(8,128)(2,1)S(1)}, bf16[2,128,128]{2,1,0:T(8,128)(2,1)S(1)}, u32[]{:S(2)}, u32[]{:S(2)}) collective-permute-start(bf16[2,128,128]{2,1,0:T(8,128)(2,1)S(1)} %slice_select_fusion.7), channel_id=1, source_target_pairs={{0,1},{1,0},{2,3},{3,2},{4,5},{5,4},{6,7},{7,6},{8,9},{9,8},{10,11... | collective-permute-start | bytes 196616 | tf_op jit(solution)/shard_map/ppermute | solution.py:484
  4.0 3.7 %tables.1 = (bf16[256,512]{1,0:T(8,128)(2,1)}, bf16[64,256]{1,0:T(8,128)(2,1)}, bf16[512,512]{1,0:T(8,128)(2,1)}, s32[2,2,1,256]{3,2,1,0:T(1,128)}, s32[2,2,8,12...) custom-call(bf16[2,64]{1,0:T(2,128)(2,1)} %refs_0_.1, f32[256,256]{1,0:T(8,128)} %refs_1_.1, ...), custom_call_target="tpu_custom_call" | custom-call | flops 1000000000 | bytes 4194304 | tf_op jit(solution)/shard_map/tables/pallas_call | solution.py:499
  7.8 0.6 %collective-permute-done.3 = bf16[2,128,512]{2,1,0:T(8,128)(2,1)S(1)} collective-permute-done((bf16[2,128,512]{2,1,0:T(8,128)(2,1)}, bf16[2,128,512]{2,1,0:T(8,128)(2,1)S(1)}, u32[]{:S(2)}, u32[]{:S(2)}) %collective-permute-start.3) | collective-permute-done | bytes 262176 | tf_op jit(solution)/shard_map/ppermute | solution.py:547
  8.4 0.7 %collective-permute-done = bf16[2,128,512]{2,1,0:T(8,128)(2,1)S(1)} collective-permute-done((bf16[2,128,512]{2,1,0:T(8,128)(2,1)}, bf16[2,128,512]{2,1,0:T(8,128)(2,1)S(1)}, u32[]{:S(2)}, u32[]{:S(2)}) %collective-permute-start) | collective-permute-done | bytes 262176 | tf_op jit(solution)/shard_map/ppermute | solution.py:547
  9.1 0.5 %collective-permute-start.1 = (bf16[2,128,512]{2,1,0:T(8,128)(2,1)S(1)}, bf16[2,128,512]{2,1,0:T(8,128)(2,1)S(1)}, u32[]{:S(2)}, u32[]{:S(2)}) collective-permute-start(bf16[2,128,512]{2,1,0:T(8,128)(2,1)S(1)} %collective-permute-done), channel_id=1, source_target_pairs={{0,4},{4,8},{8,12},{12,14},{14,10},{10,6},{6,2},{2,0},{1,5},{5,9},... | collective-permute-start | bytes 786440 | tf_op jit(solution)/shard_map/ppermute | solution.py:550
  9.6 1.0 %collective-permute-start.5 = (bf16[2,128,512]{2,1,0:T(8,128)(2,1)S(1)}, bf16[2,128,512]{2,1,0:T(8,128)(2,1)S(1)}, u32[]{:S(2)}, u32[]{:S(2)}) collective-permute-start(bf16[2,128,512]{2,1,0:T(8,128)(2,1)S(1)} %collective-permute-done.3), channel_id=1, source_target_pairs={{4,0},{8,4},{12,8},{14,12},{10,14},{6,10},{2,6},{0,2},{5,1},{9,5},... | collective-permute-start | bytes 786440 | tf_op jit(solution)/shard_map/ppermute | solution.py:550
  10.8 2.5 %collective-permute-start.4 = (bf16[4,128,128]{2,1,0:T(8,128)(2,1)S(1)}, bf16[4,128,128]{2,1,0:T(8,128)(2,1)S(1)}, u32[]{:S(2)}, u32[]{:S(2)}) collective-permute-start(bf16[4,128,128]{2,1,0:T(8,128)(2,1)S(1)} %pad_maximum_fusion), channel_id=1, source_target_pairs={{0,1},{1,0},{2,3},{3,2},{4,5},{5,4},{6,7},{7,6},{8,9},{9,8},{10,11... | collective-permute-start | bytes 393224 | tf_op jit(solution)/shard_map/ppermute | solution.py:484
  13.3 1.8 %collective-permute-done.1 = bf16[2,128,512]{2,1,0:T(8,128)(2,1)S(1)} collective-permute-done((bf16[2,128,512]{2,1,0:T(8,128)(2,1)S(1)}, bf16[2,128,512]{2,1,0:T(8,128)(2,1)S(1)}, u32[]{:S(2)}, u32[]{:S(2)}) %collective-permute-start.1) | collective-permute-done | bytes 262176 | tf_op jit(solution)/shard_map/ppermute | solution.py:550
  15.0 0.6 %collective-permute-done.5 = bf16[2,128,512]{2,1,0:T(8,128)(2,1)S(1)} collective-permute-done((bf16[2,128,512]{2,1,0:T(8,128)(2,1)S(1)}, bf16[2,128,512]{2,1,0:T(8,128)(2,1)S(1)}, u32[]{:S(2)}, u32[]{:S(2)}) %collective-permute-start.5) | collective-permute-done | bytes 262176 | tf_op jit(solution)/shard_map/ppermute | solution.py:550
  15.8 2.7 %collective-permute-start.6 = (bf16[4,128,128]{2,1,0:T(8,128)(2,1)S(1)}, bf16[4,128,128]{2,1,0:T(8,128)(2,1)S(1)}, u32[]{:S(2)}, u32[]{:S(2)}) collective-permute-start(bf16[4,128,128]{2,1,0:T(8,128)(2,1)S(1)} %pad_maximum_fusion.1), channel_id=1, source_target_pairs={{0,1},{1,0},{2,3},{3,2},{4,5},{5,4},{6,7},{7,6},{8,9},{9,8},{10,11... | collective-permute-start | bytes 393224 | tf_op jit(solution)/shard_map/ppermute | solution.py:484
  18.5 1.3 %collective-permute-start.2 = (bf16[2,128,512]{2,1,0:T(8,128)(2,1)S(1)}, bf16[2,128,512]{2,1,0:T(8,128)(2,1)S(1)}, u32[]{:S(2)}, u32[]{:S(2)}) collective-permute-start(bf16[2,128,512]{2,1,0:T(8,128)(2,1)S(1)} %collective-permute-done.1), channel_id=1, source_target_pairs={{0,4},{4,8},{8,12},{12,14},{14,10},{10,6},{6,2},{2,0},{1,5},{5,9},... | collective-permute-start | bytes 786440 | tf_op jit(solution)/shard_map/ppermute | solution.py:552
  19.9 0.2 collective-permute-start.9
  20.1 3.4 %first_stage.1 = (f32[2176,128]{1,0:T(8,128)S(1)}, bf16[2,576,128]{2,1,0:T(8,128)(2,1)S(1)}, bf16[2,576,128]{2,1,0:T(8,128)(2,1)S(1)}, bf16[2,576,128]{2,1,0:T(8,128)(2,1)S(1)}) custom-call(bf16[2,128,512]{2,1,0:T(8,128)(2,1)S(1)} %get-tuple-element.52.refs_0_, bf16[2,128,128]{2,1,0:T(8,128)(2,1)S(1)} %get-tuple-element.56.refs_1_, ...), custom_call_target="tpu_custom_call" | custom-call | flops 3000000000 | bytes 4194304 | tf_op jit(solution)/shard_map/first_stage/pallas_call | solution.py:531
  23.5 3.9 %collective-permute-done.9 = bf16[2,128,512]{2,1,0:T(8,128)(2,1)S(1)} collective-permute-done((bf16[2,128,512]{2,1,0:T(8,128)(2,1)S(1)}, bf16[2,128,512]{2,1,0:T(8,128)(2,1)S(1)}, u32[]{:S(2)}, u32[]{:S(2)}) %collective-permute-start.9) | collective-permute-done | bytes 262176 | tf_op jit(solution)/shard_map/ppermute | solution.py:552
  27.6 1.2 %collective-permute-start.10 = (bf16[4,128,128]{2,1,0:T(8,128)(2,1)S(1)}, bf16[4,128,128]{2,1,0:T(8,128)(2,1)S(1)}, u32[]{:S(2)}, u32[]{:S(2)}) collective-permute-start(bf16[4,128,128]{2,1,0:T(8,128)(2,1)S(1)} %pad_maximum_fusion.2), channel_id=1, source_target_pairs={{0,1},{1,0},{2,3},{3,2},{4,5},{5,4},{6,7},{7,6},{8,9},{9,8},{10,11... | collective-permute-start | bytes 393224 | tf_op jit(solution)/shard_map/ppermute | solution.py:484
  28.8 0.2 collective-permute-start.11
  29.0 1.4 %collective-permute-start.8 = (bf16[1,128,512]{2,1,0:T(8,128)(2,1)S(1)}, bf16[1,128,512]{2,1,0:T(8,128)(2,1)S(1)}, u32[]{:S(2)}, u32[]{:S(2)}) collective-permute-start(bf16[1,128,512]{2,1,0:T(8,128)(2,1)S(1)} %slice.86), channel_id=1, source_target_pairs={{0,4},{4,8},{8,12},{12,14},{14,10},{10,6},{6,2},{2,0},{1,5},{5,9},... | collective-permute-start | bytes 393224 | tf_op jit(solution)/shard_map/ppermute | solution.py:562
  30.4 4.4 %second_stage.1 = (f32[2048,128]{1,0:T(8,128)S(1)}, bf16[2,576,128]{2,1,0:T(8,128)(2,1)S(1)}, bf16[2,576,128]{2,1,0:T(8,128)(2,1)S(1)}) custom-call(bf16[2,128,512]{2,1,0:T(8,128)(2,1)S(1)} %get-tuple-element.48.refs_0_, bf16[2,128,128]{2,1,0:T(8,128)(2,1)S(1)} %get-tuple-element.54.refs_1_, bf16[2,128,512]{2,1,0:T(8,128)(2,1)S(1)} %get-tuple-element.47.refs_2_, ...), custom_call_target="tpu_custom_call" | custom-call | flops 3000000000 | bytes 4194304 | tf_op jit(solution)/shard_map/second_stage/pallas_call | solution.py:531
  35.0 0.6 %collective-permute-start.12 = (bf16[2,128,128]{2,1,0:T(8,128)(2,1)S(1)}, bf16[2,128,128]{2,1,0:T(8,128)(2,1)S(1)}, u32[]{:S(2)}, u32[]{:S(2)}) collective-permute-start(bf16[2,128,128]{2,1,0:T(8,128)(2,1)S(1)} %slice_select_fusion), channel_id=1, source_target_pairs={{0,1},{1,0},{2,3},{3,2},{4,5},{5,4},{6,7},{7,6},{8,9},{9,8},{10,11... | collective-permute-start | bytes 196616 | tf_op jit(solution)/shard_map/ppermute | solution.py:484
  35.5 2.2 %third_stage.1.refs_10_ = f32[2176,128]{1,0:T(8,128)S(1)} custom-call(bf16[256,512]{1,0:T(8,128)(2,1)S(1)} %copy-done.4, bf16[64,256]{1,0:T(8,128)(2,1)S(1)} %copy-done.5, bf16[512,512]{1,0:T(8,128)(2,1)S(1)} %copy-done.3, s32[2,2,1,256]{3,2,1,0:T(1,128)S(1)} %copy-done.7, s32[2,2,8,128]{3,2,1,0:T(8,128)S(1)} %copy-done.6, f32[2,82,8,128]{3,2,1,0:T(8,128)S(1)} %copy-done.1, ...), custom_call_target="tpu_custom_call" | custom-call | flops 3000000000 | bytes 4194304 | tf_op jit(solution)/shard_map/third_stage/pallas_call | solution.py:531
  37.8 5.6 %last_stage.1 = f32[1,2,256,512]{3,2,1,0:T(8,128)} custom-call(bf16[2,128,512]{2,1,0:T(8,128)(2,1)S(1)} %constant_dynamic-update-slice_fusion.refs_0_, bf16[2,128,128]{2,1,0:T(8,128)(2,1)S(1)} %collective-permute-done.12.refs_1_, bf16[256,512]{1,0:T(8,128)(2,1)S(1)} %copy-done.4, bf16[64,256]{1,0:T(8,128)(2,1)S(1)} %copy-done.5, ...), custom_call_target="tpu_custom_call" | custom-call | flops 3000000000 | bytes 4194304 | tf_op jit(solution)/shard_map/last_stage/pallas_call | solution.py:531
  (42 shorter events, 0.4 us)
Async XLA Ops:
  0.0 8.4 %collective-permute-start.3 = (bf16[2,128,512]{2,1,0:T(8,128)(2,1)}, bf16[2,128,512]{2,1,0:T(8,128)(2,1)S(1)}, u32[]{:S(2)}, u32[]{:S(2)}) collective-permute-start(bf16[2,128,512]{2,1,0:T(8,128)(2,1)} %refs_4_.3), channel_id=1, source_target_pairs={{4,0},{8,4},{12,8},{14,12},{10,14},{6,10},{2,6},{0,2},{5,1},{9,5},... | collective-permute-start | bytes 786440 | tf_op jit(solution)/shard_map/ppermute | solution.py:547
  2.0 7.1 %collective-permute-start = (bf16[2,128,512]{2,1,0:T(8,128)(2,1)}, bf16[2,128,512]{2,1,0:T(8,128)(2,1)S(1)}, u32[]{:S(2)}, u32[]{:S(2)}) collective-permute-start(bf16[2,128,512]{2,1,0:T(8,128)(2,1)} %refs_4_.3), channel_id=1, source_target_pairs={{0,4},{4,8},{8,12},{12,14},{14,10},{10,6},{6,2},{2,0},{1,5},{5,9},... | collective-permute-start | bytes 786440 | tf_op jit(solution)/shard_map/ppermute | solution.py:547
  3.0 17.0 %collective-permute-start.7 = (bf16[2,128,128]{2,1,0:T(8,128)(2,1)S(1)}, bf16[2,128,128]{2,1,0:T(8,128)(2,1)S(1)}, u32[]{:S(2)}, u32[]{:S(2)}) collective-permute-start(bf16[2,128,128]{2,1,0:T(8,128)(2,1)S(1)} %slice_select_fusion.7), channel_id=1, source_target_pairs={{0,1},{1,0},{2,3},{3,2},{4,5},{5,4},{6,7},{7,6},{8,9},{9,8},{10,11... | collective-permute-start | bytes 196616 | tf_op jit(solution)/shard_map/ppermute | solution.py:484
  9.1 5.9 %collective-permute-start.1 = (bf16[2,128,512]{2,1,0:T(8,128)(2,1)S(1)}, bf16[2,128,512]{2,1,0:T(8,128)(2,1)S(1)}, u32[]{:S(2)}, u32[]{:S(2)}) collective-permute-start(bf16[2,128,512]{2,1,0:T(8,128)(2,1)S(1)} %collective-permute-done), channel_id=1, source_target_pairs={{0,4},{4,8},{8,12},{12,14},{14,10},{10,6},{6,2},{2,0},{1,5},{5,9},... | collective-permute-start | bytes 786440 | tf_op jit(solution)/shard_map/ppermute | solution.py:550
  9.6 6.0 %collective-permute-start.5 = (bf16[2,128,512]{2,1,0:T(8,128)(2,1)S(1)}, bf16[2,128,512]{2,1,0:T(8,128)(2,1)S(1)}, u32[]{:S(2)}, u32[]{:S(2)}) collective-permute-start(bf16[2,128,512]{2,1,0:T(8,128)(2,1)S(1)} %collective-permute-done.3), channel_id=1, source_target_pairs={{4,0},{8,4},{12,8},{14,12},{10,14},{6,10},{2,6},{0,2},{5,1},{9,5},... | collective-permute-start | bytes 786440 | tf_op jit(solution)/shard_map/ppermute | solution.py:550
  10.7 9.4 %copy-start = (bf16[2,128,512]{2,1,0:T(8,128)(2,1)S(1)}, bf16[2,128,512]{2,1,0:T(8,128)(2,1)}, u32[]{:S(2)}) copy-start(bf16[2,128,512]{2,1,0:T(8,128)(2,1)} %refs_4_.3) | copy-start | bytes 786436
  10.7 9.4 %copy-start.1 = (f32[2,82,8,128]{3,2,1,0:T(8,128)S(1)}, f32[2,82,8,128]{3,2,1,0:T(8,128)}, u32[]{:S(2)}) copy-start(f32[2,82,8,128]{3,2,1,0:T(8,128)} %get-tuple-element.33.refs_15_.refs_9_.refs_5_.refs_7_) | copy-start | bytes 2015236
  10.7 9.4 %copy-start.3 = (bf16[512,512]{1,0:T(8,128)(2,1)S(1)}, bf16[512,512]{1,0:T(8,128)(2,1)}, u32[]{:S(2)}) copy-start(bf16[512,512]{1,0:T(8,128)(2,1)} %get-tuple-element.30.refs_12_.refs_6_.refs_2_.refs_4_) | copy-start | bytes 1572868
  10.7 9.4 %copy-start.4 = (bf16[256,512]{1,0:T(8,128)(2,1)S(1)}, bf16[256,512]{1,0:T(8,128)(2,1)}, u32[]{:S(2)}) copy-start(bf16[256,512]{1,0:T(8,128)(2,1)} %get-tuple-element.26.refs_10_.refs_4_.refs_0_.refs_2_) | copy-start | bytes 786436
  10.7 9.4 %copy-start.5 = (bf16[64,256]{1,0:T(8,128)(2,1)S(1)}, bf16[64,256]{1,0:T(8,128)(2,1)}, u32[]{:S(2)}) copy-start(bf16[64,256]{1,0:T(8,128)(2,1)} %get-tuple-element.29.refs_11_.refs_5_.refs_1_.refs_3_) | copy-start | bytes 98308
  10.7 9.4 %copy-start.6 = (s32[2,2,8,128]{3,2,1,0:T(8,128)S(1)}, s32[2,2,8,128]{3,2,1,0:T(8,128)}, u32[]{:S(2)}) copy-start(s32[2,2,8,128]{3,2,1,0:T(8,128)} %get-tuple-element.32.refs_14_.refs_8_.refs_4_.refs_6_) | copy-start | bytes 49156
  10.8 9.4 %copy-start.7 = (s32[2,2,1,256]{3,2,1,0:T(1,128)S(1)}, s32[2,2,1,256]{3,2,1,0:T(1,128)}, u32[]{:S(2)}) copy-start(s32[2,2,1,256]{3,2,1,0:T(1,128)} %get-tuple-element.31.refs_13_.refs_7_.refs_3_.refs_5_) | copy-start | bytes 12292
  10.8 7.7 %collective-permute-start.4 = (bf16[4,128,128]{2,1,0:T(8,128)(2,1)S(1)}, bf16[4,128,128]{2,1,0:T(8,128)(2,1)S(1)}, u32[]{:S(2)}, u32[]{:S(2)}) collective-permute-start(bf16[4,128,128]{2,1,0:T(8,128)(2,1)S(1)} %pad_maximum_fusion), channel_id=1, source_target_pairs={{0,1},{1,0},{2,3},{3,2},{4,5},{5,4},{6,7},{7,6},{8,9},{9,8},{10,11... | collective-permute-start | bytes 393224 | tf_op jit(solution)/shard_map/ppermute | solution.py:484
  15.8 4.3 %collective-permute-start.6 = (bf16[4,128,128]{2,1,0:T(8,128)(2,1)S(1)}, bf16[4,128,128]{2,1,0:T(8,128)(2,1)S(1)}, u32[]{:S(2)}, u32[]{:S(2)}) collective-permute-start(bf16[4,128,128]{2,1,0:T(8,128)(2,1)S(1)} %pad_maximum_fusion.1), channel_id=1, source_target_pairs={{0,1},{1,0},{2,3},{3,2},{4,5},{5,4},{6,7},{7,6},{8,9},{9,8},{10,11... | collective-permute-start | bytes 393224 | tf_op jit(solution)/shard_map/ppermute | solution.py:484
  18.5 8.9 %collective-permute-start.2 = (bf16[2,128,512]{2,1,0:T(8,128)(2,1)S(1)}, bf16[2,128,512]{2,1,0:T(8,128)(2,1)S(1)}, u32[]{:S(2)}, u32[]{:S(2)}) collective-permute-start(bf16[2,128,512]{2,1,0:T(8,128)(2,1)S(1)} %collective-permute-done.1), channel_id=1, source_target_pairs={{0,4},{4,8},{8,12},{12,14},{14,10},{10,6},{6,2},{2,0},{1,5},{5,9},... | collective-permute-start | bytes 786440 | tf_op jit(solution)/shard_map/ppermute | solution.py:552
  19.9 7.6 %collective-permute-start.9 = (bf16[2,128,512]{2,1,0:T(8,128)(2,1)S(1)}, bf16[2,128,512]{2,1,0:T(8,128)(2,1)S(1)}, u32[]{:S(2)}, u32[]{:S(2)}) collective-permute-start(bf16[2,128,512]{2,1,0:T(8,128)(2,1)S(1)} %collective-permute-done.5), channel_id=1, source_target_pairs={{4,0},{8,4},{12,8},{14,12},{10,14},{6,10},{2,6},{0,2},{5,1},{9,5},... | collective-permute-start | bytes 786440 | tf_op jit(solution)/shard_map/ppermute | solution.py:552
  27.5 3.0 %copy-start.2 = (f32[2,80,8,128]{3,2,1,0:T(8,128)S(1)}, f32[2,80,8,128]{3,2,1,0:T(8,128)}, u32[]{:S(2)}) copy-start(f32[2,80,8,128]{3,2,1,0:T(8,128)} %get-tuple-element.37.refs_10_.refs_8_) | copy-start | bytes 1966084
  27.6 2.8 %collective-permute-start.10 = (bf16[4,128,128]{2,1,0:T(8,128)(2,1)S(1)}, bf16[4,128,128]{2,1,0:T(8,128)(2,1)S(1)}, u32[]{:S(2)}, u32[]{:S(2)}) collective-permute-start(bf16[4,128,128]{2,1,0:T(8,128)(2,1)S(1)} %pad_maximum_fusion.2), channel_id=1, source_target_pairs={{0,1},{1,0},{2,3},{3,2},{4,5},{5,4},{6,7},{7,6},{8,9},{9,8},{10,11... | collective-permute-start | bytes 393224 | tf_op jit(solution)/shard_map/ppermute | solution.py:484
  28.8 6.1 %collective-permute-start.11 = (bf16[1,128,512]{2,1,0:T(8,128)(2,1)S(1)}, bf16[1,128,512]{2,1,0:T(8,128)(2,1)S(1)}, u32[]{:S(2)}, u32[]{:S(2)}) collective-permute-start(bf16[1,128,512]{2,1,0:T(8,128)(2,1)S(1)} %slice.93), channel_id=1, source_target_pairs={{4,0},{8,4},{12,8},{14,12},{10,14},{6,10},{2,6},{0,2},{5,1},{9,5},... | collective-permute-start | bytes 393224 | tf_op jit(solution)/shard_map/ppermute | solution.py:562
  29.0 5.8 %collective-permute-start.8 = (bf16[1,128,512]{2,1,0:T(8,128)(2,1)S(1)}, bf16[1,128,512]{2,1,0:T(8,128)(2,1)S(1)}, u32[]{:S(2)}, u32[]{:S(2)}) collective-permute-start(bf16[1,128,512]{2,1,0:T(8,128)(2,1)S(1)} %slice.86), channel_id=1, source_target_pairs={{0,4},{4,8},{8,12},{12,14},{14,10},{10,6},{6,2},{2,0},{1,5},{5,9},... | collective-permute-start | bytes 393224 | tf_op jit(solution)/shard_map/ppermute | solution.py:562
  35.0 2.8 %collective-permute-start.12 = (bf16[2,128,128]{2,1,0:T(8,128)(2,1)S(1)}, bf16[2,128,128]{2,1,0:T(8,128)(2,1)S(1)}, u32[]{:S(2)}, u32[]{:S(2)}) collective-permute-start(bf16[2,128,128]{2,1,0:T(8,128)(2,1)S(1)} %slice_select_fusion), channel_id=1, source_target_pairs={{0,1},{1,0},{2,3},{3,2},{4,5},{5,4},{6,7},{7,6},{8,9},{9,8},{10,11... | collective-permute-start | bytes 196616 | tf_op jit(solution)/shard_map/ppermute | solution.py:484
